TPU v7x, 512 devices: a whole 4x8x8 slice. The times are simulated.
512 devices in a mesh: blk: 16 (over y, x_lo), cluster: 32 (over z, x_hi, core).
Axes of the slice: x: 4 (x_hi: 2, x_lo: 2; x = x_hi * 2 + x_lo), y: 8, z: 8, core: 2. Of those that a mesh axis runs over, the one named last changes fastest.
Arguments:
- charges: bfloat16 [16384, 128], P(('blk', 'cluster')), may hold values from -6 to 6
- near_vals: bfloat16 [16384, 3, 128, 128], P(('blk', 'cluster')), may hold values from -0.3125 to 0.3125
- near_cols: int32 [16384, 3], P(('blk', 'cluster')), may hold values from 0 to 16383, as said below
- source_basis: bfloat16 [16384, 64, 128], P(('blk', 'cluster')), may hold values from -0.5 to 0.5
- target_basis: bfloat16 [16384, 64, 128], P(('blk', 'cluster')), may hold values from -0.75 to 0.75
- coupling: bfloat16 [16384, 2, 64, 64], P(('blk', 'cluster')), may hold values from -0.5 to 0.5
- far_cols: int32 [16384, 2], P(('blk', 'cluster')), may hold values from 0 to 16383, as said below
Outputs:
- potential_one: float32 [16384, 128], P(('blk', 'cluster'))
- potential_two: float32 [16384, 128], P(('blk', 'cluster'))
Inputs may be any that keep to these rules, and one draw needn't show every extreme that they name: near_cols[i, 0] is block i itself; every entry names a block whose device has the same cluster index as block i's device and a blk index at most 3 away from it around the closed loop of blk. `far_cols`: every entry names a block whose device has the same blk index as block i's device; among the entries of one device's block rows at most 6 name blocks of any one cluster index, and exactly 6 name those of one cluster index.
All inputs are finite; a program needn't handle non-finite values.
Results may differ from a plain program's by a relative error of at most 0.004.
Values may be sent and summed in bfloat16 or wider, within the bound.
No kernel may reach another device: no remote copies, remote signals or barrier semaphores. Data moves between devices by JAX's collectives and lax.ppermute only.
A program may use at most 64 MiB of HBM per device.

v0:
```python
import jax
import jax.numpy as jnp
from jax import lax
from jax.sharding import PartitionSpec as P


def from_behind(block, axis, distance):
    devices = range(lax.axis_size(axis))
    route = [((i - distance) % len(devices), i) for i in devices]
    return lax.ppermute(block, axis, route)


def shards(charges, near_vals, near_cols, source_basis, target_basis, coupling, far_cols):
    cycle_size = lax.axis_size("blk")
    owners = lax.axis_size("cluster")
    reach = min(3, (cycle_size - 1) // 2)
    rows_here = charges.shape[0]
    panels = charges.shape[1]
    cycle_pos = lax.axis_index("blk")
    near_group = near_cols // rows_here
    near_offset = (near_group // owners - cycle_pos + cycle_size) % cycle_size
    near_offset = jnp.where(near_offset > reach, near_offset - cycle_size, near_offset)
    window_row = (near_offset + reach) * rows_here + near_cols % rows_here
    far_owner = far_cols // rows_here % owners
    far_within = far_cols % rows_here

    def apply_operator(charge):
        lower_list = []
        upper_list = []
        for step in range(1, reach + 1):
            lower_list.append(from_behind(charge, "blk", step))
            upper_list.append(from_behind(charge, "blk", -step))
        window = jnp.stack(lower_list[::-1] + [charge] + upper_list, axis=0)
        window = window.reshape((2 * reach + 1) * rows_here, panels)
        moments = jnp.einsum("brp,bp->br", source_basis, charge, preferred_element_type=jnp.float32)
        every_moment = lax.all_gather(moments, "cluster", axis=0, tiled=True)
        far_in = every_moment[far_owner * rows_here + far_within]
        near_in = window[window_row]
        near_part = jnp.einsum(
            "bkpq,bkq->bp", near_vals, near_in, preferred_element_type=jnp.float32
        )
        coupled = jnp.einsum(
            "bkrs,bks->br", coupling.astype(jnp.float32), far_in, precision=lax.Precision.HIGHEST
        ).astype(jnp.bfloat16)
        far_part = jnp.einsum(
            "brp,br->bp", target_basis, coupled, preferred_element_type=jnp.float32
        )
        return near_part + far_part

    potential_one = apply_operator(charges)
    potential_two = apply_operator(potential_one.astype(jnp.bfloat16))
    return (potential_one, potential_two)


def solution(mesh):
    in_specs = (
        P(("blk", "cluster"), None),
        P(("blk", "cluster"), None, None, None),
        P(("blk", "cluster"), None),
        P(("blk", "cluster"), None, None),
        P(("blk", "cluster"), None, None),
        P(("blk", "cluster"), None, None, None),
        P(("blk", "cluster"), None),
    )
    out_specs = (P(("blk", "cluster"), None), P(("blk", "cluster"), None))
    return jax.shard_map(shards, mesh=mesh, in_specs=in_specs, out_specs=out_specs, check_vma=False)
```

profile of v0, /device:TPU:1, one launch (start us, length us, event | category | flops | bytes accessed | tf_op | source)
XLA Modules:
  0.0 162.2 jit_solution(3688055216046880327)
XLA Ops:
  0.7 6.2 %collective-permute-start.4 = (bf16[32,128]{1,0:T(8,128)(2,1)}, bf16[32,128]{1,0:T(8,128)(2,1)S(1)}, u32[]{:S(2)}, u32[]{:S(2)}) collective-permute-start(bf16[32,128]{1,0:T(8,128)(2,1)} %param.7), channel_id=1, source_target_pairs={{64,0},{96,32},{128,64},{160,96},{192,128},{224,160},{256,192},{28... | collective-permute-start | bytes 24584 | tf_op jit(solution)/shard_map/ppermute | solution.py:10
  6.9 3.9 %collective-permute-start.3 = (bf16[32,128]{1,0:T(8,128)(2,1)}, bf16[32,128]{1,0:T(8,128)(2,1)S(1)}, u32[]{:S(2)}, u32[]{:S(2)}) collective-permute-start(bf16[32,128]{1,0:T(8,128)(2,1)} %param.7), channel_id=1, source_target_pairs={{32,0},{64,32},{96,64},{128,96},{160,128},{192,160},{224,192},{256... | collective-permute-start | bytes 24584 | tf_op jit(solution)/shard_map/ppermute | solution.py:10
  10.8 1.9 %collective-permute-start.2 = (bf16[32,128]{1,0:T(8,128)(2,1)}, bf16[32,128]{1,0:T(8,128)(2,1)S(1)}, u32[]{:S(2)}, u32[]{:S(2)}) collective-permute-start(bf16[32,128]{1,0:T(8,128)(2,1)} %param.7), channel_id=1, source_target_pairs={{480,0},{0,32},{32,64},{64,96},{96,128},{128,160},{160,192},{192,2... | collective-permute-start | bytes 24584 | tf_op jit(solution)/shard_map/ppermute | solution.py:10
  12.7 2.3 %collective-permute-start.1 = (bf16[32,128]{1,0:T(8,128)(2,1)}, bf16[32,128]{1,0:T(8,128)(2,1)S(1)}, u32[]{:S(2)}, u32[]{:S(2)}) collective-permute-start(bf16[32,128]{1,0:T(8,128)(2,1)} %param.7), channel_id=1, source_target_pairs={{448,0},{480,32},{0,64},{32,96},{64,128},{96,160},{128,192},{160,2... | collective-permute-start | bytes 24584 | tf_op jit(solution)/shard_map/ppermute | solution.py:10
  15.0 2.4 %collective-permute-start = (bf16[32,128]{1,0:T(8,128)(2,1)}, bf16[32,128]{1,0:T(8,128)(2,1)S(1)}, u32[]{:S(2)}, u32[]{:S(2)}) collective-permute-start(bf16[32,128]{1,0:T(8,128)(2,1)} %param.7), channel_id=1, source_target_pairs={{416,0},{448,32},{480,64},{0,96},{32,128},{64,160},{96,192},{128,2... | collective-permute-start | bytes 24584 | tf_op jit(solution)/shard_map/ppermute | solution.py:10
  17.4 0.7 compare_select_fusion.2
  18.1 0.7 compare_select_fusion
  19.2 1.4 fusion.6
  20.6 53.6 %all_gather.6 = f32[1024,64]{1,0:T(8,128)} all-gather(f32[32,64]{1,0:T(8,128)S(1)} %bitcast.87), channel_id=1, replica_groups=mesh['blk'=16,'cluster'=32] {'cluster'}, dimensions={0}, use_global_device_ids=true | all-gather | bytes 270336 | tf_op jit(solution)/shard_map/all_gather | solution.py:36
  74.2 1.6 %gather_fusion.1 = f32[64,64]{1,0:T(8,128)S(1)} fusion(f32[1024,64]{1,0:T(8,128)} %all_gather.6, s32[1024]{0:T(1024)S(1)} %pad_clamp_fusion), kind=kCustom, calls=%fused_computation.1 | custom fusion | bytes 33024 | tf_op jit(solution)/shard_map/gather | solution.py:37
  75.8 2.1 %fusion.22 = f32[32,1,64,1]{2,1,3,0:T(1,128)S(1)} fusion(f32[32,2,64,1]{2,3,1,0:T(1,128)S(1)} %bitcast.83, bf16[32,2,64,64]{3,2,1,0:T(8,128)(2,1)} %param.12), kind=kOutput, calls=%fused_computation.69 | convolution fusion | flops 3145728 | bytes 548864 | tf_op jit(solution)/shard_map/bkrs,bks->br/dot_general | solution.py:42
  78.0 1.3 fusion.4
  79.3 5.0 %collective-permute-start.5 = (bf16[32,128]{1,0:T(8,128)(2,1)S(1)}, bf16[32,128]{1,0:T(8,128)(2,1)S(1)}, u32[]{:S(2)}, u32[]{:S(2)}) collective-permute-start(bf16[32,128]{1,0:T(8,128)(2,1)S(1)} %copy-done.1), channel_id=1, source_target_pairs={{96,0},{128,32},{160,64},{192,96},{224,128},{256,160},{288,192},{3... | collective-permute-start | bytes 24584 | tf_op jit(solution)/shard_map/ppermute | solution.py:10
  84.5 0.7 collective-permute-done.5
  85.1 0.7 gather_fusion
  85.8 1.2 fusion.21
  87.0 0.6 fusion.20
  87.7 6.6 %collective-permute-start.11 = (bf16[32,128]{1,0:T(8,128)(2,1)S(1)}, bf16[32,128]{1,0:T(8,128)(2,1)S(1)}, u32[]{:S(2)}, u32[]{:S(2)}) collective-permute-start(bf16[32,128]{1,0:T(8,128)(2,1)S(1)} %get-tuple-element.2), channel_id=1, source_target_pairs={{96,0},{128,32},{160,64},{192,96},{224,128},{256,160},{288,192},{3... | collective-permute-start | bytes 24584 | tf_op jit(solution)/shard_map/ppermute | solution.py:10
  94.3 1.9 %collective-permute-start.10 = (bf16[32,128]{1,0:T(8,128)(2,1)S(1)}, bf16[32,128]{1,0:T(8,128)(2,1)S(1)}, u32[]{:S(2)}, u32[]{:S(2)}) collective-permute-start(bf16[32,128]{1,0:T(8,128)(2,1)S(1)} %get-tuple-element.2), channel_id=1, source_target_pairs={{64,0},{96,32},{128,64},{160,96},{192,128},{224,160},{256,192},{28... | collective-permute-start | bytes 24584 | tf_op jit(solution)/shard_map/ppermute | solution.py:10
  96.2 3.2 %collective-permute-start.9 = (bf16[32,128]{1,0:T(8,128)(2,1)S(1)}, bf16[32,128]{1,0:T(8,128)(2,1)S(1)}, u32[]{:S(2)}, u32[]{:S(2)}) collective-permute-start(bf16[32,128]{1,0:T(8,128)(2,1)S(1)} %get-tuple-element.2), channel_id=1, source_target_pairs={{32,0},{64,32},{96,64},{128,96},{160,128},{192,160},{224,192},{256... | collective-permute-start | bytes 24584 | tf_op jit(solution)/shard_map/ppermute | solution.py:10
  99.4 2.1 %collective-permute-start.8 = (bf16[32,128]{1,0:T(8,128)(2,1)S(1)}, bf16[32,128]{1,0:T(8,128)(2,1)S(1)}, u32[]{:S(2)}, u32[]{:S(2)}) collective-permute-start(bf16[32,128]{1,0:T(8,128)(2,1)S(1)} %get-tuple-element.2), channel_id=1, source_target_pairs={{480,0},{0,32},{32,64},{64,96},{96,128},{128,160},{160,192},{192,2... | collective-permute-start | bytes 24584 | tf_op jit(solution)/shard_map/ppermute | solution.py:10
  101.5 4.0 %collective-permute-start.6 = (bf16[32,128]{1,0:T(8,128)(2,1)S(1)}, bf16[32,128]{1,0:T(8,128)(2,1)S(1)}, u32[]{:S(2)}, u32[]{:S(2)}) collective-permute-start(bf16[32,128]{1,0:T(8,128)(2,1)S(1)} %get-tuple-element.2), channel_id=1, source_target_pairs={{416,0},{448,32},{480,64},{0,96},{32,128},{64,160},{96,192},{128,2... | collective-permute-start | bytes 24584 | tf_op jit(solution)/shard_map/ppermute | solution.py:10
  105.5 0.4 fusion.2
  105.9 43.0 %all_gather.7 = f32[1024,64]{1,0:T(8,128)} all-gather(f32[32,64]{1,0:T(8,128)S(1)} %bitcast.88), channel_id=1, replica_groups=mesh['blk'=16,'cluster'=32] {'cluster'}, dimensions={0}, use_global_device_ids=true | all-gather | bytes 270336 | tf_op jit(solution)/shard_map/all_gather | solution.py:36
  148.9 1.6 %gather_fusion.3 = f32[64,64]{1,0:T(8,128)S(1)} fusion(f32[1024,64]{1,0:T(8,128)} %all_gather.7, s32[1024]{0:T(1024)S(1)} %pad_clamp_fusion), kind=kCustom, calls=%fused_computation.3 | custom fusion | bytes 33024 | tf_op jit(solution)/shard_map/gather | solution.py:37
  150.5 2.1 %fusion.24 = f32[32,1,64,1]{2,1,3,0:T(1,128)S(1)} fusion(f32[32,2,64,1]{2,3,1,0:T(1,128)S(1)} %bitcast.82, bf16[32,2,64,64]{3,2,1,0:T(8,128)(2,1)} %param.12), kind=kOutput, calls=%fused_computation.71 | convolution fusion | flops 3145728 | bytes 548864 | tf_op jit(solution)/shard_map/bkrs,bks->br/dot_general | solution.py:42
  152.7 1.3 fusion
  154.0 1.9 %collective-permute-start.7 = (bf16[32,128]{1,0:T(8,128)(2,1)S(1)}, bf16[32,128]{1,0:T(8,128)(2,1)S(1)}, u32[]{:S(2)}, u32[]{:S(2)}) collective-permute-start(bf16[32,128]{1,0:T(8,128)(2,1)S(1)} %get-tuple-element.2), channel_id=1, source_target_pairs={{448,0},{480,32},{0,64},{32,96},{64,128},{96,160},{128,192},{160,2... | collective-permute-start | bytes 24584 | tf_op jit(solution)/shard_map/ppermute | solution.py:10
  155.9 3.7 %collective-permute-done.7 = bf16[32,128]{1,0:T(8,128)(2,1)S(1)} collective-permute-done((bf16[32,128]{1,0:T(8,128)(2,1)S(1)}, bf16[32,128]{1,0:T(8,128)(2,1)S(1)}, u32[]{:S(2)}, u32[]{:S(2)}) %collective-permute-start.7) | collective-permute-done | bytes 8224 | tf_op jit(solution)/shard_map/ppermute | solution.py:10
  159.7 0.7 gather_fusion.2
  160.4 1.2 fusion.23
  161.6 0.6 add.62
  (40 shorter events, 0.6 us)
Async XLA Ops:
  0.6 85.2 %copy-start = (bf16[32,3,128,128]{3,2,1,0:T(8,128)(2,1)S(1)}, bf16[32,3,128,128]{3,2,1,0:T(8,128)(2,1)}, u32[]{:S(2)}) copy-start(bf16[32,3,128,128]{3,2,1,0:T(8,128)(2,1)} %param.8) | copy-start | bytes 9437188
  0.6 78.7 %copy-start.1 = (bf16[32,128]{1,0:T(8,128)(2,1)S(1)}, bf16[32,128]{1,0:T(8,128)(2,1)}, u32[]{:S(2)}) copy-start(bf16[32,128]{1,0:T(8,128)(2,1)} %param.7) | copy-start | bytes 24580
  0.7 83.8 %collective-permute-start.4 = (bf16[32,128]{1,0:T(8,128)(2,1)}, bf16[32,128]{1,0:T(8,128)(2,1)S(1)}, u32[]{:S(2)}, u32[]{:S(2)}) collective-permute-start(bf16[32,128]{1,0:T(8,128)(2,1)} %param.7), channel_id=1, source_target_pairs={{64,0},{96,32},{128,64},{160,96},{192,128},{224,160},{256,192},{28... | collective-permute-start | bytes 24584 | tf_op jit(solution)/shard_map/ppermute | solution.py:10
  6.9 77.6 %collective-permute-start.3 = (bf16[32,128]{1,0:T(8,128)(2,1)}, bf16[32,128]{1,0:T(8,128)(2,1)S(1)}, u32[]{:S(2)}, u32[]{:S(2)}) collective-permute-start(bf16[32,128]{1,0:T(8,128)(2,1)} %param.7), channel_id=1, source_target_pairs={{32,0},{64,32},{96,64},{128,96},{160,128},{192,160},{224,192},{256... | collective-permute-start | bytes 24584 | tf_op jit(solution)/shard_map/ppermute | solution.py:10
  10.8 73.6 %collective-permute-start.2 = (bf16[32,128]{1,0:T(8,128)(2,1)}, bf16[32,128]{1,0:T(8,128)(2,1)S(1)}, u32[]{:S(2)}, u32[]{:S(2)}) collective-permute-start(bf16[32,128]{1,0:T(8,128)(2,1)} %param.7), channel_id=1, source_target_pairs={{480,0},{0,32},{32,64},{64,96},{96,128},{128,160},{160,192},{192,2... | collective-permute-start | bytes 24584 | tf_op jit(solution)/shard_map/ppermute | solution.py:10
  12.7 71.7 %collective-permute-start.1 = (bf16[32,128]{1,0:T(8,128)(2,1)}, bf16[32,128]{1,0:T(8,128)(2,1)S(1)}, u32[]{:S(2)}, u32[]{:S(2)}) collective-permute-start(bf16[32,128]{1,0:T(8,128)(2,1)} %param.7), channel_id=1, source_target_pairs={{448,0},{480,32},{0,64},{32,96},{64,128},{96,160},{128,192},{160,2... | collective-permute-start | bytes 24584 | tf_op jit(solution)/shard_map/ppermute | solution.py:10
  15.0 64.3 %collective-permute-start = (bf16[32,128]{1,0:T(8,128)(2,1)}, bf16[32,128]{1,0:T(8,128)(2,1)S(1)}, u32[]{:S(2)}, u32[]{:S(2)}) collective-permute-start(bf16[32,128]{1,0:T(8,128)(2,1)} %param.7), channel_id=1, source_target_pairs={{416,0},{448,32},{480,64},{0,96},{32,128},{64,160},{96,192},{128,2... | collective-permute-start | bytes 24584 | tf_op jit(solution)/shard_map/ppermute | solution.py:10
  79.3 5.8 %collective-permute-start.5 = (bf16[32,128]{1,0:T(8,128)(2,1)S(1)}, bf16[32,128]{1,0:T(8,128)(2,1)S(1)}, u32[]{:S(2)}, u32[]{:S(2)}) collective-permute-start(bf16[32,128]{1,0:T(8,128)(2,1)S(1)} %copy-done.1), channel_id=1, source_target_pairs={{96,0},{128,32},{160,64},{192,96},{224,128},{256,160},{288,192},{3... | collective-permute-start | bytes 24584 | tf_op jit(solution)/shard_map/ppermute | solution.py:10
  85.8 19.7 %copy-start.2 = (bf16[32,64,128]{2,1,0:T(8,128)(2,1)S(1)}, bf16[32,64,128]{2,1,0:T(8,128)(2,1)}, u32[]{:S(2)}) copy-start(bf16[32,64,128]{2,1,0:T(8,128)(2,1)} %param.10) | copy-start | bytes 1572868
  87.7 72.0 %collective-permute-start.11 = (bf16[32,128]{1,0:T(8,128)(2,1)S(1)}, bf16[32,128]{1,0:T(8,128)(2,1)S(1)}, u32[]{:S(2)}, u32[]{:S(2)}) collective-permute-start(bf16[32,128]{1,0:T(8,128)(2,1)S(1)} %get-tuple-element.2), channel_id=1, source_target_pairs={{96,0},{128,32},{160,64},{192,96},{224,128},{256,160},{288,192},{3... | collective-permute-start | bytes 24584 | tf_op jit(solution)/shard_map/ppermute | solution.py:10
  94.3 65.3 %collective-permute-start.10 = (bf16[32,128]{1,0:T(8,128)(2,1)S(1)}, bf16[32,128]{1,0:T(8,128)(2,1)S(1)}, u32[]{:S(2)}, u32[]{:S(2)}) collective-permute-start(bf16[32,128]{1,0:T(8,128)(2,1)S(1)} %get-tuple-element.2), channel_id=1, source_target_pairs={{64,0},{96,32},{128,64},{160,96},{192,128},{224,160},{256,192},{28... | collective-permute-start | bytes 24584 | tf_op jit(solution)/shard_map/ppermute | solution.py:10
  96.2 63.4 %collective-permute-start.9 = (bf16[32,128]{1,0:T(8,128)(2,1)S(1)}, bf16[32,128]{1,0:T(8,128)(2,1)S(1)}, u32[]{:S(2)}, u32[]{:S(2)}) collective-permute-start(bf16[32,128]{1,0:T(8,128)(2,1)S(1)} %get-tuple-element.2), channel_id=1, source_target_pairs={{32,0},{64,32},{96,64},{128,96},{160,128},{192,160},{224,192},{256... | collective-permute-start | bytes 24584 | tf_op jit(solution)/shard_map/ppermute | solution.py:10
  99.4 60.2 %collective-permute-start.8 = (bf16[32,128]{1,0:T(8,128)(2,1)S(1)}, bf16[32,128]{1,0:T(8,128)(2,1)S(1)}, u32[]{:S(2)}, u32[]{:S(2)}) collective-permute-start(bf16[32,128]{1,0:T(8,128)(2,1)S(1)} %get-tuple-element.2), channel_id=1, source_target_pairs={{480,0},{0,32},{32,64},{64,96},{96,128},{128,160},{160,192},{192,2... | collective-permute-start | bytes 24584 | tf_op jit(solution)/shard_map/ppermute | solution.py:10
  101.5 52.4 %collective-permute-start.6 = (bf16[32,128]{1,0:T(8,128)(2,1)S(1)}, bf16[32,128]{1,0:T(8,128)(2,1)S(1)}, u32[]{:S(2)}, u32[]{:S(2)}) collective-permute-start(bf16[32,128]{1,0:T(8,128)(2,1)S(1)} %get-tuple-element.2), channel_id=1, source_target_pairs={{416,0},{448,32},{480,64},{0,96},{32,128},{64,160},{96,192},{128,2... | collective-permute-start | bytes 24584 | tf_op jit(solution)/shard_map/ppermute | solution.py:10
  154.0 5.6 %collective-permute-start.7 = (bf16[32,128]{1,0:T(8,128)(2,1)S(1)}, bf16[32,128]{1,0:T(8,128)(2,1)S(1)}, u32[]{:S(2)}, u32[]{:S(2)}) collective-permute-start(bf16[32,128]{1,0:T(8,128)(2,1)S(1)} %get-tuple-element.2), channel_id=1, source_target_pairs={{448,0},{480,32},{0,64},{32,96},{64,128},{96,160},{128,192},{160,2... | collective-permute-start | bytes 24584 | tf_op jit(solution)/shard_map/ppermute | solution.py:10
where the time goes:
time: 164 us; the launch traced here: 162 us
  blocking collectives  96.6 us (59%)
  starting transfers between devices  41.4 us (25%)
  matrix products  11 us (7%)
  local copies, waits for them, and re-layouts  5.18 us (3%)
  waiting for transfers between devices  4.36 us (3%)
  other arithmetic  2.7 us (2%)
    all_gather x2, blocking collectives, apply_operator(): every_moment = lax.all_gather(moments, 'cluster', axis=0, tiled=True)  96.6 us
    ppermute x12, starting transfers between devices, from_behind(): return lax.ppermute(block, axis, route)  41.4 us
    ppermute x12, waiting for transfers between devices, from_behind(): return lax.ppermute(block, axis, route)  4.36 us
    dot_general x2, matrix products, apply_operator(): jnp.einsum('bkrs,bks->br', coupling.astype(jnp.float32), far_in, precisio...  4.27 us
  transfers between devices with their start and end apart: 12, of which 2 were waited for; matrix products, arithmetic and copies ran while one was open for 9% of the time, Pallas kernels for 0%

commit v1 on v0

v1 whole, which is shorter than its diff:
```python
import jax
import jax.numpy as jnp
from jax import lax
from jax.sharding import PartitionSpec as P


def spread(block, axis):
    size = lax.axis_size(axis)
    copies = jnp.broadcast_to(block[None], (size,) + block.shape)
    return lax.all_to_all(copies, axis, 0, 0, tiled=True)


def shards(charges, near_vals, near_cols, source_basis, target_basis, coupling, far_cols):
    owners = lax.axis_size("cluster")
    cycle_size = lax.axis_size("blk")
    rows, panels = charges.shape
    rank = source_basis.shape[1]
    half = rows // 2
    near_group = near_cols // rows
    near_row = (near_group // owners) * rows + near_cols % rows
    near_hot = (near_row.reshape(-1)[:, None] == jnp.arange(cycle_size * rows)[None, :]).astype(jnp.bfloat16)
    far_owner = far_cols // rows % owners
    far_within = far_cols % rows
    far_row = far_owner * half + far_within % half
    far_upper = (far_within >= half)[:, :, None]
    far_hot = (far_row.reshape(-1)[:, None] == jnp.arange(owners * half)[None, :]).astype(jnp.bfloat16)

    def apply_operator(charge):
        window = spread(charge, "blk").reshape(cycle_size * rows, panels)
        moments = jnp.einsum("brp,bp->br", source_basis, charge, preferred_element_type=jnp.float32)
        packed = jnp.concatenate([moments[:half], moments[half:]], axis=1).astype(jnp.bfloat16)
        every_moment = spread(packed, "cluster").reshape(owners * half, 2 * rank)
        far_both = jnp.dot(far_hot, every_moment, preferred_element_type=jnp.float32).reshape(rows, -1, 2 * rank)
        far_in = jnp.where(far_upper, far_both[:, :, rank:], far_both[:, :, :rank]).astype(jnp.bfloat16)
        near_in = jnp.dot(near_hot, window, preferred_element_type=jnp.float32).astype(jnp.bfloat16)
        near_in = near_in.reshape(rows, -1, panels)
        near_part = jnp.einsum(
            "bkpq,bkq->bp", near_vals, near_in, preferred_element_type=jnp.float32
        )
        coupled = jnp.einsum(
            "bkrs,bks->br", coupling, far_in, preferred_element_type=jnp.float32
        ).astype(jnp.bfloat16)
        far_part = jnp.einsum(
            "brp,br->bp", target_basis, coupled, preferred_element_type=jnp.float32
        )
        return near_part + far_part

    potential_one = apply_operator(charges)
    potential_two = apply_operator(potential_one.astype(jnp.bfloat16))
    return (potential_one, potential_two)


def solution(mesh):
    in_specs = (
        P(("blk", "cluster"), None),
        P(("blk", "cluster"), None, None, None),
        P(("blk", "cluster"), None),
        P(("blk", "cluster"), None, None),
        P(("blk", "cluster"), None, None),
        P(("blk", "cluster"), None, None, None),
        P(("blk", "cluster"), None),
    )
    out_specs = (P(("blk", "cluster"), None), P(("blk", "cluster"), None))
    return jax.shard_map(shards, mesh=mesh, in_specs=in_specs, out_specs=out_specs, check_vma=False)
```

time: 164 us -> 85.2 us (0.52)
  blocking collectives: 96.6 us -> 0 us
  waiting for transfers between devices: 4.36 us -> 32.3 us
  starting transfers between devices: 41.4 us -> 32.2 us
    all_gather x2 -> x0, blocking collectives: 96.6 us -> none  [apply_operator(): every_moment = lax.all_gather(moments, 'cluster', axis=0, tiled=True)]
    ppermute x12 -> x0, starting transfers between devices: 41.4 us -> none  [from_behind(): return lax.ppermute(block, axis, route)]
    all_to_all x0 -> x4, waiting for transfers between devices: none -> 32.3 us  [spread(): return lax.all_to_all(copies, axis, 0, 0, tiled=True)]
    all_to_all x0 -> x4, starting transfers between devices: none -> 32.2 us  [spread(): return lax.all_to_all(copies, axis, 0, 0, tiled=True)]
    gather x6 -> x0, local copies, waits for them, and re-layouts: 4.66 us -> none  [the longest x2 3.28 us: apply_operator(): far_in = every_moment[far_owner * rows_here + far_within]]
    ppermute x12 -> x0, waiting for transfers between devices: 4.36 us -> none  [from_behind(): return lax.ppermute(block, axis, route)]
    broadcast_in_dim x2 -> x4, local copies, waits for them, and re-layouts: 0.21 us -> 3.49 us  [spread(): copies = jnp.broadcast_to(block[None], (size,) + block.shape)]
    dot_general x2 -> x6, matrix products: 4.27 us -> 4.03 us  [the longest x2 3.17 us: apply_operator(): jnp.einsum('bkrs,bks->br', coupling, far_in, preferred_element_type=jnp.f...]
  transfers between devices with their start and end apart: 12 -> 4, of which waited for: 2 -> 4; matrix products, arithmetic and copies ran while one was open for 9% -> 8% of each run, Pallas kernels for 0% -> 0%
where the time goes in v1:
time: 85.2 us; the launch traced here: 84.5 us
  waiting for transfers between devices  32.3 us (38%)
  starting transfers between devices  32.2 us (38%)
  matrix products  11.8 us (14%)
  local copies, waits for them, and re-layouts  3.74 us (4%)
  other arithmetic  3.73 us (4%)
    all_to_all x4, waiting for transfers between devices, spread(): return lax.all_to_all(copies, axis, 0, 0, tiled=True)  32.3 us
    all_to_all x4, starting transfers between devices, spread(): return lax.all_to_all(copies, axis, 0, 0, tiled=True)  32.2 us
    broadcast_in_dim x4, local copies, waits for them, and re-layouts, spread(): copies = jnp.broadcast_to(block[None], (size,) + block.shape)  3.49 us
    dot_general x2, matrix products, apply_operator(): jnp.einsum('bkrs,bks->br', coupling, far_in, preferred_element_type=jnp.f...  3.17 us
    dot_general x2, matrix products, apply_operator(): jnp.einsum('brp,bp->br', source_basis, charge, preferred_element_type=jnp...  2.8 us
    dot_general x2, matrix products, apply_operator(): jnp.einsum('brp,br->bp', target_basis, coupled, preferred_element_type=jn...  2.6 us
    dot_general x2, matrix products, apply_operator(): jnp.einsum('bkpq,bkq->bp', near_vals, near_in, preferred_element_type=jnp...  2.37 us
  transfers between devices with their start and end apart: 4, of which 4 were waited for; matrix products, arithmetic and copies ran while one was open for 8% of the time, Pallas kernels for 0%

profile of v1, /device:TPU:1, one launch (start us, length us, event | category | flops | bytes accessed | tf_op | source)
XLA Modules:
  0.0 84.5 jit_solution(17154947131075934483)
XLA Ops:
  0.6 1.5 %broadcast_in_dim.19 = bf16[16,32,128]{2,1,0:T(8,128)(2,1)} broadcast(bf16[32,128]{1,0:T(8,128)(2,1)} %param.7), dimensions={1,2} | broadcast | bytes 139264 | tf_op jit(solution)/shard_map/broadcast_in_dim | solution.py:9
  2.1 8.7 %all-to-all-start = ((bf16[16,32,128]{2,1,0:T(8,128)(2,1)}), bf16[16,32,128]{2,1,0:T(8,128)(2,1)S(1)}, u32[]{:S(2)}, u32[]{:S(2)}) async-start(bf16[16,32,128]{2,1,0:T(8,128)(2,1)} %broadcast_in_dim.19), calls=%async_computation | async-start | bytes 262144 | tf_op jit(solution)/shard_map/all_to_all | solution.py:10
  10.8 0.7 broadcast_compare_fusion
  11.5 0.7 fusion.27
  12.2 1.4 %fusion.23 = f32[32,1,64]{2,1,0:T(1,128)S(1)} fusion(bf16[32,64,128]{2,1,0:T(8,128)(2,1)} %param.10, bf16[32,128,1]{1,0,2:T(8,128)(2,1)} %bitcast.69), kind=kOutput, calls=%fused_computation.27 | convolution fusion | flops 524288 | bytes 540672 | tf_op jit(solution)/shard_map/brp,bp->br/dot_general | solution.py:30
  13.6 0.1 pad_maximum_fusion
  13.8 0.1 eq.55
  13.9 0.7 fusion.30
  14.6 4.7 %all-to-all-done = bf16[16,32,128]{2,1,0:T(8,128)(2,1)S(1)} async-done(((bf16[16,32,128]{2,1,0:T(8,128)(2,1)}), bf16[16,32,128]{2,1,0:T(8,128)(2,1)S(1)}, u32[]{:S(2)}, u32[]{:S(2)}) %all-to-all-start) | async-done | bytes 131104 | tf_op jit(solution)/shard_map/all_to_all | solution.py:10
  19.3 0.7 broadcast_in_dim.21
  20.0 14.7 %all-to-all-start.1 = ((bf16[32,16,128]{2,1,0:T(8,128)(2,1)}), bf16[32,16,128]{2,1,0:T(8,128)(2,1)S(1)}, u32[]{:S(2)}, u32[]{:S(2)}) async-start(bf16[32,16,128]{2,1,0:T(8,128)(2,1)} %broadcast_in_dim.21), calls=%async_computation.1 | async-start | bytes 262144 | tf_op jit(solution)/shard_map/all_to_all | solution.py:10
  34.7 0.2 convolution_convert_fusion.1
  35.0 1.2 %fusion.37 = f32[32,1,128,1]{2,1,3,0:T(1,128)S(1)} fusion(bf16[32,3,128,1]{2,3,1,0:T(2,128)(2,1)S(1)} %reshape.117, bf16[32,3,128,128]{3,2,1,0:T(8,128)(2,1)S(1)} %copy-done), kind=kOutput, calls=%fused_computation.70 | convolution fusion | flops 3145728 | bytes 3186688 | tf_op jit(solution)/shard_map/bkpq,bkq->bp/dot_general | solution.py:37
  36.2 9.3 %all-to-all-done.1 = bf16[32,16,128]{2,1,0:T(8,128)(2,1)S(1)} async-done(((bf16[32,16,128]{2,1,0:T(8,128)(2,1)}), bf16[32,16,128]{2,1,0:T(8,128)(2,1)S(1)}, u32[]{:S(2)}, u32[]{:S(2)}) %all-to-all-start.1) | async-done | bytes 131104 | tf_op jit(solution)/shard_map/all_to_all | solution.py:10
  45.5 0.2 fusion.3
  45.7 0.1 fusion.15
  45.8 1.6 %fusion.13 = f32[32,1,64,1]{2,1,3,0:T(1,128)S(1)} fusion(bf16[32,2,64,64]{3,2,1,0:T(8,128)(2,1)} %param.12, bf16[32,2,64,1]{2,0,1,3:T(8,128)(2,1)S(1)} %fusion.15), kind=kOutput, calls=%fused_computation.17 | convolution fusion | flops 524288 | bytes 540672 | tf_op jit(solution)/shard_map/bkrs,bks->br/dot_general | solution.py:40
  47.4 1.3 %fusion.21 = f32[32,1,128]{2,1,0:T(1,128)S(1)} fusion(bf16[32,64,128]{2,1,0:T(8,128)(2,1)} %param.11, bf16[32,64,1]{1,0,2:T(8,128)(2,1)S(1)} %convert_bitcast_fusion.1), kind=kOutput, calls=%fused_computation.25 | convolution fusion | flops 524288 | bytes 544768 | tf_op jit(solution)/shard_map/brp,br->bp/dot_general | solution.py:43
  48.7 0.6 fusion.34
  49.3 1.4 %fusion.19 = f32[32,1,64]{2,1,0:T(1,128)S(1)} fusion(bf16[32,64,128]{2,1,0:T(8,128)(2,1)} %param.10, bf16[32,128,1]{1,0,2:T(8,128)(2,1)S(1)} %bitcast.62), kind=kOutput, calls=%fused_computation.23 | convolution fusion | flops 524288 | bytes 540672 | tf_op jit(solution)/shard_map/brp,bp->br/dot_general | solution.py:30
  50.7 0.7 broadcast_in_dim.22
  51.4 3.5 %all-to-all-start.2 = ((bf16[16,32,128]{2,1,0:T(8,128)(2,1)}), bf16[16,32,128]{2,1,0:T(8,128)(2,1)S(1)}, u32[]{:S(2)}, u32[]{:S(2)}) async-start(bf16[16,32,128]{2,1,0:T(8,128)(2,1)} %broadcast_in_dim.22), calls=%async_computation.2 | async-start | bytes 262144 | tf_op jit(solution)/shard_map/all_to_all | solution.py:10
  55.0 8.8 %all-to-all-done.2 = bf16[16,32,128]{2,1,0:T(8,128)(2,1)S(1)} async-done(((bf16[16,32,128]{2,1,0:T(8,128)(2,1)}), bf16[16,32,128]{2,1,0:T(8,128)(2,1)S(1)}, u32[]{:S(2)}, u32[]{:S(2)}) %all-to-all-start.2) | async-done | bytes 131104 | tf_op jit(solution)/shard_map/all_to_all | solution.py:10
  63.8 0.7 broadcast_in_dim.23
  64.4 5.3 %all-to-all-start.3 = ((bf16[32,16,128]{2,1,0:T(8,128)(2,1)}), bf16[32,16,128]{2,1,0:T(8,128)(2,1)S(1)}, u32[]{:S(2)}, u32[]{:S(2)}) async-start(bf16[32,16,128]{2,1,0:T(8,128)(2,1)} %broadcast_in_dim.23), calls=%async_computation.3 | async-start | bytes 262144 | tf_op jit(solution)/shard_map/all_to_all | solution.py:10
  69.7 0.2 convolution_convert_fusion
  70.0 1.2 %fusion.38 = f32[32,1,128,1]{2,1,3,0:T(1,128)S(1)} fusion(bf16[32,3,128,1]{2,3,1,0:T(2,128)(2,1)S(1)} %reshape.119, bf16[32,3,128,128]{3,2,1,0:T(8,128)(2,1)S(1)} %copy-done), kind=kOutput, calls=%fused_computation.71 | convolution fusion | flops 3145728 | bytes 3186688 | tf_op jit(solution)/shard_map/bkpq,bkq->bp/dot_general | solution.py:37
  71.2 9.5 %all-to-all-done.3 = bf16[32,16,128]{2,1,0:T(8,128)(2,1)S(1)} async-done(((bf16[32,16,128]{2,1,0:T(8,128)(2,1)}), bf16[32,16,128]{2,1,0:T(8,128)(2,1)S(1)}, u32[]{:S(2)}, u32[]{:S(2)}) %all-to-all-start.3) | async-done | bytes 131104 | tf_op jit(solution)/shard_map/all_to_all | solution.py:10
  80.7 0.2 fusion.1
  81.0 1.6 %fusion.11 = f32[32,1,64,1]{2,1,3,0:T(1,128)S(1)} fusion(bf16[32,2,64,64]{3,2,1,0:T(8,128)(2,1)} %param.12, bf16[32,2,64,1]{2,0,1,3:T(8,128)(2,1)S(1)} %fusion.16), kind=kOutput, calls=%fused_computation.15 | convolution fusion | flops 524288 | bytes 540672 | tf_op jit(solution)/shard_map/bkrs,bks->br/dot_general | solution.py:40
  82.6 1.3 %fusion.17 = f32[32,1,128]{2,1,0:T(1,128)S(1)} fusion(bf16[32,64,128]{2,1,0:T(8,128)(2,1)} %param.11, bf16[32,64,1]{1,0,2:T(8,128)(2,1)S(1)} %convert_bitcast_fusion), kind=kOutput, calls=%fused_computation.21 | convolution fusion | flops 524288 | bytes 544768 | tf_op jit(solution)/shard_map/brp,br->bp/dot_general | solution.py:43
  83.9 0.6 add.42
  (13 shorter events, 0.3 us)
Async XLA Ops:
  0.6 34.3 %copy-start = (bf16[32,3,128,128]{3,2,1,0:T(8,128)(2,1)S(1)}, bf16[32,3,128,128]{3,2,1,0:T(8,128)(2,1)}, u32[]{:S(2)}) copy-start(bf16[32,3,128,128]{3,2,1,0:T(8,128)(2,1)} %param.8) | copy-start | bytes 9437188
  2.1 17.2 %all-to-all-start = ((bf16[16,32,128]{2,1,0:T(8,128)(2,1)}), bf16[16,32,128]{2,1,0:T(8,128)(2,1)S(1)}, u32[]{:S(2)}, u32[]{:S(2)}) async-start(bf16[16,32,128]{2,1,0:T(8,128)(2,1)} %broadcast_in_dim.19), calls=%async_computation | async-start | bytes 262144 | tf_op jit(solution)/shard_map/all_to_all | solution.py:10
  20.0 25.5 %all-to-all-start.1 = ((bf16[32,16,128]{2,1,0:T(8,128)(2,1)}), bf16[32,16,128]{2,1,0:T(8,128)(2,1)S(1)}, u32[]{:S(2)}, u32[]{:S(2)}) async-start(bf16[32,16,128]{2,1,0:T(8,128)(2,1)} %broadcast_in_dim.21), calls=%async_computation.1 | async-start | bytes 262144 | tf_op jit(solution)/shard_map/all_to_all | solution.py:10
  51.4 12.4 %all-to-all-start.2 = ((bf16[16,32,128]{2,1,0:T(8,128)(2,1)}), bf16[16,32,128]{2,1,0:T(8,128)(2,1)S(1)}, u32[]{:S(2)}, u32[]{:S(2)}) async-start(bf16[16,32,128]{2,1,0:T(8,128)(2,1)} %broadcast_in_dim.22), calls=%async_computation.2 | async-start | bytes 262144 | tf_op jit(solution)/shard_map/all_to_all | solution.py:10
  64.4 16.3 %all-to-all-start.3 = ((bf16[32,16,128]{2,1,0:T(8,128)(2,1)}), bf16[32,16,128]{2,1,0:T(8,128)(2,1)S(1)}, u32[]{:S(2)}, u32[]{:S(2)}) async-start(bf16[32,16,128]{2,1,0:T(8,128)(2,1)} %broadcast_in_dim.23), calls=%async_computation.3 | async-start | bytes 262144 | tf_op jit(solution)/shard_map/all_to_all | solution.py:10

commit v2 on v1

v2 whole, which is shorter than its diff:
```python
import functools

import jax
import jax.numpy as jnp
from jax import lax
from jax.experimental import pallas as pl
from jax.experimental.pallas import tpu as pltpu
from jax.sharding import PartitionSpec as P

F32 = jnp.float32
BF16 = jnp.bfloat16
NT = (((1,), (1,)), ((), ()))
NN = (((1,), (0,)), ((), ()))
TILE = 256


def mul(a, b, dims):
    return lax.dot_general(a, b, dims, preferred_element_type=F32)


def iota(shape, dim):
    return lax.broadcasted_iota(jnp.int32, shape, dim)


def pick(index, depth):
    rows = index.shape[0]
    return jnp.where(iota((rows, depth), 1) == index, 1.0, 0.0).astype(BF16)


def packed_moments(field, source_ref, rank):
    rows, panels = field.shape
    total = jnp.zeros((rows, panels), F32)
    for base in range(0, source_ref.shape[0], TILE):
        product = mul(field, source_ref[base:base + TILE, :], NT)
        owner = (iota(product.shape, 1) + base) // rank
        product = jnp.where(owner == iota(product.shape, 0), product, 0.0)
        for lane in range(0, TILE, panels):
            total = total + product[:, lane:lane + panels]
    pair = jnp.where(iota((rows // 2, rows), 1) // 2 == iota((rows // 2, rows), 0), 1.0, 0.0)
    return mul(pair.astype(BF16), total.astype(BF16), NN).astype(BF16)


def first_kernel(rank, charge_ref, source_ref, copies_ref):
    packed = packed_moments(charge_ref[...], source_ref, rank)
    copies_ref[...] = jnp.broadcast_to(packed[None], copies_ref.shape)


def near_kernel(cycle_size, owners, pos_ref, cols_ref, low_ref, mid_ref, high_ref, vals_ref, near_ref):
    rows, panels = near_ref.shape
    kinds = cols_ref.shape[1]
    cols = cols_ref[...]
    target = lax.div(cols, jnp.int32(rows * owners))
    offset = lax.rem(target - pos_ref[0] + (cycle_size + 4), jnp.int32(cycle_size))
    row = offset * rows + lax.rem(cols, jnp.int32(rows))
    span = 3 * rows
    fields = []
    for k in range(kinds):
        index = row[:, k:k + 1]
        field = mul(pick(index, span), low_ref[...], NN)
        field = field + mul(pick(index - span, span), mid_ref[...], NN)
        field = field + mul(pick(index - 2 * span, span), high_ref[...], NN)
        fields.append(field.astype(BF16))
    group = 16
    for base in range(0, rows, group):
        parts = [field[base:base + group] for field in fields]
        total = jnp.zeros((group, panels), F32)
        for i in range(group):
            product = mul(parts[0], vals_ref[base + i, 0], NT)
            for k in range(1, kinds):
                product = product + mul(parts[k], vals_ref[base + i, k], NT)
            total = jnp.where(iota((group, panels), 0) == i, product, total)
        near_ref[base:base + group, :] = total


def potential(owners, rank, cols_ref, moments_ref, coupling_ref, target_ref, near_ref):
    rows, panels = near_ref.shape
    cols = cols_ref[...]
    owner = lax.rem(lax.div(cols, jnp.int32(rows)), jnp.int32(owners))
    within = lax.rem(cols, jnp.int32(rows))
    row = owner * (rows // 2) + lax.div(within, jnp.int32(2))
    upper = lax.rem(within, jnp.int32(2))
    lane_upper = iota((rows, panels), 1) // rank
    far_in = jnp.zeros((rows, panels), F32)
    for k in range(2):
        both = mul(pick(row[:, k:k + 1], moments_ref.shape[0]), moments_ref[...], NN)
        moved = jnp.where(upper[:, k:k + 1] == k, both, pltpu.roll(both, rank, 1))
        far_in = jnp.where(lane_upper == k, moved, far_in)
    far_in = far_in.astype(BF16)
    total = near_ref[...]
    for base in range(0, coupling_ref.shape[0], TILE):
        coupled = mul(far_in, coupling_ref[base:base + TILE, :], NT)
        block = (iota(coupled.shape, 1) + base) // rank
        coupled = jnp.where(block == iota(coupled.shape, 0), coupled, 0.0).astype(BF16)
        total = total + mul(coupled, target_ref[base:base + TILE, :], NN)
    return total


def middle_kernel(owners, rank, cols_ref, moments_ref, coupling_ref, target_ref, near_ref, source_ref,
                  potential_ref, second_ref, copies_ref):
    total = potential(owners, rank, cols_ref, moments_ref, coupling_ref, target_ref, near_ref)
    potential_ref[...] = total
    second = total.astype(BF16)
    second_ref[...] = second
    packed = packed_moments(second, source_ref, rank)
    copies_ref[...] = jnp.broadcast_to(packed[None], copies_ref.shape)


def last_kernel(owners, rank, cols_ref, moments_ref, coupling_ref, target_ref, near_ref, potential_ref):
    potential_ref[...] = potential(owners, rank, cols_ref, moments_ref, coupling_ref, target_ref, near_ref)


def call(kernel, outs, scalars=0):
    vmem = pl.BlockSpec(memory_space=pltpu.VMEM)

    def run(*operands):
        specs = [pl.BlockSpec(memory_space=pltpu.SMEM)] * scalars + [vmem] * (len(operands) - scalars)
        return pl.pallas_call(
            kernel,
            out_shape=outs,
            in_specs=specs,
            out_specs=jax.tree.map(lambda _: vmem, outs),
            compiler_params=pltpu.CompilerParams(vmem_limit_bytes=16 << 20),
        )(*operands)

    return run


def from_behind(block, axis, distance):
    size = lax.axis_size(axis)
    return lax.ppermute(block, axis, [((i - distance) % size, i) for i in range(size)])


def shards(charges, near_vals, near_cols, source_basis, target_basis, coupling, far_cols):
    owners = lax.axis_size("cluster")
    cycle_size = lax.axis_size("blk")
    rows, panels = charges.shape
    rank = source_basis.shape[1]
    pos = lax.axis_index("blk").reshape(1)
    source = source_basis.reshape(rows * rank, panels)
    target = target_basis.reshape(rows * rank, panels)
    coupling = coupling.transpose(0, 2, 1, 3).reshape(rows * rank, 2 * rank)
    copies = jax.ShapeDtypeStruct((owners, rows // 2, 2 * rank), BF16)
    field32 = jax.ShapeDtypeStruct((rows, panels), F32)
    field16 = jax.ShapeDtypeStruct((rows, panels), BF16)

    def far_exchange(copies):
        return lax.all_to_all(copies, "cluster", 0, 0, tiled=True).reshape(-1, 2 * rank)

    def near_part(charge):
        mid = jnp.concatenate([from_behind(charge, "blk", 1), charge, from_behind(charge, "blk", -1)], axis=0)
        low = from_behind(mid, "blk", 3)
        high = from_behind(mid, "blk", -3)
        run = call(functools.partial(near_kernel, cycle_size, owners), field32, 1)
        return run(pos, near_cols, low, mid, high, near_vals)

    first = call(functools.partial(first_kernel, rank), copies)(charges, source)
    near = near_part(charges)
    moments = far_exchange(first)
    middle = call(functools.partial(middle_kernel, owners, rank), (field32, field16, copies))
    potential_one, second, sent = middle(far_cols, moments, coupling, target, near, source)
    near = near_part(second)
    moments = far_exchange(sent)
    potential_two = call(functools.partial(last_kernel, owners, rank), field32)(far_cols, moments, coupling, target, near)
    return (potential_one, potential_two)


def solution(mesh):
    in_specs = (
        P(("blk", "cluster"), None),
        P(("blk", "cluster"), None, None, None),
        P(("blk", "cluster"), None),
        P(("blk", "cluster"), None, None),
        P(("blk", "cluster"), None, None),
        P(("blk", "cluster"), None, None, None),
        P(("blk", "cluster"), None),
    )
    out_specs = (P(("blk", "cluster"), None), P(("blk", "cluster"), None))
    return jax.shard_map(shards, mesh=mesh, in_specs=in_specs, out_specs=out_specs, check_vma=False)
```

time: 85.2 us -> 88.4 us (1.038)
  the two profiles are of different devices: /device:TPU:1 before, /device:TPU:22 now
where the time goes in v2:
time: 88.4 us; the launch traced here: 87.5 us
  starting transfers between devices  56.1 us (63%)
  local copies, waits for them, and re-layouts  14.4 us (16%)
  Pallas kernels  9.32 us (11%)
  waiting for transfers between devices  6.82 us (8%)
    ppermute x8, starting transfers between devices, from_behind(): lax.ppermute(block, axis, [((i - distance) % size, i) for i in range(size)])  32.9 us
    all_to_all x2, starting transfers between devices, far_exchange(): lax.all_to_all(copies, 'cluster', 0, 0, tiled=True).reshape(-1, 2 * rank)  23.2 us
    pallas_call x5, Pallas kernels, run(): pl.pallas_call(kernel, out_shape=outs, in_specs=specs, out_specs=jax.tree...  9.32 us
    unnamed x24, local copies, waits for them, and re-layouts  8.03 us
    ppermute x8, waiting for transfers between devices, from_behind(): lax.ppermute(block, axis, [((i - distance) % size, i) for i in range(size)])  6.81 us
    transpose x1, local copies, waits for them, and re-layouts, shards(): coupling = coupling.transpose(0, 2, 1, 3).reshape(rows * rank, 2 * rank)  3.29 us
    reshape x1, local copies, waits for them, and re-layouts, shards(): coupling = coupling.transpose(0, 2, 1, 3).reshape(rows * rank, 2 * rank)  3.07 us
  transfers between devices with their start and end apart: 10, of which 1 were waited for; matrix products, arithmetic and copies ran while one was open for 8% of the time, Pallas kernels for 5%

profile of v2, /device:TPU:22, one launch (start us, length us, event | category | flops | bytes accessed | tf_op | source)
XLA Modules:
  0.0 87.5 jit_solution(12064630608252971271)
XLA Ops:
  0.6 4.0 %collective-permute-start = (bf16[32,128]{1,0:T(8,128)(2,1)}, bf16[32,128]{1,0:T(8,128)(2,1)S(1)}, u32[]{:S(2)}, u32[]{:S(2)}) collective-permute-start(bf16[32,128]{1,0:T(8,128)(2,1)} %charge_ref.1), channel_id=1, source_target_pairs={{480,0},{0,32},{32,64},{64,96},{96,128},{128,160},{160,192},{192,2... | collective-permute-start | bytes 24584 | tf_op jit(solution)/shard_map/ppermute | solution.py:130
  4.7 2.1 %collective-permute-start.1 = (bf16[32,128]{1,0:T(8,128)(2,1)}, bf16[32,128]{1,0:T(8,128)(2,1)S(1)}, u32[]{:S(2)}, u32[]{:S(2)}) collective-permute-start(bf16[32,128]{1,0:T(8,128)(2,1)} %charge_ref.1), channel_id=1, source_target_pairs={{32,0},{64,32},{96,64},{128,96},{160,128},{192,160},{224,192},{256... | collective-permute-start | bytes 24584 | tf_op jit(solution)/shard_map/ppermute | solution.py:130
  6.8 0.0 copy-start.5
  6.8 1.0 %copy-done.5 = bf16[32,64,128]{2,1,0:T(8,128)(2,1)S(1)} copy-done((bf16[32,64,128]{2,1,0:T(8,128)(2,1)S(1)}, bf16[32,64,128]{2,1,0:T(8,128)(2,1)}, u32[]{:S(2)}) %copy-start.5) | copy-done | bytes 524312
  7.8 0.7 copy-done.7
  8.5 1.1 %shard_map.86 = bf16[32,16,128]{2,1,0:T(8,128)(2,1)} custom-call(bf16[32,128]{1,0:T(8,128)(2,1)S(1)} %copy-done.7, bf16[2048,128]{1,0:T(8,128)(2,1)S(1)} %bitcast.8), custom_call_target="tpu_custom_call" | custom-call | tf_op jit(solution)/shard_map/pallas_call | solution.py:117
  9.6 13.4 %all-to-all-start = ((bf16[32,16,128]{2,1,0:T(8,128)(2,1)}), bf16[32,16,128]{2,1,0:T(8,128)(2,1)S(1)}, u32[]{:S(2)}, u32[]{:S(2)}) async-start(bf16[32,16,128]{2,1,0:T(8,128)(2,1)} %shard_map.86), calls=%async_computation | async-start | bytes 262144 | tf_op jit(solution)/shard_map/all_to_all | solution.py:147
  23.1 8.1 %collective-permute-start.2 = (bf16[96,128]{1,0:T(8,128)(2,1)S(1)}, bf16[96,128]{1,0:T(8,128)(2,1)S(1)}, u32[]{:S(2)}, u32[]{:S(2)}) collective-permute-start(bf16[96,128]{1,0:T(8,128)(2,1)S(1)} %constant_dynamic-update-slice_fusion.mid_ref), channel_id=1, source_target_pairs={{416,0},{448,32},{480,64},{0,96},{32,128},{64,160},{96,192},{128,2... | collective-permute-start | bytes 73736 | tf_op jit(solution)/shard_map/ppermute | solution.py:130
  31.2 1.9 %collective-permute-start.3 = (bf16[96,128]{1,0:T(8,128)(2,1)S(1)}, bf16[96,128]{1,0:T(8,128)(2,1)S(1)}, u32[]{:S(2)}, u32[]{:S(2)}) collective-permute-start(bf16[96,128]{1,0:T(8,128)(2,1)S(1)} %constant_dynamic-update-slice_fusion.mid_ref), channel_id=1, source_target_pairs={{96,0},{128,32},{160,64},{192,96},{224,128},{256,160},{288,192},{3... | collective-permute-start | bytes 73736 | tf_op jit(solution)/shard_map/ppermute | solution.py:130
  33.1 0.8 copy.10.cols_ref
  33.9 3.3 %copy.9 = bf16[32,64,2,64]{3,2,1,0:T(2,128)(2,1)} copy(bf16[32,64,2,64]{3,1,2,0:T(8,128)(2,1)} %bitcast.12) | data formatting | bytes 1048576 | tf_op jit(solution)/shard_map/transpose | solution.py:141
  37.1 3.1 %reshape.24.coupling_ref = bf16[2048,128]{1,0:T(8,128)(2,1)} reshape(bf16[32,64,2,64]{3,2,1,0:T(2,128)(2,1)} %copy.9) | data formatting | bytes 1048576 | tf_op jit(solution)/shard_map/reshape | solution.py:141
  40.2 0.1 copy.11.cols_ref
  40.3 1.8 %shard_map.87.near_ref = f32[32,128]{1,0:T(8,128)S(1)} custom-call(s32[1]{0:T(128)} %bitcast.4.pos_ref, s32[32,3]{1,0:T(8,128)S(1)} %copy.10.cols_ref, bf16[96,128]{1,0:T(8,128)(2,1)S(1)} %collective-permute-done.2.low_ref, bf16[96,128]{1,0:T(8,128)(2,1)S(1)} %constant_dynamic-update-slice_fusion.mid_ref, ...), custom_call_target="tpu_custom_call" | custom-call | tf_op jit(solution)/shard_map/pallas_call | solution.py:117
  42.2 0.0 all-to-all-done
  42.2 0.0 copy-start.1
  42.2 1.1 %copy-done.1 = bf16[2048,128]{1,0:T(8,128)(2,1)S(1)} copy-done((bf16[2048,128]{1,0:T(8,128)(2,1)S(1)}, bf16[2048,128]{1,0:T(8,128)(2,1)}, u32[]{:S(2)}) %copy-start.1) | copy-done | bytes 524312
  43.3 1.0 %copy-done.3 = bf16[32,64,128]{2,1,0:T(8,128)(2,1)S(1)} copy-done((bf16[32,64,128]{2,1,0:T(8,128)(2,1)S(1)}, bf16[32,64,128]{2,1,0:T(8,128)(2,1)}, u32[]{:S(2)}) %copy-start.3) | copy-done | bytes 524312
  44.4 1.0 %copy-done.6 = bf16[32,64,128]{2,1,0:T(8,128)(2,1)S(1)} copy-done((bf16[32,64,128]{2,1,0:T(8,128)(2,1)S(1)}, bf16[32,64,128]{2,1,0:T(8,128)(2,1)}, u32[]{:S(2)}) %copy-start.6) | copy-done | bytes 524312
  45.4 2.5 %shard_map.88 = (f32[32,128]{1,0:T(8,128)}, bf16[32,128]{1,0:T(8,128)(2,1)S(1)}, bf16[32,16,128]{2,1,0:T(8,128)(2,1)}) custom-call(s32[32,2]{1,0:T(8,128)S(1)} %copy.11.cols_ref, bf16[512,128]{1,0:T(8,128)(2,1)S(1)} %bitcast.11, bf16[2048,128]{1,0:T(8,128)(2,1)S(1)} %copy-done.1, bf16[2048,128]{1,0:T(8,128)(2,1)S(1)} %bitcast.6, ...), custom_call_target="tpu_custom_call" | custom-call | tf_op jit(solution)/shard_map/pallas_call | solution.py:117
  47.9 2.3 %collective-permute-start.4 = (bf16[32,128]{1,0:T(8,128)(2,1)S(1)}, bf16[32,128]{1,0:T(8,128)(2,1)S(1)}, u32[]{:S(2)}, u32[]{:S(2)}) collective-permute-start(bf16[32,128]{1,0:T(8,128)(2,1)S(1)} %get-tuple-element.7), channel_id=1, source_target_pairs={{480,0},{0,32},{32,64},{64,96},{96,128},{128,160},{160,192},{192,2... | collective-permute-start | bytes 24584 | tf_op jit(solution)/shard_map/ppermute | solution.py:130
  50.2 3.6 %collective-permute-start.5 = (bf16[32,128]{1,0:T(8,128)(2,1)S(1)}, bf16[32,128]{1,0:T(8,128)(2,1)S(1)}, u32[]{:S(2)}, u32[]{:S(2)}) collective-permute-start(bf16[32,128]{1,0:T(8,128)(2,1)S(1)} %get-tuple-element.7), channel_id=1, source_target_pairs={{32,0},{64,32},{96,64},{128,96},{160,128},{192,160},{224,192},{256... | collective-permute-start | bytes 24584 | tf_op jit(solution)/shard_map/ppermute | solution.py:130
  53.7 9.8 %all-to-all-start.1 = ((bf16[32,16,128]{2,1,0:T(8,128)(2,1)}), bf16[32,16,128]{2,1,0:T(8,128)(2,1)S(1)}, u32[]{:S(2)}, u32[]{:S(2)}) async-start(bf16[32,16,128]{2,1,0:T(8,128)(2,1)} %get-tuple-element.6), calls=%async_computation.1 | async-start | bytes 262144 | tf_op jit(solution)/shard_map/all_to_all | solution.py:147
  63.6 9.0 %collective-permute-start.6 = (bf16[96,128]{1,0:T(8,128)(2,1)S(1)}, bf16[96,128]{1,0:T(8,128)(2,1)S(1)}, u32[]{:S(2)}, u32[]{:S(2)}) collective-permute-start(bf16[96,128]{1,0:T(8,128)(2,1)S(1)} %constant_dynamic-update-slice_fusion.3.mid_ref), channel_id=1, source_target_pairs={{416,0},{448,32},{480,64},{0,96},{32,128},{64,160},{96,192},{128,2... | collective-permute-start | bytes 73736 | tf_op jit(solution)/shard_map/ppermute | solution.py:130
  72.6 1.9 %collective-permute-start.7 = (bf16[96,128]{1,0:T(8,128)(2,1)S(1)}, bf16[96,128]{1,0:T(8,128)(2,1)S(1)}, u32[]{:S(2)}, u32[]{:S(2)}) collective-permute-start(bf16[96,128]{1,0:T(8,128)(2,1)S(1)} %constant_dynamic-update-slice_fusion.3.mid_ref), channel_id=1, source_target_pairs={{96,0},{128,32},{160,64},{192,96},{224,128},{256,160},{288,192},{3... | collective-permute-start | bytes 73736 | tf_op jit(solution)/shard_map/ppermute | solution.py:130
  74.6 6.8 %collective-permute-done.7.high_ref = bf16[96,128]{1,0:T(8,128)(2,1)S(1)} collective-permute-done((bf16[96,128]{1,0:T(8,128)(2,1)S(1)}, bf16[96,128]{1,0:T(8,128)(2,1)S(1)}, u32[]{:S(2)}, u32[]{:S(2)}) %collective-permute-start.7) | collective-permute-done | bytes 24608 | tf_op jit(solution)/shard_map/ppermute | solution.py:130
  81.4 1.8 %shard_map.89.near_ref = f32[32,128]{1,0:T(8,128)S(1)} custom-call(s32[1]{0:T(128)} %bitcast.4.pos_ref, s32[32,3]{1,0:T(8,128)S(1)} %copy.10.cols_ref, bf16[96,128]{1,0:T(8,128)(2,1)S(1)} %collective-permute-done.6.low_ref, bf16[96,128]{1,0:T(8,128)(2,1)S(1)} %constant_dynamic-update-slice_fusion.3.mid_ref, ...), custom_call_target="tpu_custom_call" | custom-call | tf_op jit(solution)/shard_map/pallas_call | solution.py:117
  83.2 0.0 all-to-all-done.1
  83.2 0.0 copy-start.2
  83.2 1.1 %copy-done.2 = bf16[2048,128]{1,0:T(8,128)(2,1)S(1)} copy-done((bf16[2048,128]{1,0:T(8,128)(2,1)S(1)}, bf16[2048,128]{1,0:T(8,128)(2,1)}, u32[]{:S(2)}) %copy-start.2) | copy-done | bytes 524312
  84.4 1.0 %copy-done.4 = bf16[32,64,128]{2,1,0:T(8,128)(2,1)S(1)} copy-done((bf16[32,64,128]{2,1,0:T(8,128)(2,1)S(1)}, bf16[32,64,128]{2,1,0:T(8,128)(2,1)}, u32[]{:S(2)}) %copy-start.4) | copy-done | bytes 524312
  85.4 2.1 %shard_map.90 = f32[32,128]{1,0:T(8,128)} custom-call(s32[32,2]{1,0:T(8,128)S(1)} %copy.11.cols_ref, bf16[512,128]{1,0:T(8,128)(2,1)S(1)} %bitcast.10, bf16[2048,128]{1,0:T(8,128)(2,1)S(1)} %copy-done.2, bf16[2048,128]{1,0:T(8,128)(2,1)S(1)} %bitcast.7, f32[32,128]{1,0:T(8,128)S(1)} %shard_map.89.near_ref), custom_call_target="tpu_custom_call" | custom-call | tf_op jit(solution)/shard_map/pallas_call | solution.py:117
  (21 shorter events, 0.1 us)
Async XLA Ops:
  0.6 39.7 %copy-start = (bf16[32,3,128,128]{3,2,1,0:T(8,128)(2,1)S(1)}, bf16[32,3,128,128]{3,2,1,0:T(8,128)(2,1)}, u32[]{:S(2)}) copy-start(bf16[32,3,128,128]{3,2,1,0:T(8,128)(2,1)} %vals_ref.3) | copy-start | bytes 9437188
  0.6 22.4 %collective-permute-start = (bf16[32,128]{1,0:T(8,128)(2,1)}, bf16[32,128]{1,0:T(8,128)(2,1)S(1)}, u32[]{:S(2)}, u32[]{:S(2)}) collective-permute-start(bf16[32,128]{1,0:T(8,128)(2,1)} %charge_ref.1), channel_id=1, source_target_pairs={{480,0},{0,32},{32,64},{64,96},{96,128},{128,160},{160,192},{192,2... | collective-permute-start | bytes 24584 | tf_op jit(solution)/shard_map/ppermute | solution.py:130
  4.7 18.4 %collective-permute-start.1 = (bf16[32,128]{1,0:T(8,128)(2,1)}, bf16[32,128]{1,0:T(8,128)(2,1)S(1)}, u32[]{:S(2)}, u32[]{:S(2)}) collective-permute-start(bf16[32,128]{1,0:T(8,128)(2,1)} %charge_ref.1), channel_id=1, source_target_pairs={{32,0},{64,32},{96,64},{128,96},{160,128},{192,160},{224,192},{256... | collective-permute-start | bytes 24584 | tf_op jit(solution)/shard_map/ppermute | solution.py:130
  6.8 1.0 %copy-start.5 = (bf16[32,64,128]{2,1,0:T(8,128)(2,1)S(1)}, bf16[32,64,128]{2,1,0:T(8,128)(2,1)}, u32[]{:S(2)}) copy-start(bf16[32,64,128]{2,1,0:T(8,128)(2,1)} %param.10) | copy-start | bytes 1572868
  7.8 0.7 copy-start.7
  8.5 31.7 %copy-start.8 = (s32[32,2]{0,1:T(2,128)S(1)}, s32[32,2]{0,1:T(2,128)}, u32[]{:S(2)}) copy-start(s32[32,2]{0,1:T(2,128)} %param.13) | copy-start | bytes 772
  9.6 32.6 %all-to-all-start = ((bf16[32,16,128]{2,1,0:T(8,128)(2,1)}), bf16[32,16,128]{2,1,0:T(8,128)(2,1)S(1)}, u32[]{:S(2)}, u32[]{:S(2)}) async-start(bf16[32,16,128]{2,1,0:T(8,128)(2,1)} %shard_map.86), calls=%async_computation | async-start | bytes 262144 | tf_op jit(solution)/shard_map/all_to_all | solution.py:147
  23.1 17.2 %collective-permute-start.2 = (bf16[96,128]{1,0:T(8,128)(2,1)S(1)}, bf16[96,128]{1,0:T(8,128)(2,1)S(1)}, u32[]{:S(2)}, u32[]{:S(2)}) collective-permute-start(bf16[96,128]{1,0:T(8,128)(2,1)S(1)} %constant_dynamic-update-slice_fusion.mid_ref), channel_id=1, source_target_pairs={{416,0},{448,32},{480,64},{0,96},{32,128},{64,160},{96,192},{128,2... | collective-permute-start | bytes 73736 | tf_op jit(solution)/shard_map/ppermute | solution.py:130
  31.2 9.2 %collective-permute-start.3 = (bf16[96,128]{1,0:T(8,128)(2,1)S(1)}, bf16[96,128]{1,0:T(8,128)(2,1)S(1)}, u32[]{:S(2)}, u32[]{:S(2)}) collective-permute-start(bf16[96,128]{1,0:T(8,128)(2,1)S(1)} %constant_dynamic-update-slice_fusion.mid_ref), channel_id=1, source_target_pairs={{96,0},{128,32},{160,64},{192,96},{224,128},{256,160},{288,192},{3... | collective-permute-start | bytes 73736 | tf_op jit(solution)/shard_map/ppermute | solution.py:130
  42.2 1.2 %copy-start.1 = (bf16[2048,128]{1,0:T(8,128)(2,1)S(1)}, bf16[2048,128]{1,0:T(8,128)(2,1)}, u32[]{:S(2)}) copy-start(bf16[2048,128]{1,0:T(8,128)(2,1)} %reshape.24.coupling_ref) | copy-start | bytes 1572868
  43.3 1.0 %copy-start.3 = (bf16[32,64,128]{2,1,0:T(8,128)(2,1)S(1)}, bf16[32,64,128]{2,1,0:T(8,128)(2,1)}, u32[]{:S(2)}) copy-start(bf16[32,64,128]{2,1,0:T(8,128)(2,1)} %param.11) | copy-start | bytes 1572868
  44.4 1.0 %copy-start.6 = (bf16[32,64,128]{2,1,0:T(8,128)(2,1)S(1)}, bf16[32,64,128]{2,1,0:T(8,128)(2,1)}, u32[]{:S(2)}) copy-start(bf16[32,64,128]{2,1,0:T(8,128)(2,1)} %param.10) | copy-start | bytes 1572868
  47.9 15.6 %collective-permute-start.4 = (bf16[32,128]{1,0:T(8,128)(2,1)S(1)}, bf16[32,128]{1,0:T(8,128)(2,1)S(1)}, u32[]{:S(2)}, u32[]{:S(2)}) collective-permute-start(bf16[32,128]{1,0:T(8,128)(2,1)S(1)} %get-tuple-element.7), channel_id=1, source_target_pairs={{480,0},{0,32},{32,64},{64,96},{96,128},{128,160},{160,192},{192,2... | collective-permute-start | bytes 24584 | tf_op jit(solution)/shard_map/ppermute | solution.py:130
  50.2 13.4 %collective-permute-start.5 = (bf16[32,128]{1,0:T(8,128)(2,1)S(1)}, bf16[32,128]{1,0:T(8,128)(2,1)S(1)}, u32[]{:S(2)}, u32[]{:S(2)}) collective-permute-start(bf16[32,128]{1,0:T(8,128)(2,1)S(1)} %get-tuple-element.7), channel_id=1, source_target_pairs={{32,0},{64,32},{96,64},{128,96},{160,128},{192,160},{224,192},{256... | collective-permute-start | bytes 24584 | tf_op jit(solution)/shard_map/ppermute | solution.py:130
  53.7 29.5 %all-to-all-start.1 = ((bf16[32,16,128]{2,1,0:T(8,128)(2,1)}), bf16[32,16,128]{2,1,0:T(8,128)(2,1)S(1)}, u32[]{:S(2)}, u32[]{:S(2)}) async-start(bf16[32,16,128]{2,1,0:T(8,128)(2,1)} %get-tuple-element.6), calls=%async_computation.1 | async-start | bytes 262144 | tf_op jit(solution)/shard_map/all_to_all | solution.py:147
  63.6 11.0 %collective-permute-start.6 = (bf16[96,128]{1,0:T(8,128)(2,1)S(1)}, bf16[96,128]{1,0:T(8,128)(2,1)S(1)}, u32[]{:S(2)}, u32[]{:S(2)}) collective-permute-start(bf16[96,128]{1,0:T(8,128)(2,1)S(1)} %constant_dynamic-update-slice_fusion.3.mid_ref), channel_id=1, source_target_pairs={{416,0},{448,32},{480,64},{0,96},{32,128},{64,160},{96,192},{128,2... | collective-permute-start | bytes 73736 | tf_op jit(solution)/shard_map/ppermute | solution.py:130
  72.6 8.7 %collective-permute-start.7 = (bf16[96,128]{1,0:T(8,128)(2,1)S(1)}, bf16[96,128]{1,0:T(8,128)(2,1)S(1)}, u32[]{:S(2)}, u32[]{:S(2)}) collective-permute-start(bf16[96,128]{1,0:T(8,128)(2,1)S(1)} %constant_dynamic-update-slice_fusion.3.mid_ref), channel_id=1, source_target_pairs={{96,0},{128,32},{160,64},{192,96},{224,128},{256,160},{288,192},{3... | collective-permute-start | bytes 73736 | tf_op jit(solution)/shard_map/ppermute | solution.py:130
  83.2 1.2 %copy-start.2 = (bf16[2048,128]{1,0:T(8,128)(2,1)S(1)}, bf16[2048,128]{1,0:T(8,128)(2,1)}, u32[]{:S(2)}) copy-start(bf16[2048,128]{1,0:T(8,128)(2,1)} %reshape.24.coupling_ref) | copy-start | bytes 1572868
  84.4 1.0 %copy-start.4 = (bf16[32,64,128]{2,1,0:T(8,128)(2,1)S(1)}, bf16[32,64,128]{2,1,0:T(8,128)(2,1)}, u32[]{:S(2)}) copy-start(bf16[32,64,128]{2,1,0:T(8,128)(2,1)} %param.11) | copy-start | bytes 1572868

commit v3 on v1

v3 whole, which is shorter than its diff:
```python
import functools

import jax
import jax.numpy as jnp
from jax import lax
from jax.experimental import pallas as pl
from jax.experimental.pallas import tpu as pltpu
from jax.sharding import PartitionSpec as P

F32 = jnp.float32
BF16 = jnp.bfloat16
NT = (((1,), (1,)), ((), ()))
NN = (((1,), (0,)), ((), ()))
CHUNK = 4
LANES = 128


def mul(a, b, dims):
    return lax.dot_general(a, b, dims, preferred_element_type=F32)


def iota(shape, dim):
    return lax.broadcasted_iota(jnp.int32, shape, dim)


def pick(index, depth):
    rows = index.shape[0]
    return jnp.where(iota((rows, depth), 1) == index, 1.0, 0.0).astype(BF16)


def column(row):
    size = row.shape[1]
    square = (size, size)
    spread = jnp.broadcast_to(row.astype(F32), square)
    chosen = jnp.where(iota(square, 0) == iota(square, 1), spread, 0.0)
    return jnp.sum(chosen, axis=1, keepdims=True).astype(jnp.int32)


def padded(field):
    rows = field.shape[0]
    return jnp.concatenate([field, jnp.zeros((LANES - rows, field.shape[1]), field.dtype)], axis=0)


def own_columns(blocks, height, product):
    total = jnp.zeros((height, LANES), F32)
    lane = iota((height, LANES), 1)
    for base in range(0, blocks, CHUNK):
        result = product(base)
        for i in range(CHUNK):
            total = jnp.where(lane == base + i, result[i * height:(i + 1) * height], total)
    return total


def send_moments(field, source_ref, copies_ref):
    blocks = field.shape[0]
    rank = source_ref.shape[0] // blocks
    wide = padded(field)

    def product(base):
        return mul(source_ref[base * rank:(base + CHUNK) * rank, :], wide, NT)

    moments = own_columns(blocks, rank, product)
    moments = jnp.concatenate([moments, jnp.zeros((LANES - rank, LANES), F32)], axis=0).T
    half = blocks // 2
    packed = moments[:half] + pltpu.roll(moments[half:blocks], rank, 1)
    copies_ref[...] = jnp.broadcast_to(packed.astype(BF16)[None], copies_ref.shape)


def first_kernel(charge_hbm, source_hbm, target_hbm, coupling_hbm, copies_ref, source_ref, target_ref, coupling_ref,
                 charge_ref, sems):
    pairs = [(charge_hbm, charge_ref), (source_hbm, source_ref), (coupling_hbm, coupling_ref), (target_hbm, target_ref)]
    moves = [pltpu.make_async_copy(a, b, sems.at[n]) for n, (a, b) in enumerate(pairs)]
    for move in moves:
        move.start()
    moves[0].wait()
    moves[1].wait()
    send_moments(charge_ref[...], source_ref, copies_ref)
    moves[2].wait()
    moves[3].wait()


def moments_kernel(field_ref, source_ref, copies_ref):
    send_moments(field_ref[...], source_ref, copies_ref)


def fetch(source, dest, sems):
    moves = []
    for n in range(dest.shape[0] // CHUNK):
        part = pl.ds(n * CHUNK, CHUNK)
        moves.append(pltpu.make_async_copy(source.at[part], dest.at[part], sems.at[n]))
    for move in moves:
        move.start()
    return moves


def own_kernel(field_ref, vals_hbm, near_ref, vals_ref, sems):
    blocks, panels = field_ref.shape
    moves = fetch(vals_hbm.at[:, pl.ds(0, 1)], vals_ref, sems)
    wide = padded(field_ref[...])

    def product(base):
        moves[base // CHUNK].wait()
        return mul(vals_ref[base:base + CHUNK, 0].reshape(CHUNK * panels, panels), wide, NT)

    near_ref[...] = own_columns(blocks, panels, product).T[:blocks]


def near_kernel(cycle_size, owners, pos_ref, cols_ref, low_ref, high_ref, vals_hbm, own_ref, near_ref, vals_ref, sems):
    blocks, panels = own_ref.shape
    moves = fetch(vals_hbm.at[:, pl.ds(1, vals_ref.shape[1])], vals_ref, sems)
    kinds = cols_ref.shape[0]
    cols = cols_ref[...]
    target = lax.div(cols, jnp.int32(blocks * owners))
    offset = lax.rem(target - pos_ref[0] + (cycle_size + 3), jnp.int32(cycle_size))
    row = offset * blocks + lax.rem(cols, jnp.int32(blocks))
    span = low_ref.shape[0]
    fields = []
    for k in range(1, kinds):
        index = column(row[k:k + 1])
        field = mul(pick(index, span), low_ref[...], NN)
        beyond = jnp.where(index >= span, index - (span - blocks), -1)
        field = field + mul(pick(beyond, span), high_ref[...], NN)
        fields.append(field.astype(BF16))
    wide = padded(jnp.concatenate(fields, axis=1))

    def product(base):
        moves[base // CHUNK].wait()
        vals = [vals_ref[base:base + CHUNK, k].reshape(CHUNK * panels, panels) for k in range(kinds - 1)]
        return mul(jnp.concatenate(vals, axis=1), wide, NT)

    near_ref[...] = own_ref[...] + own_columns(blocks, panels, product).T[:blocks]


def potential(owners, cols_ref, moments_ref, coupling_ref, target_ref, near_ref):
    blocks, panels = near_ref.shape
    kinds = cols_ref.shape[0]
    rank = coupling_ref.shape[2]
    half = blocks // 2
    cols = cols_ref[...]
    owner = lax.rem(lax.div(cols, jnp.int32(blocks)), jnp.int32(owners))
    within = lax.rem(cols, jnp.int32(blocks))
    row = owner * half + lax.rem(within, jnp.int32(half))
    upper = lax.div(within, jnp.int32(half))
    fields = []
    for k in range(kinds):
        both = mul(pick(column(row[k:k + 1]), moments_ref.shape[0]), moments_ref[...], NN)
        both = jnp.where(column(upper[k:k + 1]) == 1, pltpu.roll(both, rank, 1), both)
        fields.append(padded(both[:, :rank].astype(BF16)))

    def product(base):
        result = None
        for k in range(kinds):
            couple = coupling_ref[base:base + CHUNK, k].reshape(CHUNK * rank, rank)
            part = mul(couple, fields[k], NT)
            result = part if result is None else result + part
        return result

    coupled = own_columns(blocks, rank, product)
    coupled = jnp.concatenate([coupled, coupled], axis=0).T[:blocks]
    total = near_ref[...]
    step = 2 * LANES
    wide = jnp.concatenate([coupled, coupled], axis=1)
    for base in range(0, target_ref.shape[0], step):
        block = (iota(wide.shape, 1) + base) // rank
        kept = jnp.where(block == iota(wide.shape, 0), wide, 0.0).astype(BF16)
        total = total + mul(kept, target_ref[base:base + step, :], NN)
    return total


def middle_kernel(owners, cols_ref, moments_ref, coupling_ref, target_ref, near_ref, potential_ref, second_ref):
    total = potential(owners, cols_ref, moments_ref, coupling_ref, target_ref, near_ref)
    potential_ref[...] = total
    second_ref[...] = total.astype(BF16)


def last_kernel(owners, cols_ref, moments_ref, coupling_ref, target_ref, near_ref, potential_ref):
    potential_ref[...] = potential(owners, cols_ref, moments_ref, coupling_ref, target_ref, near_ref)


VMEM = pl.BlockSpec(memory_space=pltpu.VMEM)
SMEM = pl.BlockSpec(memory_space=pltpu.SMEM)
HBM = pl.BlockSpec(memory_space=pltpu.HBM)


def call(kernel, outs, *operands, specs=None, scratch=(), flops=0, moved=0):
    return pl.pallas_call(
        kernel,
        out_shape=outs,
        in_specs=specs or [VMEM] * len(operands),
        out_specs=[VMEM] * len(outs) if isinstance(outs, tuple) else VMEM,
        scratch_shapes=scratch,
        compiler_params=pltpu.CompilerParams(vmem_limit_bytes=16 << 20),
        cost_estimate=pl.CostEstimate(flops=flops, bytes_accessed=moved, transcendentals=0),
    )(*operands)


def from_behind(block, axis, distance):
    size = lax.axis_size(axis)
    return lax.ppermute(block, axis, [((i - distance) % size, i) for i in range(size)])


def shards(charges, near_vals, near_cols, source_basis, target_basis, coupling, far_cols):
    owners = lax.axis_size("cluster")
    cycle_size = lax.axis_size("blk")
    blocks, panels = charges.shape
    rank = source_basis.shape[1]
    pos = lax.axis_index("blk").reshape(1)
    near_cols = near_cols.T
    far_cols = far_cols.T
    shape = jax.ShapeDtypeStruct
    basis = shape((blocks * rank, panels), BF16)
    copies = shape((owners, blocks // 2, 2 * rank), BF16)
    field32 = shape((blocks, panels), F32)
    field16 = shape((blocks, panels), BF16)
    tile = 2 * blocks * panels * panels

    def far_exchange(copies):
        return lax.all_to_all(copies, "cluster", 0, 0, tiled=True).reshape(-1, 2 * rank)

    def near_part(charge, behind):
        own = call(own_kernel, field32, charge, near_vals, specs=[VMEM, HBM], scratch=stage(1), flops=32 * tile, moved=tile)
        pair = jnp.concatenate([behind, charge], axis=0)
        low = jnp.concatenate([from_behind(pair, "blk", 2), pair], axis=0)
        high = from_behind(low, "blk", -3)
        kernel = functools.partial(near_kernel, cycle_size, owners)
        return call(kernel, field32, pos, near_cols, low, high, near_vals, own,
                    specs=[SMEM] + [VMEM] * 3 + [HBM, VMEM], scratch=stage(near_vals.shape[1] - 1), flops=64 * tile, moved=2 * tile)

    def stage(kinds):
        return [pltpu.VMEM((blocks, kinds, panels, panels), BF16), pltpu.SemaphoreType.DMA((blocks // CHUNK,))]

    def pinned(place, *arrays):
        return [pltpu.with_memory_space_constraint(array, place) for array in arrays]

    near_vals, = pinned(pltpu.HBM, near_vals)
    kept = pltpu.VMEM(basis.shape, BF16)
    operands = (charges, source_basis.reshape(basis.shape), target_basis.reshape(basis.shape), coupling)
    sent, source, target, coupling = call(
        first_kernel, (copies, kept, kept, pltpu.VMEM(coupling.shape, BF16)), *pinned(pltpu.HBM, *operands),
        specs=[HBM] * 4, scratch=[pltpu.VMEM(charges.shape, BF16), pltpu.SemaphoreType.DMA((4,))],
        flops=16 * tile, moved=2 * tile)
    source, target, coupling = pinned(pltpu.VMEM, source, target, coupling)
    behind, sent = lax.optimization_barrier((from_behind(charges, "blk", 1), sent))
    near = near_part(charges, behind)
    moments = far_exchange(sent)
    potential_one, second = call(functools.partial(middle_kernel, owners), (field32, field16),
                                 far_cols, moments, coupling, target, near, flops=48 * tile, moved=tile)
    sent = call(moments_kernel, copies, second, source, flops=16 * tile, moved=tile)
    behind, sent = lax.optimization_barrier((from_behind(second, "blk", 1), sent))
    near = near_part(second, behind)
    moments = far_exchange(sent)
    potential_two = call(functools.partial(last_kernel, owners), field32,
                         far_cols, moments, coupling, target, near, flops=48 * tile, moved=tile)
    return (potential_one, potential_two)


def solution(mesh):
    in_specs = (
        P(("blk", "cluster"), None),
        P(("blk", "cluster"), None, None, None),
        P(("blk", "cluster"), None),
        P(("blk", "cluster"), None, None),
        P(("blk", "cluster"), None, None),
        P(("blk", "cluster"), None, None, None),
        P(("blk", "cluster"), None),
    )
    out_specs = (P(("blk", "cluster"), None), P(("blk", "cluster"), None))
    return jax.shard_map(shards, mesh=mesh, in_specs=in_specs, out_specs=out_specs, check_vma=False)
```

time: 85.2 us -> 73.6 us (0.86)
  the two profiles are of different devices: /device:TPU:1 before, /device:TPU:17 now
where the time goes in v3:
time: 73.6 us; the launch traced here: 73 us
  starting transfers between devices  46.8 us (64%)
  Pallas kernels  17.8 us (24%)
  waiting for transfers between devices  5.35 us (7%)
  local copies, waits for them, and re-layouts  1.44 us (2%)
  between operations  0.8 us (1%)
    all_to_all x2, starting transfers between devices, far_exchange(): lax.all_to_all(copies, 'cluster', 0, 0, tiled=True).reshape(-1, 2 * rank)  27.1 us
    ppermute x6, starting transfers between devices, from_behind(): lax.ppermute(block, axis, [((i - distance) % size, i) for i in range(size)])  19.7 us
    pallas_call x8, Pallas kernels, call(): pl.pallas_call(kernel, out_shape=outs, in_specs=specs or [VMEM] * len(ope...  17.8 us
    all_to_all x2, waiting for transfers between devices, far_exchange(): lax.all_to_all(copies, 'cluster', 0, 0, tiled=True).reshape(-1, 2 * rank)  2.76 us
    ppermute x6, waiting for transfers between devices, from_behind(): lax.ppermute(block, axis, [((i - distance) % size, i) for i in range(size)])  2.59 us
  transfers between devices with their start and end apart: 8, of which 6 were waited for; matrix products, arithmetic and copies ran while one was open for 1% of the time, Pallas kernels for 20%

profile of v3, /device:TPU:17, one launch (start us, length us, event | category | flops | bytes accessed | tf_op | source)
XLA Modules:
  0.0 73.0 jit_solution(1450423264720041752)
XLA Ops:
  0.6 0.0 copy-start.1
  0.6 3.1 %collective-permute-start = (bf16[32,128]{1,0:T(8,128)(2,1)}, bf16[32,128]{1,0:T(8,128)(2,1)S(1)}, u32[]{:S(2)}, u32[]{:S(2)}) collective-permute-start(bf16[32,128]{1,0:T(8,128)(2,1)} %field_ref.1), channel_id=1, source_target_pairs={{480,0},{0,32},{32,64},{64,96},{96,128},{128,160},{160,192},{192,2... | collective-permute-start | bytes 24584 | tf_op jit(solution)/shard_map/ppermute | solution.py:199
  3.8 2.2 %shard_map.86 = (bf16[32,16,128]{2,1,0:T(8,128)(2,1)}, bf16[2048,128]{1,0:T(8,128)(2,1)S(1)}, bf16[2048,128]{1,0:T(8,128)(2,1)S(1)}, bf16[32,2,64,64]{3,2,1,0:T(8,128)(2,1)S(1)}) custom-call(bf16[32,128]{1,0:T(8,128)(2,1)} %field_ref.1, bf16[2048,128]{1,0:T(8,128)(2,1)} %bitcast.13, bf16[2048,128]{1,0:T(8,128)(2,1)} %bitcast.14, ...), custom_call_target="tpu_custom_call" | custom-call | flops 16777216 | bytes 2097152 | tf_op jit(solution)/shard_map/pallas_call | solution.py:186
  6.0 0.2 collective-permute-done
  6.1 0.7 pad_maximum_fusion
  6.8 3.2 %collective-permute-start.1 = (bf16[64,128]{1,0:T(8,128)(2,1)S(1)}, bf16[64,128]{1,0:T(8,128)(2,1)S(1)}, u32[]{:S(2)}, u32[]{:S(2)}) collective-permute-start(bf16[64,128]{1,0:T(8,128)(2,1)S(1)} %pad_maximum_fusion), channel_id=1, source_target_pairs={{448,0},{480,32},{0,64},{32,96},{64,128},{96,160},{128,192},{160,2... | collective-permute-start | bytes 49160 | tf_op jit(solution)/shard_map/ppermute | solution.py:199
  10.0 15.0 %all-to-all-start = ((bf16[32,16,128]{2,1,0:T(8,128)(2,1)}), bf16[32,16,128]{2,1,0:T(8,128)(2,1)S(1)}, u32[]{:S(2)}, u32[]{:S(2)}) async-start(bf16[32,16,128]{2,1,0:T(8,128)(2,1)} %get-tuple-element.13), calls=%async_computation | async-start | bytes 262144 | tf_op jit(solution)/shard_map/all_to_all | solution.py:218
  25.1 0.0 collective-permute-done.1
  25.1 0.7 constant_dynamic-update-slice_fusion.low_ref
  25.8 1.9 %collective-permute-start.2 = (bf16[128,128]{1,0:T(8,128)(2,1)S(1)}, bf16[128,128]{1,0:T(8,128)(2,1)S(1)}, u32[]{:S(2)}, u32[]{:S(2)}) collective-permute-start(bf16[128,128]{1,0:T(8,128)(2,1)S(1)} %constant_dynamic-update-slice_fusion.low_ref), channel_id=1, source_target_pairs={{96,0},{128,32},{160,64},{192,96},{224,128},{256,160},{288,192},{3... | collective-permute-start | bytes 98312 | tf_op jit(solution)/shard_map/ppermute | solution.py:199
  27.8 0.0 copy-start
  27.8 0.7 copy-done
  28.5 0.0 copy-start.2
  28.5 2.6 %shard_map.87.own_ref = f32[32,128]{1,0:T(8,128)S(1)} custom-call(bf16[32,128]{1,0:T(8,128)(2,1)S(1)} %copy-done, bf16[32,3,128,128]{3,2,1,0:T(8,128)(2,1)} %vals_hbm.7), custom_call_target="tpu_custom_call" | custom-call | flops 33554432 | bytes 1048576 | tf_op jit(solution)/shard_map/pallas_call | solution.py:186
  31.0 0.6 collective-permute-done.2.high_ref
  31.7 0.0 copy-done.1
  31.7 3.1 %shard_map.88.near_ref = f32[32,128]{1,0:T(8,128)S(1)} custom-call(s32[1]{0:T(128)} %bitcast.4.pos_ref, s32[3,32]{1,0:T(4,128)S(1)} %bitcast.9, bf16[128,128]{1,0:T(8,128)(2,1)S(1)} %constant_dynamic-update-slice_fusion.low_ref, bf16[128,128]{1,0:T(8,128)(2,1)S(1)} %collective-permute-done.2.high_ref, bf16[32,3,128,128]{3,2,1,0:T(8,128)(2,1)} %vals_hbm.7, ...), custom_call_target="tpu_custom_call" | custom-call | flops 67108864 | bytes 2097152 | tf_op jit(solution)/shard_map/pallas_call | solution.py:186
  34.8 1.0 %all-to-all-done = bf16[32,16,128]{2,1,0:T(8,128)(2,1)S(1)} async-done(((bf16[32,16,128]{2,1,0:T(8,128)(2,1)}), bf16[32,16,128]{2,1,0:T(8,128)(2,1)S(1)}, u32[]{:S(2)}, u32[]{:S(2)}) %all-to-all-start) | async-done | bytes 131104 | tf_op jit(solution)/shard_map/all_to_all | solution.py:218
  35.9 0.0 copy-done.2
  35.9 1.6 %shard_map.89 = (f32[32,128]{1,0:T(8,128)}, bf16[32,128]{1,0:T(8,128)(2,1)S(1)}) custom-call(s32[2,32]{1,0:T(2,128)S(1)} %bitcast.11, bf16[512,128]{1,0:T(8,128)(2,1)S(1)} %bitcast.7, bf16[32,2,64,64]{3,2,1,0:T(8,128)(2,1)S(1)} %get-tuple-element.14.coupling_ref, bf16[2048,128]{1,0:T(8,128)(2,1)S(1)} %get-tuple-element.15.target_ref, ...), custom_call_target="tpu_custom_call" | custom-call | flops 50331648 | bytes 1048576 | tf_op jit(solution)/shard_map/pallas_call | solution.py:186
  37.5 3.8 %collective-permute-start.3 = (bf16[32,128]{1,0:T(8,128)(2,1)S(1)}, bf16[32,128]{1,0:T(8,128)(2,1)S(1)}, u32[]{:S(2)}, u32[]{:S(2)}) collective-permute-start(bf16[32,128]{1,0:T(8,128)(2,1)S(1)} %get-tuple-element.18.field_ref), channel_id=1, source_target_pairs={{480,0},{0,32},{32,64},{64,96},{96,128},{128,160},{160,192},{192,2... | collective-permute-start | bytes 24584 | tf_op jit(solution)/shard_map/ppermute | solution.py:199
  41.3 1.1 %shard_map.90 = bf16[32,16,128]{2,1,0:T(8,128)(2,1)} custom-call(bf16[32,128]{1,0:T(8,128)(2,1)S(1)} %get-tuple-element.18.field_ref, bf16[2048,128]{1,0:T(8,128)(2,1)S(1)} %get-tuple-element.19.source_ref), custom_call_target="tpu_custom_call" | custom-call | flops 16777216 | bytes 1048576 | tf_op jit(solution)/shard_map/pallas_call | solution.py:186
  42.4 0.4 collective-permute-done.3
  42.8 5.7 %collective-permute-start.4 = (bf16[64,128]{1,0:T(8,128)(2,1)S(1)}, bf16[64,128]{1,0:T(8,128)(2,1)S(1)}, u32[]{:S(2)}, u32[]{:S(2)}) collective-permute-start(bf16[64,128]{1,0:T(8,128)(2,1)S(1)} %pad_maximum_fusion.1), channel_id=1, source_target_pairs={{448,0},{480,32},{0,64},{32,96},{64,128},{96,160},{128,192},{160,2... | collective-permute-start | bytes 49160 | tf_op jit(solution)/shard_map/ppermute | solution.py:199
  48.6 12.1 %all-to-all-start.1 = ((bf16[32,16,128]{2,1,0:T(8,128)(2,1)}), bf16[32,16,128]{2,1,0:T(8,128)(2,1)S(1)}, u32[]{:S(2)}, u32[]{:S(2)}) async-start(bf16[32,16,128]{2,1,0:T(8,128)(2,1)} %shard_map.90), calls=%async_computation.1 | async-start | bytes 262144 | tf_op jit(solution)/shard_map/all_to_all | solution.py:218
  60.6 0.0 collective-permute-done.4
  60.7 1.9 %collective-permute-start.5 = (bf16[128,128]{1,0:T(8,128)(2,1)S(1)}, bf16[128,128]{1,0:T(8,128)(2,1)S(1)}, u32[]{:S(2)}, u32[]{:S(2)}) collective-permute-start(bf16[128,128]{1,0:T(8,128)(2,1)S(1)} %constant_dynamic-update-slice_fusion.3.low_ref), channel_id=1, source_target_pairs={{96,0},{128,32},{160,64},{192,96},{224,128},{256,160},{288,192},{3... | collective-permute-start | bytes 98312 | tf_op jit(solution)/shard_map/ppermute | solution.py:199
  62.6 2.6 %shard_map.91.own_ref = f32[32,128]{1,0:T(8,128)S(1)} custom-call(bf16[32,128]{1,0:T(8,128)(2,1)S(1)} %get-tuple-element.18.field_ref, bf16[32,3,128,128]{3,2,1,0:T(8,128)(2,1)} %vals_hbm.7), custom_call_target="tpu_custom_call" | custom-call | flops 33554432 | bytes 1048576 | tf_op jit(solution)/shard_map/pallas_call | solution.py:186
  65.2 1.4 %collective-permute-done.5.high_ref = bf16[128,128]{1,0:T(8,128)(2,1)S(1)} collective-permute-done((bf16[128,128]{1,0:T(8,128)(2,1)S(1)}, bf16[128,128]{1,0:T(8,128)(2,1)S(1)}, u32[]{:S(2)}, u32[]{:S(2)}) %collective-permute-start.5) | collective-permute-done | bytes 32800 | tf_op jit(solution)/shard_map/ppermute | solution.py:199
  66.5 3.1 %shard_map.92.near_ref = f32[32,128]{1,0:T(8,128)S(1)} custom-call(s32[1]{0:T(128)} %bitcast.4.pos_ref, s32[3,32]{1,0:T(4,128)S(1)} %bitcast.10, bf16[128,128]{1,0:T(8,128)(2,1)S(1)} %constant_dynamic-update-slice_fusion.3.low_ref, bf16[128,128]{1,0:T(8,128)(2,1)S(1)} %collective-permute-done.5.high_ref, bf16[32,3,128,128]{3,2,1,0:T(8,128)(2,1)} %vals_hbm.7, ...), custom_call_target="tpu_custom_call" | custom-call | flops 67108864 | bytes 2097152 | tf_op jit(solution)/shard_map/pallas_call | solution.py:186
  69.7 1.7 %all-to-all-done.1 = bf16[32,16,128]{2,1,0:T(8,128)(2,1)S(1)} async-done(((bf16[32,16,128]{2,1,0:T(8,128)(2,1)}), bf16[32,16,128]{2,1,0:T(8,128)(2,1)S(1)}, u32[]{:S(2)}, u32[]{:S(2)}) %all-to-all-start.1) | async-done | bytes 131104 | tf_op jit(solution)/shard_map/all_to_all | solution.py:218
  71.4 1.6 %shard_map.93 = f32[32,128]{1,0:T(8,128)} custom-call(s32[2,32]{1,0:T(2,128)S(1)} %bitcast.12, bf16[512,128]{1,0:T(8,128)(2,1)S(1)} %bitcast.8, bf16[32,2,64,64]{3,2,1,0:T(8,128)(2,1)S(1)} %get-tuple-element.14.coupling_ref, bf16[2048,128]{1,0:T(8,128)(2,1)S(1)} %get-tuple-element.15.target_ref, f32[32,128]{1,0:T(8,128)S(1)} %shard_map.92.near_ref), custom_call_target="tpu_custom_call" | custom-call | flops 50331648 | bytes 1048576 | tf_op jit(solution)/shard_map/pallas_call | solution.py:186
  (6 shorter events, 0.0 us)
Async XLA Ops:
  0.6 31.1 %copy-start.1 = (s32[32,3]{0,1:T(4,128)S(1)}, s32[32,3]{0,1:T(4,128)}, u32[]{:S(2)}) copy-start(s32[32,3]{0,1:T(4,128)} %param.9) | copy-start | bytes 1156
  0.6 5.5 %collective-permute-start = (bf16[32,128]{1,0:T(8,128)(2,1)}, bf16[32,128]{1,0:T(8,128)(2,1)S(1)}, u32[]{:S(2)}, u32[]{:S(2)}) collective-permute-start(bf16[32,128]{1,0:T(8,128)(2,1)} %field_ref.1), channel_id=1, source_target_pairs={{480,0},{0,32},{32,64},{64,96},{96,128},{128,160},{160,192},{192,2... | collective-permute-start | bytes 24584 | tf_op jit(solution)/shard_map/ppermute | solution.py:199
  6.8 18.3 %collective-permute-start.1 = (bf16[64,128]{1,0:T(8,128)(2,1)S(1)}, bf16[64,128]{1,0:T(8,128)(2,1)S(1)}, u32[]{:S(2)}, u32[]{:S(2)}) collective-permute-start(bf16[64,128]{1,0:T(8,128)(2,1)S(1)} %pad_maximum_fusion), channel_id=1, source_target_pairs={{448,0},{480,32},{0,64},{32,96},{64,128},{96,160},{128,192},{160,2... | collective-permute-start | bytes 49160 | tf_op jit(solution)/shard_map/ppermute | solution.py:199
  10.0 25.8 %all-to-all-start = ((bf16[32,16,128]{2,1,0:T(8,128)(2,1)}), bf16[32,16,128]{2,1,0:T(8,128)(2,1)S(1)}, u32[]{:S(2)}, u32[]{:S(2)}) async-start(bf16[32,16,128]{2,1,0:T(8,128)(2,1)} %get-tuple-element.13), calls=%async_computation | async-start | bytes 262144 | tf_op jit(solution)/shard_map/all_to_all | solution.py:218
  25.8 5.8 %collective-permute-start.2 = (bf16[128,128]{1,0:T(8,128)(2,1)S(1)}, bf16[128,128]{1,0:T(8,128)(2,1)S(1)}, u32[]{:S(2)}, u32[]{:S(2)}) collective-permute-start(bf16[128,128]{1,0:T(8,128)(2,1)S(1)} %constant_dynamic-update-slice_fusion.low_ref), channel_id=1, source_target_pairs={{96,0},{128,32},{160,64},{192,96},{224,128},{256,160},{288,192},{3... | collective-permute-start | bytes 98312 | tf_op jit(solution)/shard_map/ppermute | solution.py:199
  27.8 0.7 copy-start
  28.5 7.4 %copy-start.2 = (s32[32,2]{0,1:T(2,128)S(1)}, s32[32,2]{0,1:T(2,128)}, u32[]{:S(2)}) copy-start(s32[32,2]{0,1:T(2,128)} %param.13) | copy-start | bytes 772
  37.5 5.4 %collective-permute-start.3 = (bf16[32,128]{1,0:T(8,128)(2,1)S(1)}, bf16[32,128]{1,0:T(8,128)(2,1)S(1)}, u32[]{:S(2)}, u32[]{:S(2)}) collective-permute-start(bf16[32,128]{1,0:T(8,128)(2,1)S(1)} %get-tuple-element.18.field_ref), channel_id=1, source_target_pairs={{480,0},{0,32},{32,64},{64,96},{96,128},{128,160},{160,192},{192,2... | collective-permute-start | bytes 24584 | tf_op jit(solution)/shard_map/ppermute | solution.py:199
  42.8 17.8 %collective-permute-start.4 = (bf16[64,128]{1,0:T(8,128)(2,1)S(1)}, bf16[64,128]{1,0:T(8,128)(2,1)S(1)}, u32[]{:S(2)}, u32[]{:S(2)}) collective-permute-start(bf16[64,128]{1,0:T(8,128)(2,1)S(1)} %pad_maximum_fusion.1), channel_id=1, source_target_pairs={{448,0},{480,32},{0,64},{32,96},{64,128},{96,160},{128,192},{160,2... | collective-permute-start | bytes 49160 | tf_op jit(solution)/shard_map/ppermute | solution.py:199
  48.6 22.8 %all-to-all-start.1 = ((bf16[32,16,128]{2,1,0:T(8,128)(2,1)}), bf16[32,16,128]{2,1,0:T(8,128)(2,1)S(1)}, u32[]{:S(2)}, u32[]{:S(2)}) async-start(bf16[32,16,128]{2,1,0:T(8,128)(2,1)} %shard_map.90), calls=%async_computation.1 | async-start | bytes 262144 | tf_op jit(solution)/shard_map/all_to_all | solution.py:218
  60.7 5.9 %collective-permute-start.5 = (bf16[128,128]{1,0:T(8,128)(2,1)S(1)}, bf16[128,128]{1,0:T(8,128)(2,1)S(1)}, u32[]{:S(2)}, u32[]{:S(2)}) collective-permute-start(bf16[128,128]{1,0:T(8,128)(2,1)S(1)} %constant_dynamic-update-slice_fusion.3.low_ref), channel_id=1, source_target_pairs={{96,0},{128,32},{160,64},{192,96},{224,128},{256,160},{288,192},{3... | collective-permute-start | bytes 98312 | tf_op jit(solution)/shard_map/ppermute | solution.py:199

commit v4 on v3

--- a/solution.py
+++ b/solution.py
@@ -64,6 +64,10 @@
     half = blocks // 2
     packed = moments[:half] + pltpu.roll(moments[half:blocks], rank, 1)
     copies_ref[...] = jnp.broadcast_to(packed.astype(BF16)[None], copies_ref.shape)
+
+
+def spread_kernel(field_ref, copies_ref):
+    copies_ref[...] = jnp.broadcast_to(field_ref[...][None], copies_ref.shape)
 
 
 def first_kernel(charge_hbm, source_hbm, target_hbm, coupling_hbm, copies_ref, source_ref, target_ref, coupling_ref,
@@ -105,22 +109,16 @@
     near_ref[...] = own_columns(blocks, panels, product).T[:blocks]
 
 
-def near_kernel(cycle_size, owners, pos_ref, cols_ref, low_ref, high_ref, vals_hbm, own_ref, near_ref, vals_ref, sems):
+def near_kernel(owners, cols_ref, window_ref, vals_hbm, own_ref, near_ref, vals_ref, sems):
     blocks, panels = own_ref.shape
     moves = fetch(vals_hbm.at[:, pl.ds(1, vals_ref.shape[1])], vals_ref, sems)
     kinds = cols_ref.shape[0]
     cols = cols_ref[...]
-    target = lax.div(cols, jnp.int32(blocks * owners))
-    offset = lax.rem(target - pos_ref[0] + (cycle_size + 3), jnp.int32(cycle_size))
-    row = offset * blocks + lax.rem(cols, jnp.int32(blocks))
-    span = low_ref.shape[0]
+    row = lax.div(cols, jnp.int32(blocks * owners)) * blocks + lax.rem(cols, jnp.int32(blocks))
     fields = []
     for k in range(1, kinds):
-        index = column(row[k:k + 1])
-        field = mul(pick(index, span), low_ref[...], NN)
-        beyond = jnp.where(index >= span, index - (span - blocks), -1)
-        field = field + mul(pick(beyond, span), high_ref[...], NN)
-        fields.append(field.astype(BF16))
+        chosen = pick(column(row[k:k + 1]), window_ref.shape[0])
+        fields.append(mul(chosen, window_ref[...], NN).astype(BF16))
     wide = padded(jnp.concatenate(fields, axis=1))
 
     def product(base):
@@ -167,10 +165,13 @@
     return total
 
 
-def middle_kernel(owners, cols_ref, moments_ref, coupling_ref, target_ref, near_ref, potential_ref, second_ref):
+def middle_kernel(owners, cols_ref, moments_ref, coupling_ref, target_ref, near_ref,
+                  potential_ref, second_ref, copies_ref):
     total = potential(owners, cols_ref, moments_ref, coupling_ref, target_ref, near_ref)
     potential_ref[...] = total
-    second_ref[...] = total.astype(BF16)
+    second = total.astype(BF16)
+    second_ref[...] = second
+    copies_ref[...] = jnp.broadcast_to(second[None], copies_ref.shape)
 
 
 def last_kernel(owners, cols_ref, moments_ref, coupling_ref, target_ref, near_ref, potential_ref):
@@ -194,22 +195,17 @@
     )(*operands)
 
 
-def from_behind(block, axis, distance):
-    size = lax.axis_size(axis)
-    return lax.ppermute(block, axis, [((i - distance) % size, i) for i in range(size)])
-
-
 def shards(charges, near_vals, near_cols, source_basis, target_basis, coupling, far_cols):
     owners = lax.axis_size("cluster")
     cycle_size = lax.axis_size("blk")
     blocks, panels = charges.shape
     rank = source_basis.shape[1]
-    pos = lax.axis_index("blk").reshape(1)
     near_cols = near_cols.T
     far_cols = far_cols.T
     shape = jax.ShapeDtypeStruct
     basis = shape((blocks * rank, panels), BF16)
     copies = shape((owners, blocks // 2, 2 * rank), BF16)
+    spread = shape((cycle_size, blocks, panels), BF16)
     field32 = shape((blocks, panels), F32)
     field16 = shape((blocks, panels), BF16)
     tile = 2 * blocks * panels * panels
@@ -217,14 +213,15 @@
     def far_exchange(copies):
         return lax.all_to_all(copies, "cluster", 0, 0, tiled=True).reshape(-1, 2 * rank)
 
-    def near_part(charge, behind):
-        own = call(own_kernel, field32, charge, near_vals, specs=[VMEM, HBM], scratch=stage(1), flops=32 * tile, moved=tile)
-        pair = jnp.concatenate([behind, charge], axis=0)
-        low = jnp.concatenate([from_behind(pair, "blk", 2), pair], axis=0)
-        high = from_behind(low, "blk", -3)
-        kernel = functools.partial(near_kernel, cycle_size, owners)
-        return call(kernel, field32, pos, near_cols, low, high, near_vals, own,
-                    specs=[SMEM] + [VMEM] * 3 + [HBM, VMEM], scratch=stage(near_vals.shape[1] - 1), flops=64 * tile, moved=2 * tile)
+    def near_exchange(copies):
+        return lax.all_to_all(copies, "blk", 0, 0, tiled=True).reshape(-1, panels)
+
+    def own_part(charge):
+        return call(own_kernel, field32, charge, near_vals, specs=[VMEM, HBM], scratch=stage(1), flops=32 * tile, moved=tile)
+
+    def near_part(window, own):
+        return call(functools.partial(near_kernel, owners), field32, near_cols, window, near_vals, own,
+                    specs=[VMEM] * 2 + [HBM, VMEM], scratch=stage(near_vals.shape[1] - 1), flops=64 * tile, moved=2 * tile)
 
     def stage(kinds):
         return [pltpu.VMEM((blocks, kinds, panels, panels), BF16), pltpu.SemaphoreType.DMA((blocks // CHUNK,))]
@@ -240,15 +237,20 @@
         specs=[HBM] * 4, scratch=[pltpu.VMEM(charges.shape, BF16), pltpu.SemaphoreType.DMA((4,))],
         flops=16 * tile, moved=2 * tile)
     source, target, coupling = pinned(pltpu.VMEM, source, target, coupling)
-    behind, sent = lax.optimization_barrier((from_behind(charges, "blk", 1), sent))
-    near = near_part(charges, behind)
+    window = near_exchange(call(spread_kernel, spread, charges, moved=tile))
+    own = own_part(charges)
+    window, sent, own = lax.optimization_barrier((window, sent, own))
     moments = far_exchange(sent)
-    potential_one, second = call(functools.partial(middle_kernel, owners), (field32, field16),
-                                 far_cols, moments, coupling, target, near, flops=48 * tile, moved=tile)
+    near = near_part(window, own)
+    potential_one, second, spread_second = call(
+        functools.partial(middle_kernel, owners), (field32, field16, spread),
+        far_cols, moments, coupling, target, near, flops=48 * tile, moved=tile)
+    window = near_exchange(spread_second)
     sent = call(moments_kernel, copies, second, source, flops=16 * tile, moved=tile)
-    behind, sent = lax.optimization_barrier((from_behind(second, "blk", 1), sent))
-    near = near_part(second, behind)
+    own = own_part(second)
+    window, sent, own = lax.optimization_barrier((window, sent, own))
     moments = far_exchange(sent)
+    near = near_part(window, own)
     potential_two = call(functools.partial(last_kernel, owners), field32,
                          far_cols, moments, coupling, target, near, flops=48 * tile, moved=tile)
     return (potential_one, potential_two)

time: 73.6 us -> 77.1 us (1.048)
  the two profiles are of different devices: /device:TPU:17 before, /device:TPU:1 now
where the time goes in v4:
time: 77.1 us; the launch traced here: 76.5 us
  starting transfers between devices  32.2 us (42%)
  waiting for transfers between devices  23.7 us (31%)
  Pallas kernels  18.5 us (24%)
  local copies, waits for them, and re-layouts  1.39 us (2%)
    all_to_all x2, starting transfers between devices, far_exchange(): lax.all_to_all(copies, 'cluster', 0, 0, tiled=True).reshape(-1, 2 * rank)  20 us
    pallas_call x9, Pallas kernels, call(): pl.pallas_call(kernel, out_shape=outs, in_specs=specs or [VMEM] * len(ope...  18.5 us
    all_to_all x2, waiting for transfers between devices, far_exchange(): lax.all_to_all(copies, 'cluster', 0, 0, tiled=True).reshape(-1, 2 * rank)  15.4 us
    all_to_all x2, starting transfers between devices, near_exchange(): return lax.all_to_all(copies, 'blk', 0, 0, tiled=True).reshape(-1, panels)  12.2 us
    all_to_all x2, waiting for transfers between devices, near_exchange(): return lax.all_to_all(copies, 'blk', 0, 0, tiled=True).reshape(-1, panels)  8.23 us
  transfers between devices with their start and end apart: 4, of which 4 were waited for; matrix products, arithmetic and copies ran while one was open for 0% of the time, Pallas kernels for 19%

profile of v4, /device:TPU:1, one launch (start us, length us, event | category | flops | bytes accessed | tf_op | source)
XLA Modules:
  0.0 76.5 jit_solution(7270184924428702910)
XLA Ops:
  0.6 0.0 copy-start
  0.6 0.7 copy-done
  1.3 0.0 copy-start.2
  1.3 0.7 shard_map.86
  2.0 8.7 %all-to-all-start = ((bf16[16,32,128]{2,1,0:T(8,128)(2,1)}), bf16[16,32,128]{2,1,0:T(8,128)(2,1)S(1)}, u32[]{:S(2)}, u32[]{:S(2)}) async-start(bf16[16,32,128]{2,1,0:T(8,128)(2,1)} %shard_map.86), calls=%async_computation | async-start | bytes 262144 | tf_op jit(solution)/shard_map/all_to_all | solution.py:217
  10.7 2.2 %shard_map.87 = (bf16[32,16,128]{2,1,0:T(8,128)(2,1)}, bf16[2048,128]{1,0:T(8,128)(2,1)S(1)}, bf16[2048,128]{1,0:T(8,128)(2,1)S(1)}, bf16[32,2,64,64]{3,2,1,0:T(8,128)(2,1)S(1)}) custom-call(bf16[32,128]{1,0:T(8,128)(2,1)} %field_ref.3, bf16[2048,128]{1,0:T(8,128)(2,1)} %bitcast.16, bf16[2048,128]{1,0:T(8,128)(2,1)} %bitcast.17, ...), custom_call_target="tpu_custom_call" | custom-call | flops 16777216 | bytes 2097152 | tf_op jit(solution)/shard_map/pallas_call | solution.py:187
  12.9 0.0 copy-start.1
  12.9 0.7 copy-done.1
  13.6 0.0 copy-start.3
  13.6 2.6 %shard_map.88.own_ref = f32[32,128]{1,0:T(8,128)S(1)} custom-call(bf16[32,128]{1,0:T(8,128)(2,1)S(1)} %copy-done.1, bf16[32,3,128,128]{3,2,1,0:T(8,128)(2,1)} %vals_hbm.7), custom_call_target="tpu_custom_call" | custom-call | flops 33554432 | bytes 1048576 | tf_op jit(solution)/shard_map/pallas_call | solution.py:187
  16.2 3.0 %all-to-all-done = bf16[16,32,128]{2,1,0:T(8,128)(2,1)S(1)} async-done(((bf16[16,32,128]{2,1,0:T(8,128)(2,1)}), bf16[16,32,128]{2,1,0:T(8,128)(2,1)S(1)}, u32[]{:S(2)}, u32[]{:S(2)}) %all-to-all-start) | async-done | bytes 131104 | tf_op jit(solution)/shard_map/all_to_all | solution.py:217
  19.2 14.7 %all-to-all-start.1 = ((bf16[32,16,128]{2,1,0:T(8,128)(2,1)}), bf16[32,16,128]{2,1,0:T(8,128)(2,1)S(1)}, u32[]{:S(2)}, u32[]{:S(2)}) async-start(bf16[32,16,128]{2,1,0:T(8,128)(2,1)} %get-tuple-element.16), calls=%async_computation.1 | async-start | bytes 262144 | tf_op jit(solution)/shard_map/all_to_all | solution.py:214
  33.9 0.0 copy-done.2
  33.9 3.1 %shard_map.89.near_ref = f32[32,128]{1,0:T(8,128)S(1)} custom-call(s32[3,32]{1,0:T(4,128)S(1)} %bitcast.12, bf16[512,128]{1,0:T(8,128)(2,1)S(1)} %bitcast.8, bf16[32,3,128,128]{3,2,1,0:T(8,128)(2,1)} %vals_hbm.7, f32[32,128]{1,0:T(8,128)S(1)} %shard_map.88.own_ref), custom_call_target="tpu_custom_call" | custom-call | flops 67108864 | bytes 2097152 | tf_op jit(solution)/shard_map/pallas_call | solution.py:187
  37.0 7.6 %all-to-all-done.1 = bf16[32,16,128]{2,1,0:T(8,128)(2,1)S(1)} async-done(((bf16[32,16,128]{2,1,0:T(8,128)(2,1)}), bf16[32,16,128]{2,1,0:T(8,128)(2,1)S(1)}, u32[]{:S(2)}, u32[]{:S(2)}) %all-to-all-start.1) | async-done | bytes 131104 | tf_op jit(solution)/shard_map/all_to_all | solution.py:214
  44.7 0.0 copy-done.3
  44.7 1.6 %shard_map.90 = (f32[32,128]{1,0:T(8,128)}, bf16[32,128]{1,0:T(8,128)(2,1)S(1)}, bf16[16,32,128]{2,1,0:T(8,128)(2,1)}) custom-call(s32[2,32]{1,0:T(2,128)S(1)} %bitcast.14, bf16[512,128]{1,0:T(8,128)(2,1)S(1)} %bitcast.10, bf16[32,2,64,64]{3,2,1,0:T(8,128)(2,1)S(1)} %get-tuple-element.17.coupling_ref, bf16[2048,128]{1,0:T(8,128)(2,1)S(1)} %get-tuple-element.18.target_ref, ...), custom_call_target="tpu_custom_call" | custom-call | flops 50331648 | bytes 1048576 | tf_op jit(solution)/shard_map/pallas_call | solution.py:187
  46.3 3.5 %all-to-all-start.2 = ((bf16[16,32,128]{2,1,0:T(8,128)(2,1)}), bf16[16,32,128]{2,1,0:T(8,128)(2,1)S(1)}, u32[]{:S(2)}, u32[]{:S(2)}) async-start(bf16[16,32,128]{2,1,0:T(8,128)(2,1)} %get-tuple-element.22), calls=%async_computation.2 | async-start | bytes 262144 | tf_op jit(solution)/shard_map/all_to_all | solution.py:217
  49.8 1.1 %shard_map.91 = bf16[32,16,128]{2,1,0:T(8,128)(2,1)} custom-call(bf16[32,128]{1,0:T(8,128)(2,1)S(1)} %get-tuple-element.23.field_ref, bf16[2048,128]{1,0:T(8,128)(2,1)S(1)} %get-tuple-element.24.source_ref), custom_call_target="tpu_custom_call" | custom-call | flops 16777216 | bytes 1048576 | tf_op jit(solution)/shard_map/pallas_call | solution.py:187
  50.9 2.6 %shard_map.92.own_ref = f32[32,128]{1,0:T(8,128)S(1)} custom-call(bf16[32,128]{1,0:T(8,128)(2,1)S(1)} %get-tuple-element.23.field_ref, bf16[32,3,128,128]{3,2,1,0:T(8,128)(2,1)} %vals_hbm.7), custom_call_target="tpu_custom_call" | custom-call | flops 33554432 | bytes 1048576 | tf_op jit(solution)/shard_map/pallas_call | solution.py:187
  53.4 5.2 %all-to-all-done.2 = bf16[16,32,128]{2,1,0:T(8,128)(2,1)S(1)} async-done(((bf16[16,32,128]{2,1,0:T(8,128)(2,1)}), bf16[16,32,128]{2,1,0:T(8,128)(2,1)S(1)}, u32[]{:S(2)}, u32[]{:S(2)}) %all-to-all-start.2) | async-done | bytes 131104 | tf_op jit(solution)/shard_map/all_to_all | solution.py:217
  58.7 5.3 %all-to-all-start.3 = ((bf16[32,16,128]{2,1,0:T(8,128)(2,1)}), bf16[32,16,128]{2,1,0:T(8,128)(2,1)S(1)}, u32[]{:S(2)}, u32[]{:S(2)}) async-start(bf16[32,16,128]{2,1,0:T(8,128)(2,1)} %shard_map.91), calls=%async_computation.3 | async-start | bytes 262144 | tf_op jit(solution)/shard_map/all_to_all | solution.py:214
  64.0 3.1 %shard_map.93.near_ref = f32[32,128]{1,0:T(8,128)S(1)} custom-call(s32[3,32]{1,0:T(4,128)S(1)} %bitcast.13, bf16[512,128]{1,0:T(8,128)(2,1)S(1)} %bitcast.9, bf16[32,3,128,128]{3,2,1,0:T(8,128)(2,1)} %vals_hbm.7, f32[32,128]{1,0:T(8,128)S(1)} %shard_map.92.own_ref), custom_call_target="tpu_custom_call" | custom-call | flops 67108864 | bytes 2097152 | tf_op jit(solution)/shard_map/pallas_call | solution.py:187
  67.1 7.8 %all-to-all-done.3 = bf16[32,16,128]{2,1,0:T(8,128)(2,1)S(1)} async-done(((bf16[32,16,128]{2,1,0:T(8,128)(2,1)}), bf16[32,16,128]{2,1,0:T(8,128)(2,1)S(1)}, u32[]{:S(2)}, u32[]{:S(2)}) %all-to-all-start.3) | async-done | bytes 131104 | tf_op jit(solution)/shard_map/all_to_all | solution.py:214
  75.0 1.6 %shard_map.94 = f32[32,128]{1,0:T(8,128)} custom-call(s32[2,32]{1,0:T(2,128)S(1)} %bitcast.15, bf16[512,128]{1,0:T(8,128)(2,1)S(1)} %bitcast.11, bf16[32,2,64,64]{3,2,1,0:T(8,128)(2,1)S(1)} %get-tuple-element.17.coupling_ref, bf16[2048,128]{1,0:T(8,128)(2,1)S(1)} %get-tuple-element.18.target_ref, f32[32,128]{1,0:T(8,128)S(1)} %shard_map.93.near_ref), custom_call_target="tpu_custom_call" | custom-call | flops 50331648 | bytes 1048576 | tf_op jit(solution)/shard_map/pallas_call | solution.py:187
Async XLA Ops:
  0.6 0.7 copy-start
  1.3 32.6 %copy-start.2 = (s32[32,3]{0,1:T(4,128)S(1)}, s32[32,3]{0,1:T(4,128)}, u32[]{:S(2)}) copy-start(s32[32,3]{0,1:T(4,128)} %param.9) | copy-start | bytes 1156
  2.0 17.2 %all-to-all-start = ((bf16[16,32,128]{2,1,0:T(8,128)(2,1)}), bf16[16,32,128]{2,1,0:T(8,128)(2,1)S(1)}, u32[]{:S(2)}, u32[]{:S(2)}) async-start(bf16[16,32,128]{2,1,0:T(8,128)(2,1)} %shard_map.86), calls=%async_computation | async-start | bytes 262144 | tf_op jit(solution)/shard_map/all_to_all | solution.py:217
  12.9 0.7 copy-start.1
  13.6 31.1 %copy-start.3 = (s32[32,2]{0,1:T(2,128)S(1)}, s32[32,2]{0,1:T(2,128)}, u32[]{:S(2)}) copy-start(s32[32,2]{0,1:T(2,128)} %param.13) | copy-start | bytes 772
  19.2 25.5 %all-to-all-start.1 = ((bf16[32,16,128]{2,1,0:T(8,128)(2,1)}), bf16[32,16,128]{2,1,0:T(8,128)(2,1)S(1)}, u32[]{:S(2)}, u32[]{:S(2)}) async-start(bf16[32,16,128]{2,1,0:T(8,128)(2,1)} %get-tuple-element.16), calls=%async_computation.1 | async-start | bytes 262144 | tf_op jit(solution)/shard_map/all_to_all | solution.py:214
  46.3 12.4 %all-to-all-start.2 = ((bf16[16,32,128]{2,1,0:T(8,128)(2,1)}), bf16[16,32,128]{2,1,0:T(8,128)(2,1)S(1)}, u32[]{:S(2)}, u32[]{:S(2)}) async-start(bf16[16,32,128]{2,1,0:T(8,128)(2,1)} %get-tuple-element.22), calls=%async_computation.2 | async-start | bytes 262144 | tf_op jit(solution)/shard_map/all_to_all | solution.py:217
  58.7 16.3 %all-to-all-start.3 = ((bf16[32,16,128]{2,1,0:T(8,128)(2,1)}), bf16[32,16,128]{2,1,0:T(8,128)(2,1)S(1)}, u32[]{:S(2)}, u32[]{:S(2)}) async-start(bf16[32,16,128]{2,1,0:T(8,128)(2,1)} %shard_map.91), calls=%async_computation.3 | async-start | bytes 262144 | tf_op jit(solution)/shard_map/all_to_all | solution.py:214

commit v5 on v3

--- a/solution.py
+++ b/solution.py
@@ -66,8 +66,8 @@
     copies_ref[...] = jnp.broadcast_to(packed.astype(BF16)[None], copies_ref.shape)
 
 
-def first_kernel(charge_hbm, source_hbm, target_hbm, coupling_hbm, copies_ref, source_ref, target_ref, coupling_ref,
-                 charge_ref, sems):
+def first_kernel(charge_hbm, source_hbm, target_hbm, coupling_hbm,
+                 copies_ref, charge_ref, source_ref, target_ref, coupling_ref, sems):
     pairs = [(charge_hbm, charge_ref), (source_hbm, source_ref), (coupling_hbm, coupling_ref), (target_hbm, target_ref)]
     moves = [pltpu.make_async_copy(a, b, sems.at[n]) for n, (a, b) in enumerate(pairs)]
     for move in moves:
@@ -79,10 +79,6 @@
     moves[3].wait()
 
 
-def moments_kernel(field_ref, source_ref, copies_ref):
-    send_moments(field_ref[...], source_ref, copies_ref)
-
-
 def fetch(source, dest, sems):
     moves = []
     for n in range(dest.shape[0] // CHUNK):
@@ -93,22 +89,27 @@
     return moves
 
 
+def near_product(fields, vals_ref):
+    blocks, panels = fields[0].shape
+    wide = padded(jnp.concatenate(fields, axis=1))
+
+    def product(base):
+        vals = [vals_ref[base:base + CHUNK, k].reshape(CHUNK * panels, panels) for k in range(len(fields))]
+        return mul(jnp.concatenate(vals, axis=1), wide, NT)
+
+    return own_columns(blocks, panels, product).T[:blocks]
+
+
 def own_kernel(field_ref, vals_hbm, near_ref, vals_ref, sems):
-    blocks, panels = field_ref.shape
-    moves = fetch(vals_hbm.at[:, pl.ds(0, 1)], vals_ref, sems)
-    wide = padded(field_ref[...])
-
-    def product(base):
-        moves[base // CHUNK].wait()
-        return mul(vals_ref[base:base + CHUNK, 0].reshape(CHUNK * panels, panels), wide, NT)
-
-    near_ref[...] = own_columns(blocks, panels, product).T[:blocks]
-
-
-def near_kernel(cycle_size, owners, pos_ref, cols_ref, low_ref, high_ref, vals_hbm, own_ref, near_ref, vals_ref, sems):
-    blocks, panels = own_ref.shape
-    moves = fetch(vals_hbm.at[:, pl.ds(1, vals_ref.shape[1])], vals_ref, sems)
+    for move in fetch(vals_hbm.at[:, pl.ds(0, 1)], vals_ref, sems):
+        move.wait()
+    near_ref[...] = near_product([field_ref[...]], vals_ref)
+
+
+def near_first_kernel(cycle_size, owners, pos_ref, cols_ref, low_ref, high_ref, vals_hbm, own_ref, near_ref, vals_ref, sems):
+    blocks = own_ref.shape[0]
     kinds = cols_ref.shape[0]
+    moves = fetch(vals_hbm.at[:, pl.ds(1, kinds - 1)], vals_ref, sems)
     cols = cols_ref[...]
     target = lax.div(cols, jnp.int32(blocks * owners))
     offset = lax.rem(target - pos_ref[0] + (cycle_size + 3), jnp.int32(cycle_size))
@@ -121,14 +122,23 @@
         beyond = jnp.where(index >= span, index - (span - blocks), -1)
         field = field + mul(pick(beyond, span), high_ref[...], NN)
         fields.append(field.astype(BF16))
-    wide = padded(jnp.concatenate(fields, axis=1))
-
-    def product(base):
-        moves[base // CHUNK].wait()
-        vals = [vals_ref[base:base + CHUNK, k].reshape(CHUNK * panels, panels) for k in range(kinds - 1)]
-        return mul(jnp.concatenate(vals, axis=1), wide, NT)
-
-    near_ref[...] = own_ref[...] + own_columns(blocks, panels, product).T[:blocks]
+    for move in moves:
+        move.wait()
+    near_ref[...] = own_ref[...] + near_product(fields, vals_ref)
+
+
+def near_kernel(owners, cols_ref, field_ref, window_ref, vals_hbm, near_ref, vals_ref, sems):
+    moves = fetch(vals_hbm, vals_ref, sems)
+    blocks = field_ref.shape[0]
+    cols = cols_ref[...]
+    row = lax.div(cols, jnp.int32(blocks * owners)) * blocks + lax.rem(cols, jnp.int32(blocks))
+    fields = [field_ref[...]]
+    for k in range(1, cols_ref.shape[0]):
+        chosen = pick(column(row[k:k + 1]), window_ref.shape[0])
+        fields.append(mul(chosen, window_ref[...], NN).astype(BF16))
+    for move in moves:
+        move.wait()
+    near_ref[...] = near_product(fields, vals_ref)
 
 
 def potential(owners, cols_ref, moments_ref, coupling_ref, target_ref, near_ref):
@@ -167,10 +177,14 @@
     return total
 
 
-def middle_kernel(owners, cols_ref, moments_ref, coupling_ref, target_ref, near_ref, potential_ref, second_ref):
+def middle_kernel(owners, cols_ref, moments_ref, coupling_ref, target_ref, near_ref, source_ref,
+                  potential_ref, second_ref, spread_ref, copies_ref):
     total = potential(owners, cols_ref, moments_ref, coupling_ref, target_ref, near_ref)
     potential_ref[...] = total
-    second_ref[...] = total.astype(BF16)
+    second = total.astype(BF16)
+    second_ref[...] = second
+    spread_ref[...] = jnp.broadcast_to(second[None], spread_ref.shape)
+    send_moments(second, source_ref, copies_ref)
 
 
 def last_kernel(owners, cols_ref, moments_ref, coupling_ref, target_ref, near_ref, potential_ref):
@@ -210,45 +224,48 @@
     shape = jax.ShapeDtypeStruct
     basis = shape((blocks * rank, panels), BF16)
     copies = shape((owners, blocks // 2, 2 * rank), BF16)
+    spread = shape((cycle_size, blocks, panels), BF16)
     field32 = shape((blocks, panels), F32)
     field16 = shape((blocks, panels), BF16)
     tile = 2 * blocks * panels * panels
 
+    def stage(kinds):
+        return [pltpu.VMEM((blocks, kinds, panels, panels), BF16), pltpu.SemaphoreType.DMA((blocks // CHUNK,))]
+
+    def pinned(place, *arrays):
+        return [pltpu.with_memory_space_constraint(array, place) for array in arrays]
+
     def far_exchange(copies):
         return lax.all_to_all(copies, "cluster", 0, 0, tiled=True).reshape(-1, 2 * rank)
 
-    def near_part(charge, behind):
-        own = call(own_kernel, field32, charge, near_vals, specs=[VMEM, HBM], scratch=stage(1), flops=32 * tile, moved=tile)
-        pair = jnp.concatenate([behind, charge], axis=0)
-        low = jnp.concatenate([from_behind(pair, "blk", 2), pair], axis=0)
-        high = from_behind(low, "blk", -3)
-        kernel = functools.partial(near_kernel, cycle_size, owners)
-        return call(kernel, field32, pos, near_cols, low, high, near_vals, own,
-                    specs=[SMEM] + [VMEM] * 3 + [HBM, VMEM], scratch=stage(near_vals.shape[1] - 1), flops=64 * tile, moved=2 * tile)
-
-    def stage(kinds):
-        return [pltpu.VMEM((blocks, kinds, panels, panels), BF16), pltpu.SemaphoreType.DMA((blocks // CHUNK,))]
-
-    def pinned(place, *arrays):
-        return [pltpu.with_memory_space_constraint(array, place) for array in arrays]
-
+    kept = pltpu.VMEM(basis.shape, BF16)
+    kinds = near_vals.shape[1]
     near_vals, = pinned(pltpu.HBM, near_vals)
-    kept = pltpu.VMEM(basis.shape, BF16)
     operands = (charges, source_basis.reshape(basis.shape), target_basis.reshape(basis.shape), coupling)
-    sent, source, target, coupling = call(
-        first_kernel, (copies, kept, kept, pltpu.VMEM(coupling.shape, BF16)), *pinned(pltpu.HBM, *operands),
-        specs=[HBM] * 4, scratch=[pltpu.VMEM(charges.shape, BF16), pltpu.SemaphoreType.DMA((4,))],
+    sent, charge, source, target, coupling = call(
+        first_kernel, (copies, pltpu.VMEM(charges.shape, BF16), kept, kept, pltpu.VMEM(coupling.shape, BF16)),
+        *pinned(pltpu.HBM, *operands), specs=[HBM] * 4, scratch=[pltpu.SemaphoreType.DMA((4,))],
         flops=16 * tile, moved=2 * tile)
     source, target, coupling = pinned(pltpu.VMEM, source, target, coupling)
+
     behind, sent = lax.optimization_barrier((from_behind(charges, "blk", 1), sent))
-    near = near_part(charges, behind)
+    own = call(own_kernel, field32, charge, near_vals, specs=[VMEM, HBM], scratch=stage(1), flops=32 * tile, moved=tile)
+    pair = jnp.concatenate([behind, charge], axis=0)
+    low = jnp.concatenate([from_behind(pair, "blk", 2), pair], axis=0)
+    high = from_behind(low, "blk", -3)
+    near = call(functools.partial(near_first_kernel, cycle_size, owners), field32,
+                pos, near_cols, low, high, near_vals, own, specs=[SMEM] + [VMEM] * 3 + [HBM, VMEM],
+                scratch=stage(kinds - 1), flops=64 * tile, moved=2 * tile)
     moments = far_exchange(sent)
-    potential_one, second = call(functools.partial(middle_kernel, owners), (field32, field16),
-                                 far_cols, moments, coupling, target, near, flops=48 * tile, moved=tile)
-    sent = call(moments_kernel, copies, second, source, flops=16 * tile, moved=tile)
-    behind, sent = lax.optimization_barrier((from_behind(second, "blk", 1), sent))
-    near = near_part(second, behind)
+    potential_one, second, spread_second, sent = call(
+        functools.partial(middle_kernel, owners), (field32, field16, spread, copies),
+        far_cols, moments, coupling, target, near, source, flops=64 * tile, moved=tile)
+
+    window = lax.all_to_all(spread_second, "blk", 0, 0, tiled=True).reshape(-1, panels)
+    window, sent, second = lax.optimization_barrier((window, sent, second))
     moments = far_exchange(sent)
+    near = call(functools.partial(near_kernel, owners), field32, near_cols, second, window, near_vals,
+                specs=[VMEM] * 3 + [HBM], scratch=stage(kinds), flops=96 * tile, moved=3 * tile)
     potential_two = call(functools.partial(last_kernel, owners), field32,
                          far_cols, moments, coupling, target, near, flops=48 * tile, moved=tile)
     return (potential_one, potential_two)

time: 73.6 us -> 77 us (1.046)
  the two profiles are of different devices: /device:TPU:17 before, /device:TPU:1 now
where the time goes in v5:
time: 77 us; the launch traced here: 76.5 us
  starting transfers between devices  35.1 us (46%)
  blocking collectives  15.6 us (20%)
  Pallas kernels  12.9 us (17%)
  waiting for transfers between devices  12.1 us (16%)
    all_to_all x2, starting transfers between devices, far_exchange(): lax.all_to_all(copies, 'cluster', 0, 0, tiled=True).reshape(-1, 2 * rank)  25.1 us
    all_to_all x1, blocking collectives, shards(): lax.all_to_all(spread_second, 'blk', 0, 0, tiled=True).reshape(-1, panels)  15.6 us
    pallas_call x6, Pallas kernels, call(): pl.pallas_call(kernel, out_shape=outs, in_specs=specs or [VMEM] * len(ope...  12.9 us
    all_to_all x2, waiting for transfers between devices, far_exchange(): lax.all_to_all(copies, 'cluster', 0, 0, tiled=True).reshape(-1, 2 * rank)  10.2 us
    ppermute x3, starting transfers between devices, from_behind(): lax.ppermute(block, axis, [((i - distance) % size, i) for i in range(size)])  9.97 us
    ppermute x3, waiting for transfers between devices, from_behind(): lax.ppermute(block, axis, [((i - distance) % size, i) for i in range(size)])  1.93 us
  transfers between devices with their start and end apart: 5, of which 3 were waited for; matrix products, arithmetic and copies ran while one was open for 0% of the time, Pallas kernels for 12%

profile of v5, /device:TPU:1, one launch (start us, length us, event | category | flops | bytes accessed | tf_op | source)
XLA Modules:
  0.0 76.5 jit_solution(6191344574306989891)
XLA Ops:
  0.6 0.0 copy-start
  0.6 3.9 %collective-permute-start = (bf16[32,128]{1,0:T(8,128)(2,1)}, bf16[32,128]{1,0:T(8,128)(2,1)S(1)}, u32[]{:S(2)}, u32[]{:S(2)}) collective-permute-start(bf16[32,128]{1,0:T(8,128)(2,1)} %charge_hbm.1), channel_id=1, source_target_pairs={{480,0},{0,32},{32,64},{64,96},{96,128},{128,160},{160,192},{192,2... | collective-permute-start | bytes 24584 | tf_op jit(solution)/shard_map/ppermute | solution.py:213
  4.6 2.2 %shard_map.86 = (bf16[32,16,128]{2,1,0:T(8,128)(2,1)}, bf16[32,128]{1,0:T(8,128)(2,1)S(1)}, bf16[2048,128]{1,0:T(8,128)(2,1)S(1)}, bf16[2048,128]{1,0:T(8,128)(2,1)S(1)}, bf16[32,2,64,64]{3,2,1,0:T(8,128)(2,1)S(1)}) custom-call(bf16[32,128]{1,0:T(8,128)(2,1)} %charge_hbm.1, bf16[2048,128]{1,0:T(8,128)(2,1)} %bitcast.15, bf16[2048,128]{1,0:T(8,128)(2,1)} %bitcast.16, ...), custom_call_target="tpu_custom_call" | custom-call | flops 16777216 | bytes 2097152 | tf_op jit(solution)/shard_map/pallas_call | solution.py:200
  6.8 1.9 %collective-permute-done = bf16[32,128]{1,0:T(8,128)(2,1)S(1)} collective-permute-done((bf16[32,128]{1,0:T(8,128)(2,1)}, bf16[32,128]{1,0:T(8,128)(2,1)S(1)}, u32[]{:S(2)}, u32[]{:S(2)}) %collective-permute-start) | collective-permute-done | bytes 8224 | tf_op jit(solution)/shard_map/ppermute | solution.py:213
  8.7 1.9 %collective-permute-start.1 = (bf16[64,128]{1,0:T(8,128)(2,1)S(1)}, bf16[64,128]{1,0:T(8,128)(2,1)S(1)}, u32[]{:S(2)}, u32[]{:S(2)}) collective-permute-start(bf16[64,128]{1,0:T(8,128)(2,1)S(1)} %pad_maximum_fusion), channel_id=1, source_target_pairs={{448,0},{480,32},{0,64},{32,96},{64,128},{96,160},{128,192},{160,2... | collective-permute-start | bytes 49160 | tf_op jit(solution)/shard_map/ppermute | solution.py:213
  10.7 14.6 %all-to-all-start = ((bf16[32,16,128]{2,1,0:T(8,128)(2,1)}), bf16[32,16,128]{2,1,0:T(8,128)(2,1)S(1)}, u32[]{:S(2)}, u32[]{:S(2)}) async-start(bf16[32,16,128]{2,1,0:T(8,128)(2,1)} %get-tuple-element.17), calls=%async_computation | async-start | bytes 262144 | tf_op jit(solution)/shard_map/all_to_all | solution.py:239
  25.2 0.0 collective-permute-done.1
  25.3 4.1 %collective-permute-start.2 = (bf16[128,128]{1,0:T(8,128)(2,1)S(1)}, bf16[128,128]{1,0:T(8,128)(2,1)S(1)}, u32[]{:S(2)}, u32[]{:S(2)}) collective-permute-start(bf16[128,128]{1,0:T(8,128)(2,1)S(1)} %constant_dynamic-update-slice_fusion.low_ref), channel_id=1, source_target_pairs={{96,0},{128,32},{160,64},{192,96},{224,128},{256,160},{288,192},{3... | collective-permute-start | bytes 98312 | tf_op jit(solution)/shard_map/ppermute | solution.py:213
  29.4 0.0 copy-start.1
  29.4 1.8 %shard_map.87.own_ref = f32[32,128]{1,0:T(8,128)S(1)} custom-call(bf16[32,128]{1,0:T(8,128)(2,1)S(1)} %get-tuple-element.21.field_ref, bf16[32,3,128,128]{3,2,1,0:T(8,128)(2,1)} %vals_hbm.5), custom_call_target="tpu_custom_call" | custom-call | flops 33554432 | bytes 1048576 | tf_op jit(solution)/shard_map/pallas_call | solution.py:200
  31.3 0.0 collective-permute-done.2.high_ref
  31.3 0.0 copy-done
  31.3 2.3 %shard_map.88.near_ref = f32[32,128]{1,0:T(8,128)S(1)} custom-call(s32[1]{0:T(128)} %bitcast.4.pos_ref, s32[3,32]{1,0:T(4,128)S(1)} %bitcast.11, bf16[128,128]{1,0:T(8,128)(2,1)S(1)} %constant_dynamic-update-slice_fusion.low_ref, bf16[128,128]{1,0:T(8,128)(2,1)S(1)} %collective-permute-done.2.high_ref, bf16[32,3,128,128]{3,2,1,0:T(8,128)(2,1)} %vals_hbm.5, ...), custom_call_target="tpu_custom_call" | custom-call | flops 67108864 | bytes 2097152 | tf_op jit(solution)/shard_map/pallas_call | solution.py:200
  33.6 2.4 %all-to-all-done = bf16[32,16,128]{2,1,0:T(8,128)(2,1)S(1)} async-done(((bf16[32,16,128]{2,1,0:T(8,128)(2,1)}), bf16[32,16,128]{2,1,0:T(8,128)(2,1)S(1)}, u32[]{:S(2)}, u32[]{:S(2)}) %all-to-all-start) | async-done | bytes 131104 | tf_op jit(solution)/shard_map/all_to_all | solution.py:239
  36.0 0.0 copy-done.1
  36.0 2.0 %shard_map.89 = (f32[32,128]{1,0:T(8,128)}, bf16[32,128]{1,0:T(8,128)(2,1)S(1)}, bf16[16,32,128]{2,1,0:T(8,128)(2,1)S(1)}, bf16[32,16,128]{2,1,0:T(8,128)(2,1)}) custom-call(s32[2,32]{1,0:T(2,128)S(1)} %bitcast.13, bf16[512,128]{1,0:T(8,128)(2,1)S(1)} %bitcast.8, bf16[32,2,64,64]{3,2,1,0:T(8,128)(2,1)S(1)} %get-tuple-element.18.coupling_ref, ...), custom_call_target="tpu_custom_call" | custom-call | flops 67108864 | bytes 1048576 | tf_op jit(solution)/shard_map/pallas_call | solution.py:200
  38.0 15.6 %all_to_all.15 = bf16[16,32,128]{2,1,0:T(8,128)(2,1)S(1)} all-to-all(bf16[16,32,128]{2,1,0:T(8,128)(2,1)S(1)} %get-tuple-element.24), channel_id=1, replica_groups=mesh['blk'=16,'cluster'=32] {'blk'}, dimensions={0} | all-to-all | bytes 262144 | tf_op jit(solution)/shard_map/all_to_all | solution.py:264
  53.6 10.6 %all-to-all-start.2 = ((bf16[32,16,128]{2,1,0:T(8,128)(2,1)}), bf16[32,16,128]{2,1,0:T(8,128)(2,1)S(1)}, u32[]{:S(2)}, u32[]{:S(2)}) async-start(bf16[32,16,128]{2,1,0:T(8,128)(2,1)} %get-tuple-element.27), calls=%async_computation.2 | async-start | bytes 262144 | tf_op jit(solution)/shard_map/all_to_all | solution.py:239
  64.2 2.9 %shard_map.90.near_ref = f32[32,128]{1,0:T(8,128)S(1)} custom-call(s32[3,32]{1,0:T(4,128)S(1)} %bitcast.12, bf16[32,128]{1,0:T(8,128)(2,1)S(1)} %get-tuple-element.28.field_ref, bf16[512,128]{1,0:T(8,128)(2,1)S(1)} %bitcast.10, bf16[32,3,128,128]{3,2,1,0:T(8,128)(2,1)} %vals_hbm.5), custom_call_target="tpu_custom_call" | custom-call | flops 100663296 | bytes 3145728 | tf_op jit(solution)/shard_map/pallas_call | solution.py:200
  67.1 7.8 %all-to-all-done.2 = bf16[32,16,128]{2,1,0:T(8,128)(2,1)S(1)} async-done(((bf16[32,16,128]{2,1,0:T(8,128)(2,1)}), bf16[32,16,128]{2,1,0:T(8,128)(2,1)S(1)}, u32[]{:S(2)}, u32[]{:S(2)}) %all-to-all-start.2) | async-done | bytes 131104 | tf_op jit(solution)/shard_map/all_to_all | solution.py:239
  75.0 1.6 %shard_map.91 = f32[32,128]{1,0:T(8,128)} custom-call(s32[2,32]{1,0:T(2,128)S(1)} %bitcast.14, bf16[512,128]{1,0:T(8,128)(2,1)S(1)} %bitcast.9, bf16[32,2,64,64]{3,2,1,0:T(8,128)(2,1)S(1)} %get-tuple-element.18.coupling_ref, bf16[2048,128]{1,0:T(8,128)(2,1)S(1)} %get-tuple-element.19.target_ref, f32[32,128]{1,0:T(8,128)S(1)} %shard_map.90.near_ref), custom_call_target="tpu_custom_call" | custom-call | flops 50331648 | bytes 1048576 | tf_op jit(solution)/shard_map/pallas_call | solution.py:200
  (4 shorter events, 0.0 us)
Async XLA Ops:
  0.6 30.6 %copy-start = (s32[32,3]{0,1:T(4,128)S(1)}, s32[32,3]{0,1:T(4,128)}, u32[]{:S(2)}) copy-start(s32[32,3]{0,1:T(4,128)} %param.9) | copy-start | bytes 1156
  0.6 8.1 %collective-permute-start = (bf16[32,128]{1,0:T(8,128)(2,1)}, bf16[32,128]{1,0:T(8,128)(2,1)S(1)}, u32[]{:S(2)}, u32[]{:S(2)}) collective-permute-start(bf16[32,128]{1,0:T(8,128)(2,1)} %charge_hbm.1), channel_id=1, source_target_pairs={{480,0},{0,32},{32,64},{64,96},{96,128},{128,160},{160,192},{192,2... | collective-permute-start | bytes 24584 | tf_op jit(solution)/shard_map/ppermute | solution.py:213
  8.7 16.5 %collective-permute-start.1 = (bf16[64,128]{1,0:T(8,128)(2,1)S(1)}, bf16[64,128]{1,0:T(8,128)(2,1)S(1)}, u32[]{:S(2)}, u32[]{:S(2)}) collective-permute-start(bf16[64,128]{1,0:T(8,128)(2,1)S(1)} %pad_maximum_fusion), channel_id=1, source_target_pairs={{448,0},{480,32},{0,64},{32,96},{64,128},{96,160},{128,192},{160,2... | collective-permute-start | bytes 49160 | tf_op jit(solution)/shard_map/ppermute | solution.py:213
  10.7 25.3 %all-to-all-start = ((bf16[32,16,128]{2,1,0:T(8,128)(2,1)}), bf16[32,16,128]{2,1,0:T(8,128)(2,1)S(1)}, u32[]{:S(2)}, u32[]{:S(2)}) async-start(bf16[32,16,128]{2,1,0:T(8,128)(2,1)} %get-tuple-element.17), calls=%async_computation | async-start | bytes 262144 | tf_op jit(solution)/shard_map/all_to_all | solution.py:239
  25.3 6.0 %collective-permute-start.2 = (bf16[128,128]{1,0:T(8,128)(2,1)S(1)}, bf16[128,128]{1,0:T(8,128)(2,1)S(1)}, u32[]{:S(2)}, u32[]{:S(2)}) collective-permute-start(bf16[128,128]{1,0:T(8,128)(2,1)S(1)} %constant_dynamic-update-slice_fusion.low_ref), channel_id=1, source_target_pairs={{96,0},{128,32},{160,64},{192,96},{224,128},{256,160},{288,192},{3... | collective-permute-start | bytes 98312 | tf_op jit(solution)/shard_map/ppermute | solution.py:213
  29.4 6.6 %copy-start.1 = (s32[32,2]{0,1:T(2,128)S(1)}, s32[32,2]{0,1:T(2,128)}, u32[]{:S(2)}) copy-start(s32[32,2]{0,1:T(2,128)} %param.13) | copy-start | bytes 772
  53.6 21.3 %all-to-all-start.2 = ((bf16[32,16,128]{2,1,0:T(8,128)(2,1)}), bf16[32,16,128]{2,1,0:T(8,128)(2,1)S(1)}, u32[]{:S(2)}, u32[]{:S(2)}) async-start(bf16[32,16,128]{2,1,0:T(8,128)(2,1)} %get-tuple-element.27), calls=%async_computation.2 | async-start | bytes 262144 | tf_op jit(solution)/shard_map/all_to_all | solution.py:239

commit v6 on v5

--- a/solution.py
+++ b/solution.py
@@ -66,6 +66,10 @@
     copies_ref[...] = jnp.broadcast_to(packed.astype(BF16)[None], copies_ref.shape)
 
 
+def moments_kernel(field_ref, source_ref, copies_ref):
+    send_moments(field_ref[...], source_ref, copies_ref)
+
+
 def first_kernel(charge_hbm, source_hbm, target_hbm, coupling_hbm,
                  copies_ref, charge_ref, source_ref, target_ref, coupling_ref, sems):
     pairs = [(charge_hbm, charge_ref), (source_hbm, source_ref), (coupling_hbm, coupling_ref), (target_hbm, target_ref)]
@@ -106,7 +110,15 @@
     near_ref[...] = near_product([field_ref[...]], vals_ref)
 
 
-def near_first_kernel(cycle_size, owners, pos_ref, cols_ref, low_ref, high_ref, vals_hbm, own_ref, near_ref, vals_ref, sems):
+def own_store_kernel(field_ref, vals_hbm, kept_ref, near_ref, stored_ref, vals_ref, sems):
+    moves = fetch(vals_hbm.at[:, pl.ds(0, 1)], vals_ref, sems)
+    stored_ref[...] = kept_ref[...]
+    for move in moves:
+        move.wait()
+    near_ref[...] = near_product([field_ref[...]], vals_ref)
+
+
+def near_kernel(cycle_size, owners, pos_ref, cols_ref, low_ref, high_ref, vals_hbm, own_ref, near_ref, vals_ref, sems):
     blocks = own_ref.shape[0]
     kinds = cols_ref.shape[0]
     moves = fetch(vals_hbm.at[:, pl.ds(1, kinds - 1)], vals_ref, sems)
@@ -127,20 +139,6 @@
     near_ref[...] = own_ref[...] + near_product(fields, vals_ref)
 
 
-def near_kernel(owners, cols_ref, field_ref, window_ref, vals_hbm, near_ref, vals_ref, sems):
-    moves = fetch(vals_hbm, vals_ref, sems)
-    blocks = field_ref.shape[0]
-    cols = cols_ref[...]
-    row = lax.div(cols, jnp.int32(blocks * owners)) * blocks + lax.rem(cols, jnp.int32(blocks))
-    fields = [field_ref[...]]
-    for k in range(1, cols_ref.shape[0]):
-        chosen = pick(column(row[k:k + 1]), window_ref.shape[0])
-        fields.append(mul(chosen, window_ref[...], NN).astype(BF16))
-    for move in moves:
-        move.wait()
-    near_ref[...] = near_product(fields, vals_ref)
-
-
 def potential(owners, cols_ref, moments_ref, coupling_ref, target_ref, near_ref):
     blocks, panels = near_ref.shape
     kinds = cols_ref.shape[0]
@@ -177,14 +175,10 @@
     return total
 
 
-def middle_kernel(owners, cols_ref, moments_ref, coupling_ref, target_ref, near_ref, source_ref,
-                  potential_ref, second_ref, spread_ref, copies_ref):
+def middle_kernel(owners, cols_ref, moments_ref, coupling_ref, target_ref, near_ref, potential_ref, second_ref):
     total = potential(owners, cols_ref, moments_ref, coupling_ref, target_ref, near_ref)
     potential_ref[...] = total
-    second = total.astype(BF16)
-    second_ref[...] = second
-    spread_ref[...] = jnp.broadcast_to(second[None], spread_ref.shape)
-    send_moments(second, source_ref, copies_ref)
+    second_ref[...] = total.astype(BF16)
 
 
 def last_kernel(owners, cols_ref, moments_ref, coupling_ref, target_ref, near_ref, potential_ref):
@@ -224,7 +218,6 @@
     shape = jax.ShapeDtypeStruct
     basis = shape((blocks * rank, panels), BF16)
     copies = shape((owners, blocks // 2, 2 * rank), BF16)
-    spread = shape((cycle_size, blocks, panels), BF16)
     field32 = shape((blocks, panels), F32)
     field16 = shape((blocks, panels), BF16)
     tile = 2 * blocks * panels * panels
@@ -248,24 +241,24 @@
         flops=16 * tile, moved=2 * tile)
     source, target, coupling = pinned(pltpu.VMEM, source, target, coupling)
 
-    behind, sent = lax.optimization_barrier((from_behind(charges, "blk", 1), sent))
+    def exchange(sent, field, behind, own):
+        behind, sent = lax.optimization_barrier((behind, sent))
+        pair = jnp.concatenate([behind, field], axis=0)
+        low = jnp.concatenate([from_behind(pair, "blk", 2), pair], axis=0)
+        high = from_behind(low, "blk", -3)
+        near = call(functools.partial(near_kernel, cycle_size, owners), field32,
+                    pos, near_cols, low, high, near_vals, own, specs=[SMEM] + [VMEM] * 3 + [HBM, VMEM],
+                    scratch=stage(kinds - 1), flops=64 * tile, moved=2 * tile)
+        return far_exchange(sent), near
+
     own = call(own_kernel, field32, charge, near_vals, specs=[VMEM, HBM], scratch=stage(1), flops=32 * tile, moved=tile)
-    pair = jnp.concatenate([behind, charge], axis=0)
-    low = jnp.concatenate([from_behind(pair, "blk", 2), pair], axis=0)
-    high = from_behind(low, "blk", -3)
-    near = call(functools.partial(near_first_kernel, cycle_size, owners), field32,
-                pos, near_cols, low, high, near_vals, own, specs=[SMEM] + [VMEM] * 3 + [HBM, VMEM],
-                scratch=stage(kinds - 1), flops=64 * tile, moved=2 * tile)
-    moments = far_exchange(sent)
-    potential_one, second, spread_second, sent = call(
-        functools.partial(middle_kernel, owners), (field32, field16, spread, copies),
-        far_cols, moments, coupling, target, near, source, flops=64 * tile, moved=tile)
-
-    window = lax.all_to_all(spread_second, "blk", 0, 0, tiled=True).reshape(-1, panels)
-    window, sent, second = lax.optimization_barrier((window, sent, second))
-    moments = far_exchange(sent)
-    near = call(functools.partial(near_kernel, owners), field32, near_cols, second, window, near_vals,
-                specs=[VMEM] * 3 + [HBM], scratch=stage(kinds), flops=96 * tile, moved=3 * tile)
+    moments, near = exchange(sent, charge, from_behind(charges, "blk", 1), own)
+    total, second = call(functools.partial(middle_kernel, owners), (pltpu.VMEM(charges.shape, F32), field16),
+                                 far_cols, moments, coupling, target, near, flops=48 * tile, moved=tile)
+    sent = call(moments_kernel, copies, second, source, flops=16 * tile, moved=tile)
+    own, potential_one = call(own_store_kernel, (field32, field32), second, near_vals, *pinned(pltpu.VMEM, total),
+                              specs=[VMEM, HBM, VMEM], scratch=stage(1), flops=32 * tile, moved=tile)
+    moments, near = exchange(sent, second, from_behind(second, "blk", 1), own)
     potential_two = call(functools.partial(last_kernel, owners), field32,
                          far_cols, moments, coupling, target, near, flops=48 * tile, moved=tile)
     return (potential_one, potential_two)

time: 77 us -> 70.7 us (0.918)
  the two profiles are of different devices: /device:TPU:1 before, /device:TPU:17 now
where the time goes in v6:
time: 70.7 us; the launch traced here: 70.2 us
  starting transfers between devices  44.4 us (63%)
  Pallas kernels  14.4 us (20%)
  waiting for transfers between devices  10.5 us (15%)
  between operations  0.81 us (1%)
    all_to_all x2, starting transfers between devices, far_exchange(): lax.all_to_all(copies, 'cluster', 0, 0, tiled=True).reshape(-1, 2 * rank)  25.8 us
    ppermute x6, starting transfers between devices, from_behind(): lax.ppermute(block, axis, [((i - distance) % size, i) for i in range(size)])  18.6 us
    pallas_call x8, Pallas kernels, call(): pl.pallas_call(kernel, out_shape=outs, in_specs=specs or [VMEM] * len(ope...  14.4 us
    ppermute x6, waiting for transfers between devices, from_behind(): lax.ppermute(block, axis, [((i - distance) % size, i) for i in range(size)])  5.44 us
    all_to_all x2, waiting for transfers between devices, far_exchange(): lax.all_to_all(copies, 'cluster', 0, 0, tiled=True).reshape(-1, 2 * rank)  5.09 us
  transfers between devices with their start and end apart: 8, of which 6 were waited for; matrix products, arithmetic and copies ran while one was open for 0% of the time, Pallas kernels for 17%

profile of v6, /device:TPU:17, one launch (start us, length us, event | category | flops | bytes accessed | tf_op | source)
XLA Modules:
  0.0 70.2 jit_solution(10317634880181334997)
XLA Ops:
  0.6 0.0 copy-start
  0.6 3.1 %collective-permute-start = (bf16[32,128]{1,0:T(8,128)(2,1)}, bf16[32,128]{1,0:T(8,128)(2,1)S(1)}, u32[]{:S(2)}, u32[]{:S(2)}) collective-permute-start(bf16[32,128]{1,0:T(8,128)(2,1)} %charge_hbm.1), channel_id=1, source_target_pairs={{480,0},{0,32},{32,64},{64,96},{96,128},{128,160},{160,192},{192,2... | collective-permute-start | bytes 24584 | tf_op jit(solution)/shard_map/ppermute | solution.py:207
  3.8 2.2 %shard_map.86 = (bf16[32,16,128]{2,1,0:T(8,128)(2,1)}, bf16[32,128]{1,0:T(8,128)(2,1)S(1)}, bf16[2048,128]{1,0:T(8,128)(2,1)S(1)}, bf16[2048,128]{1,0:T(8,128)(2,1)S(1)}, bf16[32,2,64,64]{3,2,1,0:T(8,128)(2,1)S(1)}) custom-call(bf16[32,128]{1,0:T(8,128)(2,1)} %charge_hbm.1, bf16[2048,128]{1,0:T(8,128)(2,1)} %bitcast.13, bf16[2048,128]{1,0:T(8,128)(2,1)} %bitcast.14, ...), custom_call_target="tpu_custom_call" | custom-call | flops 16777216 | bytes 2097152 | tf_op jit(solution)/shard_map/pallas_call | solution.py:194
  6.0 0.2 collective-permute-done
  6.1 3.2 %collective-permute-start.1 = (bf16[64,128]{1,0:T(8,128)(2,1)S(1)}, bf16[64,128]{1,0:T(8,128)(2,1)S(1)}, u32[]{:S(2)}, u32[]{:S(2)}) collective-permute-start(bf16[64,128]{1,0:T(8,128)(2,1)S(1)} %pad_maximum_fusion), channel_id=1, source_target_pairs={{448,0},{480,32},{0,64},{32,96},{64,128},{96,160},{128,192},{160,2... | collective-permute-start | bytes 49160 | tf_op jit(solution)/shard_map/ppermute | solution.py:207
  9.3 15.0 %all-to-all-start = ((bf16[32,16,128]{2,1,0:T(8,128)(2,1)}), bf16[32,16,128]{2,1,0:T(8,128)(2,1)S(1)}, u32[]{:S(2)}, u32[]{:S(2)}) async-start(bf16[32,16,128]{2,1,0:T(8,128)(2,1)} %get-tuple-element.16), calls=%async_computation | async-start | bytes 262144 | tf_op jit(solution)/shard_map/all_to_all | solution.py:232
  24.4 0.0 collective-permute-done.1
  24.4 1.9 %collective-permute-start.2 = (bf16[128,128]{1,0:T(8,128)(2,1)S(1)}, bf16[128,128]{1,0:T(8,128)(2,1)S(1)}, u32[]{:S(2)}, u32[]{:S(2)}) collective-permute-start(bf16[128,128]{1,0:T(8,128)(2,1)S(1)} %constant_dynamic-update-slice_fusion.low_ref), channel_id=1, source_target_pairs={{96,0},{128,32},{160,64},{192,96},{224,128},{256,160},{288,192},{3... | collective-permute-start | bytes 98312 | tf_op jit(solution)/shard_map/ppermute | solution.py:207
  26.4 0.0 copy-start.1
  26.4 1.8 %shard_map.87.own_ref = f32[32,128]{1,0:T(8,128)S(1)} custom-call(bf16[32,128]{1,0:T(8,128)(2,1)S(1)} %get-tuple-element.20.field_ref, bf16[32,3,128,128]{3,2,1,0:T(8,128)(2,1)} %vals_hbm.7), custom_call_target="tpu_custom_call" | custom-call | flops 33554432 | bytes 1048576 | tf_op jit(solution)/shard_map/pallas_call | solution.py:194
  28.2 2.1 %collective-permute-done.2.high_ref = bf16[128,128]{1,0:T(8,128)(2,1)S(1)} collective-permute-done((bf16[128,128]{1,0:T(8,128)(2,1)S(1)}, bf16[128,128]{1,0:T(8,128)(2,1)S(1)}, u32[]{:S(2)}, u32[]{:S(2)}) %collective-permute-start.2) | collective-permute-done | bytes 32800 | tf_op jit(solution)/shard_map/ppermute | solution.py:207
  30.3 0.0 copy-done
  30.3 2.3 %shard_map.88.near_ref = f32[32,128]{1,0:T(8,128)S(1)} custom-call(s32[1]{0:T(128)} %bitcast.4.pos_ref, s32[3,32]{1,0:T(4,128)S(1)} %bitcast.9, bf16[128,128]{1,0:T(8,128)(2,1)S(1)} %constant_dynamic-update-slice_fusion.low_ref, bf16[128,128]{1,0:T(8,128)(2,1)S(1)} %collective-permute-done.2.high_ref, bf16[32,3,128,128]{3,2,1,0:T(8,128)(2,1)} %vals_hbm.7, ...), custom_call_target="tpu_custom_call" | custom-call | flops 67108864 | bytes 2097152 | tf_op jit(solution)/shard_map/pallas_call | solution.py:194
  32.6 2.5 %all-to-all-done = bf16[32,16,128]{2,1,0:T(8,128)(2,1)S(1)} async-done(((bf16[32,16,128]{2,1,0:T(8,128)(2,1)}), bf16[32,16,128]{2,1,0:T(8,128)(2,1)S(1)}, u32[]{:S(2)}, u32[]{:S(2)}) %all-to-all-start) | async-done | bytes 131104 | tf_op jit(solution)/shard_map/all_to_all | solution.py:232
  35.2 0.0 copy-done.1
  35.2 1.0 %shard_map.89 = (f32[32,128]{1,0:T(8,128)S(1)}, bf16[32,128]{1,0:T(8,128)(2,1)S(1)}) custom-call(s32[2,32]{1,0:T(2,128)S(1)} %bitcast.11, bf16[512,128]{1,0:T(8,128)(2,1)S(1)} %bitcast.7, bf16[32,2,64,64]{3,2,1,0:T(8,128)(2,1)S(1)} %get-tuple-element.17.coupling_ref, bf16[2048,128]{1,0:T(8,128)(2,1)S(1)} %get-tuple-element.18.target_ref, ...), custom_call_target="tpu_custom_call" | custom-call | flops 50331648 | bytes 1048576 | tf_op jit(solution)/shard_map/pallas_call | solution.py:194
  36.2 2.8 %collective-permute-start.3 = (bf16[32,128]{1,0:T(8,128)(2,1)S(1)}, bf16[32,128]{1,0:T(8,128)(2,1)S(1)}, u32[]{:S(2)}, u32[]{:S(2)}) collective-permute-start(bf16[32,128]{1,0:T(8,128)(2,1)S(1)} %get-tuple-element.21.field_ref), channel_id=1, source_target_pairs={{480,0},{0,32},{32,64},{64,96},{96,128},{128,160},{160,192},{192,2... | collective-permute-start | bytes 24584 | tf_op jit(solution)/shard_map/ppermute | solution.py:207
  39.0 1.1 %shard_map.91 = bf16[32,16,128]{2,1,0:T(8,128)(2,1)} custom-call(bf16[32,128]{1,0:T(8,128)(2,1)S(1)} %get-tuple-element.21.field_ref, bf16[2048,128]{1,0:T(8,128)(2,1)S(1)} %get-tuple-element.24.source_ref), custom_call_target="tpu_custom_call" | custom-call | flops 16777216 | bytes 1048576 | tf_op jit(solution)/shard_map/pallas_call | solution.py:194
  40.0 1.4 %collective-permute-done.3 = bf16[32,128]{1,0:T(8,128)(2,1)S(1)} collective-permute-done((bf16[32,128]{1,0:T(8,128)(2,1)S(1)}, bf16[32,128]{1,0:T(8,128)(2,1)S(1)}, u32[]{:S(2)}, u32[]{:S(2)}) %collective-permute-start.3) | collective-permute-done | bytes 8224 | tf_op jit(solution)/shard_map/ppermute | solution.py:207
  41.5 5.6 %collective-permute-start.4 = (bf16[64,128]{1,0:T(8,128)(2,1)S(1)}, bf16[64,128]{1,0:T(8,128)(2,1)S(1)}, u32[]{:S(2)}, u32[]{:S(2)}) collective-permute-start(bf16[64,128]{1,0:T(8,128)(2,1)S(1)} %pad_maximum_fusion.1), channel_id=1, source_target_pairs={{448,0},{480,32},{0,64},{32,96},{64,128},{96,160},{128,192},{160,2... | collective-permute-start | bytes 49160 | tf_op jit(solution)/shard_map/ppermute | solution.py:207
  47.1 10.8 %all-to-all-start.1 = ((bf16[32,16,128]{2,1,0:T(8,128)(2,1)}), bf16[32,16,128]{2,1,0:T(8,128)(2,1)S(1)}, u32[]{:S(2)}, u32[]{:S(2)}) async-start(bf16[32,16,128]{2,1,0:T(8,128)(2,1)} %shard_map.91), calls=%async_computation.1 | async-start | bytes 262144 | tf_op jit(solution)/shard_map/all_to_all | solution.py:232
  57.8 0.0 collective-permute-done.4
  57.9 1.9 %collective-permute-start.5 = (bf16[128,128]{1,0:T(8,128)(2,1)S(1)}, bf16[128,128]{1,0:T(8,128)(2,1)S(1)}, u32[]{:S(2)}, u32[]{:S(2)}) collective-permute-start(bf16[128,128]{1,0:T(8,128)(2,1)S(1)} %constant_dynamic-update-slice_fusion.3.low_ref), channel_id=1, source_target_pairs={{96,0},{128,32},{160,64},{192,96},{224,128},{256,160},{288,192},{3... | collective-permute-start | bytes 98312 | tf_op jit(solution)/shard_map/ppermute | solution.py:207
  59.8 2.1 %shard_map.90 = (f32[32,128]{1,0:T(8,128)S(1)}, f32[32,128]{1,0:T(8,128)}) custom-call(bf16[32,128]{1,0:T(8,128)(2,1)S(1)} %get-tuple-element.21.field_ref, bf16[32,3,128,128]{3,2,1,0:T(8,128)(2,1)} %vals_hbm.7, f32[32,128]{1,0:T(8,128)S(1)} %get-tuple-element.22.kept_ref), custom_call_target="tpu_custom_call" | custom-call | flops 33554432 | bytes 1048576 | tf_op jit(solution)/shard_map/pallas_call | solution.py:194
  61.9 1.8 %collective-permute-done.5.high_ref = bf16[128,128]{1,0:T(8,128)(2,1)S(1)} collective-permute-done((bf16[128,128]{1,0:T(8,128)(2,1)S(1)}, bf16[128,128]{1,0:T(8,128)(2,1)S(1)}, u32[]{:S(2)}, u32[]{:S(2)}) %collective-permute-start.5) | collective-permute-done | bytes 32800 | tf_op jit(solution)/shard_map/ppermute | solution.py:207
  63.7 2.3 %shard_map.92.near_ref = f32[32,128]{1,0:T(8,128)S(1)} custom-call(s32[1]{0:T(128)} %bitcast.4.pos_ref, s32[3,32]{1,0:T(4,128)S(1)} %bitcast.10, bf16[128,128]{1,0:T(8,128)(2,1)S(1)} %constant_dynamic-update-slice_fusion.3.low_ref, bf16[128,128]{1,0:T(8,128)(2,1)S(1)} %collective-permute-done.5.high_ref, bf16[32,3,128,128]{3,2,1,0:T(8,128)(2,1)} %vals_hbm.7, ...), custom_call_target="tpu_custom_call" | custom-call | flops 67108864 | bytes 2097152 | tf_op jit(solution)/shard_map/pallas_call | solution.py:194
  66.1 2.5 %all-to-all-done.1 = bf16[32,16,128]{2,1,0:T(8,128)(2,1)S(1)} async-done(((bf16[32,16,128]{2,1,0:T(8,128)(2,1)}), bf16[32,16,128]{2,1,0:T(8,128)(2,1)S(1)}, u32[]{:S(2)}, u32[]{:S(2)}) %all-to-all-start.1) | async-done | bytes 131104 | tf_op jit(solution)/shard_map/all_to_all | solution.py:232
  68.6 1.6 %shard_map.93 = f32[32,128]{1,0:T(8,128)} custom-call(s32[2,32]{1,0:T(2,128)S(1)} %bitcast.12, bf16[512,128]{1,0:T(8,128)(2,1)S(1)} %bitcast.8, bf16[32,2,64,64]{3,2,1,0:T(8,128)(2,1)S(1)} %get-tuple-element.17.coupling_ref, bf16[2048,128]{1,0:T(8,128)(2,1)S(1)} %get-tuple-element.18.target_ref, f32[32,128]{1,0:T(8,128)S(1)} %shard_map.92.near_ref), custom_call_target="tpu_custom_call" | custom-call | flops 50331648 | bytes 1048576 | tf_op jit(solution)/shard_map/pallas_call | solution.py:194
  (8 shorter events, 0.0 us)
Async XLA Ops:
  0.6 29.7 %copy-start = (s32[32,3]{0,1:T(4,128)S(1)}, s32[32,3]{0,1:T(4,128)}, u32[]{:S(2)}) copy-start(s32[32,3]{0,1:T(4,128)} %param.9) | copy-start | bytes 1156
  0.6 5.5 %collective-permute-start = (bf16[32,128]{1,0:T(8,128)(2,1)}, bf16[32,128]{1,0:T(8,128)(2,1)S(1)}, u32[]{:S(2)}, u32[]{:S(2)}) collective-permute-start(bf16[32,128]{1,0:T(8,128)(2,1)} %charge_hbm.1), channel_id=1, source_target_pairs={{480,0},{0,32},{32,64},{64,96},{96,128},{128,160},{160,192},{192,2... | collective-permute-start | bytes 24584 | tf_op jit(solution)/shard_map/ppermute | solution.py:207
  6.1 18.3 %collective-permute-start.1 = (bf16[64,128]{1,0:T(8,128)(2,1)S(1)}, bf16[64,128]{1,0:T(8,128)(2,1)S(1)}, u32[]{:S(2)}, u32[]{:S(2)}) collective-permute-start(bf16[64,128]{1,0:T(8,128)(2,1)S(1)} %pad_maximum_fusion), channel_id=1, source_target_pairs={{448,0},{480,32},{0,64},{32,96},{64,128},{96,160},{128,192},{160,2... | collective-permute-start | bytes 49160 | tf_op jit(solution)/shard_map/ppermute | solution.py:207
  9.3 25.8 %all-to-all-start = ((bf16[32,16,128]{2,1,0:T(8,128)(2,1)}), bf16[32,16,128]{2,1,0:T(8,128)(2,1)S(1)}, u32[]{:S(2)}, u32[]{:S(2)}) async-start(bf16[32,16,128]{2,1,0:T(8,128)(2,1)} %get-tuple-element.16), calls=%async_computation | async-start | bytes 262144 | tf_op jit(solution)/shard_map/all_to_all | solution.py:232
  24.4 5.9 %collective-permute-start.2 = (bf16[128,128]{1,0:T(8,128)(2,1)S(1)}, bf16[128,128]{1,0:T(8,128)(2,1)S(1)}, u32[]{:S(2)}, u32[]{:S(2)}) collective-permute-start(bf16[128,128]{1,0:T(8,128)(2,1)S(1)} %constant_dynamic-update-slice_fusion.low_ref), channel_id=1, source_target_pairs={{96,0},{128,32},{160,64},{192,96},{224,128},{256,160},{288,192},{3... | collective-permute-start | bytes 98312 | tf_op jit(solution)/shard_map/ppermute | solution.py:207
  26.4 8.8 %copy-start.1 = (s32[32,2]{0,1:T(2,128)S(1)}, s32[32,2]{0,1:T(2,128)}, u32[]{:S(2)}) copy-start(s32[32,2]{0,1:T(2,128)} %param.13) | copy-start | bytes 772
  36.2 5.3 %collective-permute-start.3 = (bf16[32,128]{1,0:T(8,128)(2,1)S(1)}, bf16[32,128]{1,0:T(8,128)(2,1)S(1)}, u32[]{:S(2)}, u32[]{:S(2)}) collective-permute-start(bf16[32,128]{1,0:T(8,128)(2,1)S(1)} %get-tuple-element.21.field_ref), channel_id=1, source_target_pairs={{480,0},{0,32},{32,64},{64,96},{96,128},{128,160},{160,192},{192,2... | collective-permute-start | bytes 24584 | tf_op jit(solution)/shard_map/ppermute | solution.py:207
  41.5 16.4 %collective-permute-start.4 = (bf16[64,128]{1,0:T(8,128)(2,1)S(1)}, bf16[64,128]{1,0:T(8,128)(2,1)S(1)}, u32[]{:S(2)}, u32[]{:S(2)}) collective-permute-start(bf16[64,128]{1,0:T(8,128)(2,1)S(1)} %pad_maximum_fusion.1), channel_id=1, source_target_pairs={{448,0},{480,32},{0,64},{32,96},{64,128},{96,160},{128,192},{160,2... | collective-permute-start | bytes 49160 | tf_op jit(solution)/shard_map/ppermute | solution.py:207
  47.1 21.5 %all-to-all-start.1 = ((bf16[32,16,128]{2,1,0:T(8,128)(2,1)}), bf16[32,16,128]{2,1,0:T(8,128)(2,1)S(1)}, u32[]{:S(2)}, u32[]{:S(2)}) async-start(bf16[32,16,128]{2,1,0:T(8,128)(2,1)} %shard_map.91), calls=%async_computation.1 | async-start | bytes 262144 | tf_op jit(solution)/shard_map/all_to_all | solution.py:232
  57.9 5.9 %collective-permute-start.5 = (bf16[128,128]{1,0:T(8,128)(2,1)S(1)}, bf16[128,128]{1,0:T(8,128)(2,1)S(1)}, u32[]{:S(2)}, u32[]{:S(2)}) collective-permute-start(bf16[128,128]{1,0:T(8,128)(2,1)S(1)} %constant_dynamic-update-slice_fusion.3.low_ref), channel_id=1, source_target_pairs={{96,0},{128,32},{160,64},{192,96},{224,128},{256,160},{288,192},{3... | collective-permute-start | bytes 98312 | tf_op jit(solution)/shard_map/ppermute | solution.py:207

commit v7 on v6

--- a/solution.py
+++ b/solution.py
@@ -66,12 +66,15 @@
     copies_ref[...] = jnp.broadcast_to(packed.astype(BF16)[None], copies_ref.shape)
 
 
-def moments_kernel(field_ref, source_ref, copies_ref):
+def moments_kernel(field_ref, source_hbm, copies_ref, source_ref, sem):
+    move = pltpu.make_async_copy(source_hbm, source_ref, sem)
+    move.start()
+    move.wait()
     send_moments(field_ref[...], source_ref, copies_ref)
 
 
 def first_kernel(charge_hbm, source_hbm, target_hbm, coupling_hbm,
-                 copies_ref, charge_ref, source_ref, target_ref, coupling_ref, sems):
+                 copies_ref, charge_ref, target_ref, packed_ref, source_ref, coupling_ref, sems):
     pairs = [(charge_hbm, charge_ref), (source_hbm, source_ref), (coupling_hbm, coupling_ref), (target_hbm, target_ref)]
     moves = [pltpu.make_async_copy(a, b, sems.at[n]) for n, (a, b) in enumerate(pairs)]
     for move in moves:
@@ -80,6 +83,9 @@
     moves[1].wait()
     send_moments(charge_ref[...], source_ref, copies_ref)
     moves[2].wait()
+    blocks, kinds, rank, _ = coupling_ref.shape
+    for i in range(blocks):
+        packed_ref[i * rank:(i + 1) * rank, :] = jnp.concatenate([coupling_ref[i, k] for k in range(kinds)], axis=1)
     moves[3].wait()
 
 
@@ -104,24 +110,24 @@
     return own_columns(blocks, panels, product).T[:blocks]
 
 
-def own_kernel(field_ref, vals_hbm, near_ref, vals_ref, sems):
-    for move in fetch(vals_hbm.at[:, pl.ds(0, 1)], vals_ref, sems):
-        move.wait()
-    near_ref[...] = near_product([field_ref[...]], vals_ref)
-
-
-def own_store_kernel(field_ref, vals_hbm, kept_ref, near_ref, stored_ref, vals_ref, sems):
+def own_kernel(field_ref, vals_hbm, near_ref, rest_ref, vals_ref, sems, rest_sems):
     moves = fetch(vals_hbm.at[:, pl.ds(0, 1)], vals_ref, sems)
-    stored_ref[...] = kept_ref[...]
+    rest = fetch(vals_hbm.at[:, pl.ds(1, rest_ref.shape[1])], rest_ref, rest_sems)
     for move in moves:
         move.wait()
     near_ref[...] = near_product([field_ref[...]], vals_ref)
-
-
-def near_kernel(cycle_size, owners, pos_ref, cols_ref, low_ref, high_ref, vals_hbm, own_ref, near_ref, vals_ref, sems):
+    for move in rest:
+        move.wait()
+
+
+def own_store_kernel(field_ref, vals_hbm, kept_ref, near_ref, rest_ref, stored_ref, vals_ref, sems, rest_sems):
+    stored_ref[...] = kept_ref[...]
+    own_kernel(field_ref, vals_hbm, near_ref, rest_ref, vals_ref, sems, rest_sems)
+
+
+def near_kernel(cycle_size, owners, pos_ref, cols_ref, low_ref, high_ref, vals_ref, own_ref, near_ref):
     blocks = own_ref.shape[0]
     kinds = cols_ref.shape[0]
-    moves = fetch(vals_hbm.at[:, pl.ds(1, kinds - 1)], vals_ref, sems)
     cols = cols_ref[...]
     target = lax.div(cols, jnp.int32(blocks * owners))
     offset = lax.rem(target - pos_ref[0] + (cycle_size + 3), jnp.int32(cycle_size))
@@ -134,15 +140,13 @@
         beyond = jnp.where(index >= span, index - (span - blocks), -1)
         field = field + mul(pick(beyond, span), high_ref[...], NN)
         fields.append(field.astype(BF16))
-    for move in moves:
-        move.wait()
     near_ref[...] = own_ref[...] + near_product(fields, vals_ref)
 
 
 def potential(owners, cols_ref, moments_ref, coupling_ref, target_ref, near_ref):
     blocks, panels = near_ref.shape
     kinds = cols_ref.shape[0]
-    rank = coupling_ref.shape[2]
+    rank = coupling_ref.shape[0] // blocks
     half = blocks // 2
     cols = cols_ref[...]
     owner = lax.rem(lax.div(cols, jnp.int32(blocks)), jnp.int32(owners))
@@ -153,15 +157,11 @@
     for k in range(kinds):
         both = mul(pick(column(row[k:k + 1]), moments_ref.shape[0]), moments_ref[...], NN)
         both = jnp.where(column(upper[k:k + 1]) == 1, pltpu.roll(both, rank, 1), both)
-        fields.append(padded(both[:, :rank].astype(BF16)))
+        fields.append(both[:, :rank].astype(BF16))
+    wide = padded(jnp.concatenate(fields, axis=1))
 
     def product(base):
-        result = None
-        for k in range(kinds):
-            couple = coupling_ref[base:base + CHUNK, k].reshape(CHUNK * rank, rank)
-            part = mul(couple, fields[k], NT)
-            result = part if result is None else result + part
-        return result
+        return mul(coupling_ref[base * rank:(base + CHUNK) * rank, :], wide, NT)
 
     coupled = own_columns(blocks, rank, product)
     coupled = jnp.concatenate([coupled, coupled], axis=0).T[:blocks]
@@ -233,32 +233,37 @@
 
     kept = pltpu.VMEM(basis.shape, BF16)
     kinds = near_vals.shape[1]
-    near_vals, = pinned(pltpu.HBM, near_vals)
-    operands = (charges, source_basis.reshape(basis.shape), target_basis.reshape(basis.shape), coupling)
-    sent, charge, source, target, coupling = call(
-        first_kernel, (copies, pltpu.VMEM(charges.shape, BF16), kept, kept, pltpu.VMEM(coupling.shape, BF16)),
-        *pinned(pltpu.HBM, *operands), specs=[HBM] * 4, scratch=[pltpu.SemaphoreType.DMA((4,))],
+    rest = pltpu.VMEM((blocks, kinds - 1, panels, panels), BF16)
+    near_vals, charges_hbm, source, target, coupling = pinned(
+        pltpu.HBM, near_vals, charges, source_basis.reshape(basis.shape), target_basis.reshape(basis.shape), coupling)
+    sent, charge, target, coupling = call(
+        first_kernel, (copies, pltpu.VMEM(charges.shape, BF16), kept, kept), charges_hbm, source, target, coupling,
+        specs=[HBM] * 4, scratch=[kept, pltpu.VMEM(coupling.shape, BF16), pltpu.SemaphoreType.DMA((4,))],
         flops=16 * tile, moved=2 * tile)
-    source, target, coupling = pinned(pltpu.VMEM, source, target, coupling)
-
-    def exchange(sent, field, behind, own):
+    target, coupling = pinned(pltpu.VMEM, target, coupling)
+    own_scratch = stage(1) + stage(1)[1:]
+
+    def exchange(sent, field, behind, own, vals):
         behind, sent = lax.optimization_barrier((behind, sent))
         pair = jnp.concatenate([behind, field], axis=0)
         low = jnp.concatenate([from_behind(pair, "blk", 2), pair], axis=0)
         high = from_behind(low, "blk", -3)
         near = call(functools.partial(near_kernel, cycle_size, owners), field32,
-                    pos, near_cols, low, high, near_vals, own, specs=[SMEM] + [VMEM] * 3 + [HBM, VMEM],
-                    scratch=stage(kinds - 1), flops=64 * tile, moved=2 * tile)
+                    pos, near_cols, low, high, *pinned(pltpu.VMEM, vals), own, specs=[SMEM] + [VMEM] * 5,
+                    flops=64 * tile, moved=2 * tile)
         return far_exchange(sent), near
 
-    own = call(own_kernel, field32, charge, near_vals, specs=[VMEM, HBM], scratch=stage(1), flops=32 * tile, moved=tile)
-    moments, near = exchange(sent, charge, from_behind(charges, "blk", 1), own)
+    own, vals = call(own_kernel, (field32, rest), charge, near_vals, specs=[VMEM, HBM], scratch=own_scratch,
+                     flops=32 * tile, moved=3 * tile)
+    moments, near = exchange(sent, charge, from_behind(charges, "blk", 1), own, vals)
     total, second = call(functools.partial(middle_kernel, owners), (pltpu.VMEM(charges.shape, F32), field16),
-                                 far_cols, moments, coupling, target, near, flops=48 * tile, moved=tile)
-    sent = call(moments_kernel, copies, second, source, flops=16 * tile, moved=tile)
-    own, potential_one = call(own_store_kernel, (field32, field32), second, near_vals, *pinned(pltpu.VMEM, total),
-                              specs=[VMEM, HBM, VMEM], scratch=stage(1), flops=32 * tile, moved=tile)
-    moments, near = exchange(sent, second, from_behind(second, "blk", 1), own)
+                         far_cols, moments, coupling, target, near, flops=48 * tile, moved=tile)
+    sent = call(moments_kernel, copies, second, source, specs=[VMEM, HBM],
+                scratch=[kept, pltpu.SemaphoreType.DMA(())], flops=16 * tile, moved=tile)
+    own, vals, potential_one = call(
+        own_store_kernel, (field32, rest, field32), second, near_vals, *pinned(pltpu.VMEM, total),
+        specs=[VMEM, HBM, VMEM], scratch=own_scratch, flops=32 * tile, moved=3 * tile)
+    moments, near = exchange(sent, second, from_behind(second, "blk", 1), own, vals)
     potential_two = call(functools.partial(last_kernel, owners), field32,
                          far_cols, moments, coupling, target, near, flops=48 * tile, moved=tile)
     return (potential_one, potential_two)

time: 70.7 us -> 69.2 us (0.979)
  starting transfers between devices: 44.4 us -> 43 us
    ppermute x6, waiting for transfers between devices: 5.44 us -> 2.62 us  [from_behind(): lax.ppermute(block, axis, [((i - distance) % size, i) for i in range(size)])]
    all_to_all x2, waiting for transfers between devices: 5.09 us -> 7.85 us  [far_exchange(): lax.all_to_all(copies, 'cluster', 0, 0, tiled=True).reshape(-1, 2 * rank)]
    all_to_all x2, starting transfers between devices: 25.8 us -> 24.4 us  [far_exchange(): lax.all_to_all(copies, 'cluster', 0, 0, tiled=True).reshape(-1, 2 * rank)]
  transfers between devices with their start and end apart: 8 -> 8, of which waited for: 6 -> 5; matrix products, arithmetic and copies ran while one was open for 0% -> 0% of each run, Pallas kernels for 17% -> 17%
where the time goes in v7:
time: 69.2 us; the launch traced here: 68.7 us
  starting transfers between devices  43 us (62%)
  Pallas kernels  14.3 us (21%)
  waiting for transfers between devices  10.5 us (15%)
  between operations  0.82 us (1%)
    all_to_all x2, starting transfers between devices, far_exchange(): lax.all_to_all(copies, 'cluster', 0, 0, tiled=True).reshape(-1, 2 * rank)  24.4 us
    ppermute x6, starting transfers between devices, from_behind(): lax.ppermute(block, axis, [((i - distance) % size, i) for i in range(size)])  18.6 us
    pallas_call x8, Pallas kernels, call(): pl.pallas_call(kernel, out_shape=outs, in_specs=specs or [VMEM] * len(ope...  14.3 us
    all_to_all x2, waiting for transfers between devices, far_exchange(): lax.all_to_all(copies, 'cluster', 0, 0, tiled=True).reshape(-1, 2 * rank)  7.85 us
    ppermute x6, waiting for transfers between devices, from_behind(): lax.ppermute(block, axis, [((i - distance) % size, i) for i in range(size)])  2.62 us
  transfers between devices with their start and end apart: 8, of which 5 were waited for; matrix products, arithmetic and copies ran while one was open for 0% of the time, Pallas kernels for 17%

profile of v7, /device:TPU:17, one launch (start us, length us, event | category | flops | bytes accessed | tf_op | source)
XLA Modules:
  0.0 68.7 jit_solution(15116496386503684509)
XLA Ops:
  0.6 3.1 %collective-permute-start = (bf16[32,128]{1,0:T(8,128)(2,1)}, bf16[32,128]{1,0:T(8,128)(2,1)S(1)}, u32[]{:S(2)}, u32[]{:S(2)}) collective-permute-start(bf16[32,128]{1,0:T(8,128)(2,1)} %charge_hbm.1), channel_id=1, source_target_pairs={{480,0},{0,32},{32,64},{64,96},{96,128},{128,160},{160,192},{192,2... | collective-permute-start | bytes 24584 | tf_op jit(solution)/shard_map/ppermute | solution.py:207
  3.8 2.4 %shard_map.86 = (bf16[32,16,128]{2,1,0:T(8,128)(2,1)}, bf16[32,128]{1,0:T(8,128)(2,1)S(1)}, bf16[2048,128]{1,0:T(8,128)(2,1)S(1)}, bf16[2048,128]{1,0:T(8,128)(2,1)S(1)}) custom-call(bf16[32,128]{1,0:T(8,128)(2,1)} %charge_hbm.1, bf16[2048,128]{1,0:T(8,128)(2,1)} %bitcast.13, bf16[2048,128]{1,0:T(8,128)(2,1)} %bitcast.15, bf16[32,2,64,64]{3,2,1,0:T(8,128)(2,1)} %coupling_hbm.1), custom_call_target="tpu_custom_call" | custom-call | flops 16777216 | bytes 2097152 | tf_op jit(solution)/shard_map/pallas_call | solution.py:194
  6.1 0.0 copy-start
  6.2 0.0 collective-permute-done
  6.2 3.2 %collective-permute-start.1 = (bf16[64,128]{1,0:T(8,128)(2,1)S(1)}, bf16[64,128]{1,0:T(8,128)(2,1)S(1)}, u32[]{:S(2)}, u32[]{:S(2)}) collective-permute-start(bf16[64,128]{1,0:T(8,128)(2,1)S(1)} %pad_maximum_fusion), channel_id=1, source_target_pairs={{448,0},{480,32},{0,64},{32,96},{64,128},{96,160},{128,192},{160,2... | collective-permute-start | bytes 49160 | tf_op jit(solution)/shard_map/ppermute | solution.py:207
  9.4 15.0 %all-to-all-start = ((bf16[32,16,128]{2,1,0:T(8,128)(2,1)}), bf16[32,16,128]{2,1,0:T(8,128)(2,1)S(1)}, u32[]{:S(2)}, u32[]{:S(2)}) async-start(bf16[32,16,128]{2,1,0:T(8,128)(2,1)} %get-tuple-element.18), calls=%async_computation | async-start | bytes 262144 | tf_op jit(solution)/shard_map/all_to_all | solution.py:232
  24.4 0.0 collective-permute-done.1
  24.4 1.9 %collective-permute-start.2 = (bf16[128,128]{1,0:T(8,128)(2,1)S(1)}, bf16[128,128]{1,0:T(8,128)(2,1)S(1)}, u32[]{:S(2)}, u32[]{:S(2)}) collective-permute-start(bf16[128,128]{1,0:T(8,128)(2,1)S(1)} %constant_dynamic-update-slice_fusion.low_ref), channel_id=1, source_target_pairs={{96,0},{128,32},{160,64},{192,96},{224,128},{256,160},{288,192},{3... | collective-permute-start | bytes 98312 | tf_op jit(solution)/shard_map/ppermute | solution.py:207
  26.4 0.0 copy-start.1
  26.4 2.4 %shard_map.87 = (f32[32,128]{1,0:T(8,128)S(1)}, bf16[32,2,128,128]{3,2,1,0:T(8,128)(2,1)S(1)}) custom-call(bf16[32,128]{1,0:T(8,128)(2,1)S(1)} %get-tuple-element.22.field_ref, bf16[32,3,128,128]{3,2,1,0:T(8,128)(2,1)} %vals_hbm.3), custom_call_target="tpu_custom_call" | custom-call | flops 33554432 | bytes 3145728 | tf_op jit(solution)/shard_map/pallas_call | solution.py:194
  28.8 1.5 %collective-permute-done.2.high_ref = bf16[128,128]{1,0:T(8,128)(2,1)S(1)} collective-permute-done((bf16[128,128]{1,0:T(8,128)(2,1)S(1)}, bf16[128,128]{1,0:T(8,128)(2,1)S(1)}, u32[]{:S(2)}, u32[]{:S(2)}) %collective-permute-start.2) | collective-permute-done | bytes 32800 | tf_op jit(solution)/shard_map/ppermute | solution.py:207
  30.3 0.0 copy-done
  30.3 1.0 %shard_map.88.near_ref = f32[32,128]{1,0:T(8,128)S(1)} custom-call(s32[1]{0:T(128)} %bitcast.4.pos_ref, s32[3,32]{1,0:T(4,128)S(1)} %bitcast.9, bf16[128,128]{1,0:T(8,128)(2,1)S(1)} %constant_dynamic-update-slice_fusion.low_ref, bf16[128,128]{1,0:T(8,128)(2,1)S(1)} %collective-permute-done.2.high_ref, ...), custom_call_target="tpu_custom_call" | custom-call | flops 67108864 | bytes 2097152 | tf_op jit(solution)/shard_map/pallas_call | solution.py:194
  31.3 3.9 %all-to-all-done = bf16[32,16,128]{2,1,0:T(8,128)(2,1)S(1)} async-done(((bf16[32,16,128]{2,1,0:T(8,128)(2,1)}), bf16[32,16,128]{2,1,0:T(8,128)(2,1)S(1)}, u32[]{:S(2)}, u32[]{:S(2)}) %all-to-all-start) | async-done | bytes 131104 | tf_op jit(solution)/shard_map/all_to_all | solution.py:232
  35.2 0.0 copy-done.1
  35.2 0.9 %shard_map.89 = (f32[32,128]{1,0:T(8,128)S(1)}, bf16[32,128]{1,0:T(8,128)(2,1)S(1)}) custom-call(s32[2,32]{1,0:T(2,128)S(1)} %bitcast.11, bf16[512,128]{1,0:T(8,128)(2,1)S(1)} %bitcast.7, bf16[2048,128]{1,0:T(8,128)(2,1)S(1)} %get-tuple-element.19.coupling_ref, bf16[2048,128]{1,0:T(8,128)(2,1)S(1)} %get-tuple-element.20.target_ref, ...), custom_call_target="tpu_custom_call" | custom-call | flops 50331648 | bytes 1048576 | tf_op jit(solution)/shard_map/pallas_call | solution.py:194
  36.1 2.9 %collective-permute-start.3 = (bf16[32,128]{1,0:T(8,128)(2,1)S(1)}, bf16[32,128]{1,0:T(8,128)(2,1)S(1)}, u32[]{:S(2)}, u32[]{:S(2)}) collective-permute-start(bf16[32,128]{1,0:T(8,128)(2,1)S(1)} %get-tuple-element.25.field_ref), channel_id=1, source_target_pairs={{480,0},{0,32},{32,64},{64,96},{96,128},{128,160},{160,192},{192,2... | collective-permute-start | bytes 24584 | tf_op jit(solution)/shard_map/ppermute | solution.py:207
  39.0 2.1 %shard_map.91 = bf16[32,16,128]{2,1,0:T(8,128)(2,1)} custom-call(bf16[32,128]{1,0:T(8,128)(2,1)S(1)} %get-tuple-element.25.field_ref, bf16[2048,128]{1,0:T(8,128)(2,1)} %bitcast.14), custom_call_target="tpu_custom_call" | custom-call | flops 16777216 | bytes 1048576 | tf_op jit(solution)/shard_map/pallas_call | solution.py:194
  41.2 0.2 collective-permute-done.3
  41.4 5.6 %collective-permute-start.4 = (bf16[64,128]{1,0:T(8,128)(2,1)S(1)}, bf16[64,128]{1,0:T(8,128)(2,1)S(1)}, u32[]{:S(2)}, u32[]{:S(2)}) collective-permute-start(bf16[64,128]{1,0:T(8,128)(2,1)S(1)} %pad_maximum_fusion.1), channel_id=1, source_target_pairs={{448,0},{480,32},{0,64},{32,96},{64,128},{96,160},{128,192},{160,2... | collective-permute-start | bytes 49160 | tf_op jit(solution)/shard_map/ppermute | solution.py:207
  47.0 9.4 %all-to-all-start.1 = ((bf16[32,16,128]{2,1,0:T(8,128)(2,1)}), bf16[32,16,128]{2,1,0:T(8,128)(2,1)S(1)}, u32[]{:S(2)}, u32[]{:S(2)}) async-start(bf16[32,16,128]{2,1,0:T(8,128)(2,1)} %shard_map.91), calls=%async_computation.1 | async-start | bytes 262144 | tf_op jit(solution)/shard_map/all_to_all | solution.py:232
  56.4 0.0 collective-permute-done.4
  56.4 1.9 %collective-permute-start.5 = (bf16[128,128]{1,0:T(8,128)(2,1)S(1)}, bf16[128,128]{1,0:T(8,128)(2,1)S(1)}, u32[]{:S(2)}, u32[]{:S(2)}) collective-permute-start(bf16[128,128]{1,0:T(8,128)(2,1)S(1)} %constant_dynamic-update-slice_fusion.3.low_ref), channel_id=1, source_target_pairs={{96,0},{128,32},{160,64},{192,96},{224,128},{256,160},{288,192},{3... | collective-permute-start | bytes 98312 | tf_op jit(solution)/shard_map/ppermute | solution.py:207
  58.4 3.0 %shard_map.90 = (f32[32,128]{1,0:T(8,128)S(1)}, bf16[32,2,128,128]{3,2,1,0:T(8,128)(2,1)S(1)}, f32[32,128]{1,0:T(8,128)}) custom-call(bf16[32,128]{1,0:T(8,128)(2,1)S(1)} %get-tuple-element.25.field_ref, bf16[32,3,128,128]{3,2,1,0:T(8,128)(2,1)} %vals_hbm.3, f32[32,128]{1,0:T(8,128)S(1)} %get-tuple-element.26.kept_ref), custom_call_target="tpu_custom_call" | custom-call | flops 33554432 | bytes 3145728 | tf_op jit(solution)/shard_map/pallas_call | solution.py:194
  61.4 0.9 %collective-permute-done.5.high_ref = bf16[128,128]{1,0:T(8,128)(2,1)S(1)} collective-permute-done((bf16[128,128]{1,0:T(8,128)(2,1)S(1)}, bf16[128,128]{1,0:T(8,128)(2,1)S(1)}, u32[]{:S(2)}, u32[]{:S(2)}) %collective-permute-start.5) | collective-permute-done | bytes 32800 | tf_op jit(solution)/shard_map/ppermute | solution.py:207
  62.3 1.0 %shard_map.92.near_ref = f32[32,128]{1,0:T(8,128)S(1)} custom-call(s32[1]{0:T(128)} %bitcast.4.pos_ref, s32[3,32]{1,0:T(4,128)S(1)} %bitcast.10, bf16[128,128]{1,0:T(8,128)(2,1)S(1)} %constant_dynamic-update-slice_fusion.3.low_ref, bf16[128,128]{1,0:T(8,128)(2,1)S(1)} %collective-permute-done.5.high_ref, ...), custom_call_target="tpu_custom_call" | custom-call | flops 67108864 | bytes 2097152 | tf_op jit(solution)/shard_map/pallas_call | solution.py:194
  63.2 3.9 %all-to-all-done.1 = bf16[32,16,128]{2,1,0:T(8,128)(2,1)S(1)} async-done(((bf16[32,16,128]{2,1,0:T(8,128)(2,1)}), bf16[32,16,128]{2,1,0:T(8,128)(2,1)S(1)}, u32[]{:S(2)}, u32[]{:S(2)}) %all-to-all-start.1) | async-done | bytes 131104 | tf_op jit(solution)/shard_map/all_to_all | solution.py:232
  67.1 1.5 %shard_map.93 = f32[32,128]{1,0:T(8,128)} custom-call(s32[2,32]{1,0:T(2,128)S(1)} %bitcast.12, bf16[512,128]{1,0:T(8,128)(2,1)S(1)} %bitcast.8, bf16[2048,128]{1,0:T(8,128)(2,1)S(1)} %get-tuple-element.19.coupling_ref, bf16[2048,128]{1,0:T(8,128)(2,1)S(1)} %get-tuple-element.20.target_ref, f32[32,128]{1,0:T(8,128)S(1)} %shard_map.92.near_ref), custom_call_target="tpu_custom_call" | custom-call | flops 50331648 | bytes 1048576 | tf_op jit(solution)/shard_map/pallas_call | solution.py:194
  (8 shorter events, 0.0 us)
Async XLA Ops:
  0.6 5.5 %collective-permute-start = (bf16[32,128]{1,0:T(8,128)(2,1)}, bf16[32,128]{1,0:T(8,128)(2,1)S(1)}, u32[]{:S(2)}, u32[]{:S(2)}) collective-permute-start(bf16[32,128]{1,0:T(8,128)(2,1)} %charge_hbm.1), channel_id=1, source_target_pairs={{480,0},{0,32},{32,64},{64,96},{96,128},{128,160},{160,192},{192,2... | collective-permute-start | bytes 24584 | tf_op jit(solution)/shard_map/ppermute | solution.py:207
  6.1 24.1 %copy-start = (s32[32,3]{0,1:T(4,128)S(1)}, s32[32,3]{0,1:T(4,128)}, u32[]{:S(2)}) copy-start(s32[32,3]{0,1:T(4,128)} %param.9) | copy-start | bytes 1156
  6.2 18.2 %collective-permute-start.1 = (bf16[64,128]{1,0:T(8,128)(2,1)S(1)}, bf16[64,128]{1,0:T(8,128)(2,1)S(1)}, u32[]{:S(2)}, u32[]{:S(2)}) collective-permute-start(bf16[64,128]{1,0:T(8,128)(2,1)S(1)} %pad_maximum_fusion), channel_id=1, source_target_pairs={{448,0},{480,32},{0,64},{32,96},{64,128},{96,160},{128,192},{160,2... | collective-permute-start | bytes 49160 | tf_op jit(solution)/shard_map/ppermute | solution.py:207
  9.4 25.8 %all-to-all-start = ((bf16[32,16,128]{2,1,0:T(8,128)(2,1)}), bf16[32,16,128]{2,1,0:T(8,128)(2,1)S(1)}, u32[]{:S(2)}, u32[]{:S(2)}) async-start(bf16[32,16,128]{2,1,0:T(8,128)(2,1)} %get-tuple-element.18), calls=%async_computation | async-start | bytes 262144 | tf_op jit(solution)/shard_map/all_to_all | solution.py:232
  24.4 5.9 %collective-permute-start.2 = (bf16[128,128]{1,0:T(8,128)(2,1)S(1)}, bf16[128,128]{1,0:T(8,128)(2,1)S(1)}, u32[]{:S(2)}, u32[]{:S(2)}) collective-permute-start(bf16[128,128]{1,0:T(8,128)(2,1)S(1)} %constant_dynamic-update-slice_fusion.low_ref), channel_id=1, source_target_pairs={{96,0},{128,32},{160,64},{192,96},{224,128},{256,160},{288,192},{3... | collective-permute-start | bytes 98312 | tf_op jit(solution)/shard_map/ppermute | solution.py:207
  26.4 8.8 %copy-start.1 = (s32[32,2]{0,1:T(2,128)S(1)}, s32[32,2]{0,1:T(2,128)}, u32[]{:S(2)}) copy-start(s32[32,2]{0,1:T(2,128)} %param.13) | copy-start | bytes 772
  36.1 5.3 %collective-permute-start.3 = (bf16[32,128]{1,0:T(8,128)(2,1)S(1)}, bf16[32,128]{1,0:T(8,128)(2,1)S(1)}, u32[]{:S(2)}, u32[]{:S(2)}) collective-permute-start(bf16[32,128]{1,0:T(8,128)(2,1)S(1)} %get-tuple-element.25.field_ref), channel_id=1, source_target_pairs={{480,0},{0,32},{32,64},{64,96},{96,128},{128,160},{160,192},{192,2... | collective-permute-start | bytes 24584 | tf_op jit(solution)/shard_map/ppermute | solution.py:207
  41.4 15.0 %collective-permute-start.4 = (bf16[64,128]{1,0:T(8,128)(2,1)S(1)}, bf16[64,128]{1,0:T(8,128)(2,1)S(1)}, u32[]{:S(2)}, u32[]{:S(2)}) collective-permute-start(bf16[64,128]{1,0:T(8,128)(2,1)S(1)} %pad_maximum_fusion.1), channel_id=1, source_target_pairs={{448,0},{480,32},{0,64},{32,96},{64,128},{96,160},{128,192},{160,2... | collective-permute-start | bytes 49160 | tf_op jit(solution)/shard_map/ppermute | solution.py:207
  47.0 20.2 %all-to-all-start.1 = ((bf16[32,16,128]{2,1,0:T(8,128)(2,1)}), bf16[32,16,128]{2,1,0:T(8,128)(2,1)S(1)}, u32[]{:S(2)}, u32[]{:S(2)}) async-start(bf16[32,16,128]{2,1,0:T(8,128)(2,1)} %shard_map.91), calls=%async_computation.1 | async-start | bytes 262144 | tf_op jit(solution)/shard_map/all_to_all | solution.py:232
  56.4 5.9 %collective-permute-start.5 = (bf16[128,128]{1,0:T(8,128)(2,1)S(1)}, bf16[128,128]{1,0:T(8,128)(2,1)S(1)}, u32[]{:S(2)}, u32[]{:S(2)}) collective-permute-start(bf16[128,128]{1,0:T(8,128)(2,1)S(1)} %constant_dynamic-update-slice_fusion.3.low_ref), channel_id=1, source_target_pairs={{96,0},{128,32},{160,64},{192,96},{224,128},{256,160},{288,192},{3... | collective-permute-start | bytes 98312 | tf_op jit(solution)/shard_map/ppermute | solution.py:207

commit v8 on v7

--- a/solution.py
+++ b/solution.py
@@ -13,6 +13,7 @@
 NN = (((1,), (0,)), ((), ()))
 CHUNK = 4
 LANES = 128
+CHAIN = (-3, 2, 1)
 
 
 def mul(a, b, dims):
@@ -125,20 +126,22 @@
     own_kernel(field_ref, vals_hbm, near_ref, rest_ref, vals_ref, sems, rest_sems)
 
 
-def near_kernel(cycle_size, owners, pos_ref, cols_ref, low_ref, high_ref, vals_ref, own_ref, near_ref):
+def near_kernel(cycle_size, owners, order, pos_ref, cols_ref, low_ref, high_ref, vals_ref, own_ref, near_ref):
     blocks = own_ref.shape[0]
     kinds = cols_ref.shape[0]
     cols = cols_ref[...]
     target = lax.div(cols, jnp.int32(blocks * owners))
-    offset = lax.rem(target - pos_ref[0] + (cycle_size + 3), jnp.int32(cycle_size))
-    row = offset * blocks + lax.rem(cols, jnp.int32(blocks))
+    offset = lax.rem(target - pos_ref[0] + cycle_size, jnp.int32(cycle_size))
+    slot = jnp.zeros(cols.shape, jnp.int32)
+    for place in range(len(order) - 1, -1, -1):
+        slot = jnp.where(offset == order[place] % cycle_size, place, slot)
+    row = slot * blocks + lax.rem(cols, jnp.int32(blocks))
     span = low_ref.shape[0]
     fields = []
     for k in range(1, kinds):
         index = column(row[k:k + 1])
         field = mul(pick(index, span), low_ref[...], NN)
-        beyond = jnp.where(index >= span, index - (span - blocks), -1)
-        field = field + mul(pick(beyond, span), high_ref[...], NN)
+        field = field + mul(pick(index - span, span), high_ref[...], NN)
         fields.append(field.astype(BF16))
     near_ref[...] = own_ref[...] + near_product(fields, vals_ref)
 
@@ -241,21 +244,25 @@
         specs=[HBM] * 4, scratch=[kept, pltpu.VMEM(coupling.shape, BF16), pltpu.SemaphoreType.DMA((4,))],
         flops=16 * tile, moved=2 * tile)
     target, coupling = pinned(pltpu.VMEM, target, coupling)
+    order = [0]
+    for distance in CHAIN:
+        order = [place - distance for place in order] + order
+    order = order[4:] + order[:4]
     own_scratch = stage(1) + stage(1)[1:]
 
     def exchange(sent, field, behind, own, vals):
         behind, sent = lax.optimization_barrier((behind, sent))
         pair = jnp.concatenate([behind, field], axis=0)
-        low = jnp.concatenate([from_behind(pair, "blk", 2), pair], axis=0)
-        high = from_behind(low, "blk", -3)
-        near = call(functools.partial(near_kernel, cycle_size, owners), field32,
+        low = jnp.concatenate([from_behind(pair, "blk", CHAIN[1]), pair], axis=0)
+        high = from_behind(low, "blk", CHAIN[2])
+        near = call(functools.partial(near_kernel, cycle_size, owners, order), field32,
                     pos, near_cols, low, high, *pinned(pltpu.VMEM, vals), own, specs=[SMEM] + [VMEM] * 5,
                     flops=64 * tile, moved=2 * tile)
         return far_exchange(sent), near
 
     own, vals = call(own_kernel, (field32, rest), charge, near_vals, specs=[VMEM, HBM], scratch=own_scratch,
                      flops=32 * tile, moved=3 * tile)
-    moments, near = exchange(sent, charge, from_behind(charges, "blk", 1), own, vals)
+    moments, near = exchange(sent, charge, from_behind(charges, "blk", CHAIN[0]), own, vals)
     total, second = call(functools.partial(middle_kernel, owners), (pltpu.VMEM(charges.shape, F32), field16),
                          far_cols, moments, coupling, target, near, flops=48 * tile, moved=tile)
     sent = call(moments_kernel, copies, second, source, specs=[VMEM, HBM],
@@ -263,7 +270,7 @@
     own, vals, potential_one = call(
         own_store_kernel, (field32, rest, field32), second, near_vals, *pinned(pltpu.VMEM, total),
         specs=[VMEM, HBM, VMEM], scratch=own_scratch, flops=32 * tile, moved=3 * tile)
-    moments, near = exchange(sent, second, from_behind(second, "blk", 1), own, vals)
+    moments, near = exchange(sent, second, from_behind(second, "blk", CHAIN[0]), own, vals)
     potential_two = call(functools.partial(last_kernel, owners), field32,
                          far_cols, moments, coupling, target, near, flops=48 * tile, moved=tile)
     return (potential_one, potential_two)

time: 69.2 us -> 68 us (0.983)
  the two profiles are of different devices: /device:TPU:17 before, /device:TPU:1 now
where the time goes in v8:
time: 68 us; the launch traced here: 67.2 us
  starting transfers between devices  42.9 us (63%)
  Pallas kernels  14.3 us (21%)
  waiting for transfers between devices  9.12 us (13%)
  between operations  0.83 us (1%)
    ppermute x6, starting transfers between devices, from_behind(): lax.ppermute(block, axis, [((i - distance) % size, i) for i in range(size)])  22.2 us
    all_to_all x2, starting transfers between devices, far_exchange(): lax.all_to_all(copies, 'cluster', 0, 0, tiled=True).reshape(-1, 2 * rank)  20.7 us
    pallas_call x8, Pallas kernels, call(): pl.pallas_call(kernel, out_shape=outs, in_specs=specs or [VMEM] * len(ope...  14.3 us
    all_to_all x2, waiting for transfers between devices, far_exchange(): lax.all_to_all(copies, 'cluster', 0, 0, tiled=True).reshape(-1, 2 * rank)  5.39 us
    ppermute x6, waiting for transfers between devices, from_behind(): lax.ppermute(block, axis, [((i - distance) % size, i) for i in range(size)])  3.74 us
  transfers between devices with their start and end apart: 8, of which 4 were waited for; matrix products, arithmetic and copies ran while one was open for 0% of the time, Pallas kernels for 18%

profile of v8, /device:TPU:1, one launch (start us, length us, event | category | flops | bytes accessed | tf_op | source)
XLA Modules:
  0.0 67.2 jit_solution(16677232479088406882)
XLA Ops:
  0.6 7.6 %collective-permute-start = (bf16[32,128]{1,0:T(8,128)(2,1)}, bf16[32,128]{1,0:T(8,128)(2,1)S(1)}, u32[]{:S(2)}, u32[]{:S(2)}) collective-permute-start(bf16[32,128]{1,0:T(8,128)(2,1)} %charge_hbm.1), channel_id=1, source_target_pairs={{96,0},{128,32},{160,64},{192,96},{224,128},{256,160},{288,192},{3... | collective-permute-start | bytes 24584 | tf_op jit(solution)/shard_map/ppermute | solution.py:210
  8.3 2.4 %shard_map.86 = (bf16[32,16,128]{2,1,0:T(8,128)(2,1)}, bf16[32,128]{1,0:T(8,128)(2,1)S(1)}, bf16[2048,128]{1,0:T(8,128)(2,1)S(1)}, bf16[2048,128]{1,0:T(8,128)(2,1)S(1)}) custom-call(bf16[32,128]{1,0:T(8,128)(2,1)} %charge_hbm.1, bf16[2048,128]{1,0:T(8,128)(2,1)} %bitcast.13, bf16[2048,128]{1,0:T(8,128)(2,1)} %bitcast.15, bf16[32,2,64,64]{3,2,1,0:T(8,128)(2,1)} %coupling_hbm.1), custom_call_target="tpu_custom_call" | custom-call | flops 16777216 | bytes 2097152 | tf_op jit(solution)/shard_map/pallas_call | solution.py:197
  10.7 0.0 copy-start
  10.7 0.0 collective-permute-done
  10.7 2.3 %collective-permute-start.1 = (bf16[64,128]{1,0:T(8,128)(2,1)S(1)}, bf16[64,128]{1,0:T(8,128)(2,1)S(1)}, u32[]{:S(2)}, u32[]{:S(2)}) collective-permute-start(bf16[64,128]{1,0:T(8,128)(2,1)S(1)} %pad_maximum_fusion), channel_id=1, source_target_pairs={{448,0},{480,32},{0,64},{32,96},{64,128},{96,160},{128,192},{160,2... | collective-permute-start | bytes 49160 | tf_op jit(solution)/shard_map/ppermute | solution.py:210
  13.0 13.9 %all-to-all-start = ((bf16[32,16,128]{2,1,0:T(8,128)(2,1)}), bf16[32,16,128]{2,1,0:T(8,128)(2,1)S(1)}, u32[]{:S(2)}, u32[]{:S(2)}) async-start(bf16[32,16,128]{2,1,0:T(8,128)(2,1)} %get-tuple-element.18), calls=%async_computation | async-start | bytes 262144 | tf_op jit(solution)/shard_map/all_to_all | solution.py:235
  26.9 0.0 collective-permute-done.1
  27.0 1.9 %collective-permute-start.2 = (bf16[128,128]{1,0:T(8,128)(2,1)S(1)}, bf16[128,128]{1,0:T(8,128)(2,1)S(1)}, u32[]{:S(2)}, u32[]{:S(2)}) collective-permute-start(bf16[128,128]{1,0:T(8,128)(2,1)S(1)} %constant_dynamic-update-slice_fusion.low_ref), channel_id=1, source_target_pairs={{480,0},{0,32},{32,64},{64,96},{96,128},{128,160},{160,192},{192,2... | collective-permute-start | bytes 98312 | tf_op jit(solution)/shard_map/ppermute | solution.py:210
  28.9 0.0 copy-start.1
  28.9 2.4 %shard_map.87 = (f32[32,128]{1,0:T(8,128)S(1)}, bf16[32,2,128,128]{3,2,1,0:T(8,128)(2,1)S(1)}) custom-call(bf16[32,128]{1,0:T(8,128)(2,1)S(1)} %get-tuple-element.22.field_ref, bf16[32,3,128,128]{3,2,1,0:T(8,128)(2,1)} %vals_hbm.3), custom_call_target="tpu_custom_call" | custom-call | flops 33554432 | bytes 3145728 | tf_op jit(solution)/shard_map/pallas_call | solution.py:197
  31.3 2.7 %collective-permute-done.2.high_ref = bf16[128,128]{1,0:T(8,128)(2,1)S(1)} collective-permute-done((bf16[128,128]{1,0:T(8,128)(2,1)S(1)}, bf16[128,128]{1,0:T(8,128)(2,1)S(1)}, u32[]{:S(2)}, u32[]{:S(2)}) %collective-permute-start.2) | collective-permute-done | bytes 32800 | tf_op jit(solution)/shard_map/ppermute | solution.py:210
  34.0 0.0 copy-done
  34.0 1.0 %shard_map.88.near_ref = f32[32,128]{1,0:T(8,128)S(1)} custom-call(s32[1]{0:T(128)} %bitcast.4.pos_ref, s32[3,32]{1,0:T(4,128)S(1)} %bitcast.9, bf16[128,128]{1,0:T(8,128)(2,1)S(1)} %constant_dynamic-update-slice_fusion.low_ref, bf16[128,128]{1,0:T(8,128)(2,1)S(1)} %collective-permute-done.2.high_ref, ...), custom_call_target="tpu_custom_call" | custom-call | flops 67108864 | bytes 2097152 | tf_op jit(solution)/shard_map/pallas_call | solution.py:197
  35.0 2.7 %all-to-all-done = bf16[32,16,128]{2,1,0:T(8,128)(2,1)S(1)} async-done(((bf16[32,16,128]{2,1,0:T(8,128)(2,1)}), bf16[32,16,128]{2,1,0:T(8,128)(2,1)S(1)}, u32[]{:S(2)}, u32[]{:S(2)}) %all-to-all-start) | async-done | bytes 131104 | tf_op jit(solution)/shard_map/all_to_all | solution.py:235
  37.7 0.0 copy-done.1
  37.7 0.9 %shard_map.89 = (f32[32,128]{1,0:T(8,128)S(1)}, bf16[32,128]{1,0:T(8,128)(2,1)S(1)}) custom-call(s32[2,32]{1,0:T(2,128)S(1)} %bitcast.11, bf16[512,128]{1,0:T(8,128)(2,1)S(1)} %bitcast.7, bf16[2048,128]{1,0:T(8,128)(2,1)S(1)} %get-tuple-element.19.coupling_ref, bf16[2048,128]{1,0:T(8,128)(2,1)S(1)} %get-tuple-element.20.target_ref, ...), custom_call_target="tpu_custom_call" | custom-call | flops 50331648 | bytes 1048576 | tf_op jit(solution)/shard_map/pallas_call | solution.py:197
  38.6 5.4 %collective-permute-start.3 = (bf16[32,128]{1,0:T(8,128)(2,1)S(1)}, bf16[32,128]{1,0:T(8,128)(2,1)S(1)}, u32[]{:S(2)}, u32[]{:S(2)}) collective-permute-start(bf16[32,128]{1,0:T(8,128)(2,1)S(1)} %get-tuple-element.25.field_ref), channel_id=1, source_target_pairs={{96,0},{128,32},{160,64},{192,96},{224,128},{256,160},{288,192},{3... | collective-permute-start | bytes 24584 | tf_op jit(solution)/shard_map/ppermute | solution.py:210
  44.0 2.1 %shard_map.91 = bf16[32,16,128]{2,1,0:T(8,128)(2,1)} custom-call(bf16[32,128]{1,0:T(8,128)(2,1)S(1)} %get-tuple-element.25.field_ref, bf16[2048,128]{1,0:T(8,128)(2,1)} %bitcast.14), custom_call_target="tpu_custom_call" | custom-call | flops 16777216 | bytes 1048576 | tf_op jit(solution)/shard_map/pallas_call | solution.py:197
  46.2 0.0 collective-permute-done.3
  46.2 1.9 %collective-permute-start.4 = (bf16[64,128]{1,0:T(8,128)(2,1)S(1)}, bf16[64,128]{1,0:T(8,128)(2,1)S(1)}, u32[]{:S(2)}, u32[]{:S(2)}) collective-permute-start(bf16[64,128]{1,0:T(8,128)(2,1)S(1)} %pad_maximum_fusion.1), channel_id=1, source_target_pairs={{448,0},{480,32},{0,64},{32,96},{64,128},{96,160},{128,192},{160,2... | collective-permute-start | bytes 49160 | tf_op jit(solution)/shard_map/ppermute | solution.py:210
  48.1 6.8 %all-to-all-start.1 = ((bf16[32,16,128]{2,1,0:T(8,128)(2,1)}), bf16[32,16,128]{2,1,0:T(8,128)(2,1)S(1)}, u32[]{:S(2)}, u32[]{:S(2)}) async-start(bf16[32,16,128]{2,1,0:T(8,128)(2,1)} %shard_map.91), calls=%async_computation.1 | async-start | bytes 262144 | tf_op jit(solution)/shard_map/all_to_all | solution.py:235
  54.9 0.0 collective-permute-done.4
  55.0 3.0 %collective-permute-start.5 = (bf16[128,128]{1,0:T(8,128)(2,1)S(1)}, bf16[128,128]{1,0:T(8,128)(2,1)S(1)}, u32[]{:S(2)}, u32[]{:S(2)}) collective-permute-start(bf16[128,128]{1,0:T(8,128)(2,1)S(1)} %constant_dynamic-update-slice_fusion.3.low_ref), channel_id=1, source_target_pairs={{480,0},{0,32},{32,64},{64,96},{96,128},{128,160},{160,192},{192,2... | collective-permute-start | bytes 98312 | tf_op jit(solution)/shard_map/ppermute | solution.py:210
  58.0 3.0 %shard_map.90 = (f32[32,128]{1,0:T(8,128)S(1)}, bf16[32,2,128,128]{3,2,1,0:T(8,128)(2,1)S(1)}, f32[32,128]{1,0:T(8,128)}) custom-call(bf16[32,128]{1,0:T(8,128)(2,1)S(1)} %get-tuple-element.25.field_ref, bf16[32,3,128,128]{3,2,1,0:T(8,128)(2,1)} %vals_hbm.3, f32[32,128]{1,0:T(8,128)S(1)} %get-tuple-element.26.kept_ref), custom_call_target="tpu_custom_call" | custom-call | flops 33554432 | bytes 3145728 | tf_op jit(solution)/shard_map/pallas_call | solution.py:197
  61.0 1.0 %collective-permute-done.5.high_ref = bf16[128,128]{1,0:T(8,128)(2,1)S(1)} collective-permute-done((bf16[128,128]{1,0:T(8,128)(2,1)S(1)}, bf16[128,128]{1,0:T(8,128)(2,1)S(1)}, u32[]{:S(2)}, u32[]{:S(2)}) %collective-permute-start.5) | collective-permute-done | bytes 32800 | tf_op jit(solution)/shard_map/ppermute | solution.py:210
  62.0 1.0 %shard_map.92.near_ref = f32[32,128]{1,0:T(8,128)S(1)} custom-call(s32[1]{0:T(128)} %bitcast.4.pos_ref, s32[3,32]{1,0:T(4,128)S(1)} %bitcast.10, bf16[128,128]{1,0:T(8,128)(2,1)S(1)} %constant_dynamic-update-slice_fusion.3.low_ref, bf16[128,128]{1,0:T(8,128)(2,1)S(1)} %collective-permute-done.5.high_ref, ...), custom_call_target="tpu_custom_call" | custom-call | flops 67108864 | bytes 2097152 | tf_op jit(solution)/shard_map/pallas_call | solution.py:197
  63.0 2.7 %all-to-all-done.1 = bf16[32,16,128]{2,1,0:T(8,128)(2,1)S(1)} async-done(((bf16[32,16,128]{2,1,0:T(8,128)(2,1)}), bf16[32,16,128]{2,1,0:T(8,128)(2,1)S(1)}, u32[]{:S(2)}, u32[]{:S(2)}) %all-to-all-start.1) | async-done | bytes 131104 | tf_op jit(solution)/shard_map/all_to_all | solution.py:235
  65.7 1.5 %shard_map.93 = f32[32,128]{1,0:T(8,128)} custom-call(s32[2,32]{1,0:T(2,128)S(1)} %bitcast.12, bf16[512,128]{1,0:T(8,128)(2,1)S(1)} %bitcast.8, bf16[2048,128]{1,0:T(8,128)(2,1)S(1)} %get-tuple-element.19.coupling_ref, bf16[2048,128]{1,0:T(8,128)(2,1)S(1)} %get-tuple-element.20.target_ref, f32[32,128]{1,0:T(8,128)S(1)} %shard_map.92.near_ref), custom_call_target="tpu_custom_call" | custom-call | flops 50331648 | bytes 1048576 | tf_op jit(solution)/shard_map/pallas_call | solution.py:197
  (8 shorter events, 0.0 us)
Async XLA Ops:
  0.6 10.0 %collective-permute-start = (bf16[32,128]{1,0:T(8,128)(2,1)}, bf16[32,128]{1,0:T(8,128)(2,1)S(1)}, u32[]{:S(2)}, u32[]{:S(2)}) collective-permute-start(bf16[32,128]{1,0:T(8,128)(2,1)} %charge_hbm.1), channel_id=1, source_target_pairs={{96,0},{128,32},{160,64},{192,96},{224,128},{256,160},{288,192},{3... | collective-permute-start | bytes 24584 | tf_op jit(solution)/shard_map/ppermute | solution.py:210
  10.7 23.4 %copy-start = (s32[32,3]{0,1:T(4,128)S(1)}, s32[32,3]{0,1:T(4,128)}, u32[]{:S(2)}) copy-start(s32[32,3]{0,1:T(4,128)} %param.9) | copy-start | bytes 1156
  10.7 16.2 %collective-permute-start.1 = (bf16[64,128]{1,0:T(8,128)(2,1)S(1)}, bf16[64,128]{1,0:T(8,128)(2,1)S(1)}, u32[]{:S(2)}, u32[]{:S(2)}) collective-permute-start(bf16[64,128]{1,0:T(8,128)(2,1)S(1)} %pad_maximum_fusion), channel_id=1, source_target_pairs={{448,0},{480,32},{0,64},{32,96},{64,128},{96,160},{128,192},{160,2... | collective-permute-start | bytes 49160 | tf_op jit(solution)/shard_map/ppermute | solution.py:210
  13.0 24.7 %all-to-all-start = ((bf16[32,16,128]{2,1,0:T(8,128)(2,1)}), bf16[32,16,128]{2,1,0:T(8,128)(2,1)S(1)}, u32[]{:S(2)}, u32[]{:S(2)}) async-start(bf16[32,16,128]{2,1,0:T(8,128)(2,1)} %get-tuple-element.18), calls=%async_computation | async-start | bytes 262144 | tf_op jit(solution)/shard_map/all_to_all | solution.py:235
  27.0 7.1 %collective-permute-start.2 = (bf16[128,128]{1,0:T(8,128)(2,1)S(1)}, bf16[128,128]{1,0:T(8,128)(2,1)S(1)}, u32[]{:S(2)}, u32[]{:S(2)}) collective-permute-start(bf16[128,128]{1,0:T(8,128)(2,1)S(1)} %constant_dynamic-update-slice_fusion.low_ref), channel_id=1, source_target_pairs={{480,0},{0,32},{32,64},{64,96},{96,128},{128,160},{160,192},{192,2... | collective-permute-start | bytes 98312 | tf_op jit(solution)/shard_map/ppermute | solution.py:210
  28.9 8.8 %copy-start.1 = (s32[32,2]{0,1:T(2,128)S(1)}, s32[32,2]{0,1:T(2,128)}, u32[]{:S(2)}) copy-start(s32[32,2]{0,1:T(2,128)} %param.13) | copy-start | bytes 772
  38.6 7.6 %collective-permute-start.3 = (bf16[32,128]{1,0:T(8,128)(2,1)S(1)}, bf16[32,128]{1,0:T(8,128)(2,1)S(1)}, u32[]{:S(2)}, u32[]{:S(2)}) collective-permute-start(bf16[32,128]{1,0:T(8,128)(2,1)S(1)} %get-tuple-element.25.field_ref), channel_id=1, source_target_pairs={{96,0},{128,32},{160,64},{192,96},{224,128},{256,160},{288,192},{3... | collective-permute-start | bytes 24584 | tf_op jit(solution)/shard_map/ppermute | solution.py:210
  46.2 8.7 %collective-permute-start.4 = (bf16[64,128]{1,0:T(8,128)(2,1)S(1)}, bf16[64,128]{1,0:T(8,128)(2,1)S(1)}, u32[]{:S(2)}, u32[]{:S(2)}) collective-permute-start(bf16[64,128]{1,0:T(8,128)(2,1)S(1)} %pad_maximum_fusion.1), channel_id=1, source_target_pairs={{448,0},{480,32},{0,64},{32,96},{64,128},{96,160},{128,192},{160,2... | collective-permute-start | bytes 49160 | tf_op jit(solution)/shard_map/ppermute | solution.py:210
  48.1 17.6 %all-to-all-start.1 = ((bf16[32,16,128]{2,1,0:T(8,128)(2,1)}), bf16[32,16,128]{2,1,0:T(8,128)(2,1)S(1)}, u32[]{:S(2)}, u32[]{:S(2)}) async-start(bf16[32,16,128]{2,1,0:T(8,128)(2,1)} %shard_map.91), calls=%async_computation.1 | async-start | bytes 262144 | tf_op jit(solution)/shard_map/all_to_all | solution.py:235
  55.0 7.1 %collective-permute-start.5 = (bf16[128,128]{1,0:T(8,128)(2,1)S(1)}, bf16[128,128]{1,0:T(8,128)(2,1)S(1)}, u32[]{:S(2)}, u32[]{:S(2)}) collective-permute-start(bf16[128,128]{1,0:T(8,128)(2,1)S(1)} %constant_dynamic-update-slice_fusion.3.low_ref), channel_id=1, source_target_pairs={{480,0},{0,32},{32,64},{64,96},{96,128},{128,160},{160,192},{192,2... | collective-permute-start | bytes 98312 | tf_op jit(solution)/shard_map/ppermute | solution.py:210

commit v9 on v8

--- a/solution.py
+++ b/solution.py
@@ -67,10 +67,7 @@
     copies_ref[...] = jnp.broadcast_to(packed.astype(BF16)[None], copies_ref.shape)
 
 
-def moments_kernel(field_ref, source_hbm, copies_ref, source_ref, sem):
-    move = pltpu.make_async_copy(source_hbm, source_ref, sem)
-    move.start()
-    move.wait()
+def moments_kernel(field_ref, source_ref, copies_ref):
     send_moments(field_ref[...], source_ref, copies_ref)
 
 
@@ -178,10 +175,14 @@
     return total
 
 
-def middle_kernel(owners, cols_ref, moments_ref, coupling_ref, target_ref, near_ref, potential_ref, second_ref):
+def middle_kernel(owners, cols_ref, moments_ref, coupling_ref, target_ref, near_ref, source_hbm,
+                  potential_ref, second_ref, source_ref, sem):
+    move = pltpu.make_async_copy(source_hbm, source_ref, sem)
+    move.start()
     total = potential(owners, cols_ref, moments_ref, coupling_ref, target_ref, near_ref)
     potential_ref[...] = total
     second_ref[...] = total.astype(BF16)
+    move.wait()
 
 
 def last_kernel(owners, cols_ref, moments_ref, coupling_ref, target_ref, near_ref, potential_ref):
@@ -263,10 +264,11 @@
     own, vals = call(own_kernel, (field32, rest), charge, near_vals, specs=[VMEM, HBM], scratch=own_scratch,
                      flops=32 * tile, moved=3 * tile)
     moments, near = exchange(sent, charge, from_behind(charges, "blk", CHAIN[0]), own, vals)
-    total, second = call(functools.partial(middle_kernel, owners), (pltpu.VMEM(charges.shape, F32), field16),
-                         far_cols, moments, coupling, target, near, flops=48 * tile, moved=tile)
-    sent = call(moments_kernel, copies, second, source, specs=[VMEM, HBM],
-                scratch=[kept, pltpu.SemaphoreType.DMA(())], flops=16 * tile, moved=tile)
+    total, second, source = call(
+        functools.partial(middle_kernel, owners), (pltpu.VMEM(charges.shape, F32), field16, kept),
+        far_cols, moments, coupling, target, near, source, specs=[VMEM] * 5 + [HBM],
+        scratch=[pltpu.SemaphoreType.DMA(())], flops=48 * tile, moved=tile)
+    sent = call(moments_kernel, copies, second, *pinned(pltpu.VMEM, source), flops=16 * tile, moved=tile)
     own, vals, potential_one = call(
         own_store_kernel, (field32, rest, field32), second, near_vals, *pinned(pltpu.VMEM, total),
         specs=[VMEM, HBM, VMEM], scratch=own_scratch, flops=32 * tile, moved=3 * tile)

time: 68 us -> 68.1 us (level)
  starting transfers between devices: 42.9 us -> 44 us
  Pallas kernels: 14.3 us -> 13.4 us
    all_to_all x2, starting transfers between devices: 20.7 us -> 21.8 us  [far_exchange(): lax.all_to_all(copies, 'cluster', 0, 0, tiled=True).reshape(-1, 2 * rank)]
    pallas_call x8, Pallas kernels: 14.3 us -> 13.4 us  [call(): pl.pallas_call(kernel, out_shape=outs, in_specs=specs or [VMEM] * len(ope...]
  transfers between devices with their start and end apart: 8 -> 8, of which waited for: 4 -> 4; matrix products, arithmetic and copies ran while one was open for 0% -> 0% of each run, Pallas kernels for 18% -> 16%
where the time goes in v9:
time: 68.1 us; the launch traced here: 67.4 us
  starting transfers between devices  44 us (65%)
  Pallas kernels  13.4 us (20%)
  waiting for transfers between devices  9.12 us (13%)
  between operations  0.81 us (1%)
    ppermute x6, starting transfers between devices, from_behind(): lax.ppermute(block, axis, [((i - distance) % size, i) for i in range(size)])  22.2 us
    all_to_all x2, starting transfers between devices, far_exchange(): lax.all_to_all(copies, 'cluster', 0, 0, tiled=True).reshape(-1, 2 * rank)  21.8 us
    pallas_call x8, Pallas kernels, call(): pl.pallas_call(kernel, out_shape=outs, in_specs=specs or [VMEM] * len(ope...  13.4 us
    all_to_all x2, waiting for transfers between devices, far_exchange(): lax.all_to_all(copies, 'cluster', 0, 0, tiled=True).reshape(-1, 2 * rank)  5.39 us
    ppermute x6, waiting for transfers between devices, from_behind(): lax.ppermute(block, axis, [((i - distance) % size, i) for i in range(size)])  3.74 us
  transfers between devices with their start and end apart: 8, of which 4 were waited for; matrix products, arithmetic and copies ran while one was open for 0% of the time, Pallas kernels for 16%

profile of v9, /device:TPU:1, one launch (start us, length us, event | category | flops | bytes accessed | tf_op | source)
XLA Modules:
  0.0 67.4 jit_solution(13593661626680504595)
XLA Ops:
  0.6 7.6 %collective-permute-start = (bf16[32,128]{1,0:T(8,128)(2,1)}, bf16[32,128]{1,0:T(8,128)(2,1)S(1)}, u32[]{:S(2)}, u32[]{:S(2)}) collective-permute-start(bf16[32,128]{1,0:T(8,128)(2,1)} %charge_hbm.1), channel_id=1, source_target_pairs={{96,0},{128,32},{160,64},{192,96},{224,128},{256,160},{288,192},{3... | collective-permute-start | bytes 24584 | tf_op jit(solution)/shard_map/ppermute | solution.py:211
  8.3 2.4 %shard_map.86 = (bf16[32,16,128]{2,1,0:T(8,128)(2,1)}, bf16[32,128]{1,0:T(8,128)(2,1)S(1)}, bf16[2048,128]{1,0:T(8,128)(2,1)S(1)}, bf16[2048,128]{1,0:T(8,128)(2,1)S(1)}) custom-call(bf16[32,128]{1,0:T(8,128)(2,1)} %charge_hbm.1, bf16[2048,128]{1,0:T(8,128)(2,1)} %bitcast.13, bf16[2048,128]{1,0:T(8,128)(2,1)} %bitcast.15, bf16[32,2,64,64]{3,2,1,0:T(8,128)(2,1)} %coupling_hbm.1), custom_call_target="tpu_custom_call" | custom-call | flops 16777216 | bytes 2097152 | tf_op jit(solution)/shard_map/pallas_call | solution.py:198
  10.7 0.0 copy-start
  10.7 0.0 collective-permute-done
  10.7 2.3 %collective-permute-start.1 = (bf16[64,128]{1,0:T(8,128)(2,1)S(1)}, bf16[64,128]{1,0:T(8,128)(2,1)S(1)}, u32[]{:S(2)}, u32[]{:S(2)}) collective-permute-start(bf16[64,128]{1,0:T(8,128)(2,1)S(1)} %pad_maximum_fusion), channel_id=1, source_target_pairs={{448,0},{480,32},{0,64},{32,96},{64,128},{96,160},{128,192},{160,2... | collective-permute-start | bytes 49160 | tf_op jit(solution)/shard_map/ppermute | solution.py:211
  13.0 13.9 %all-to-all-start = ((bf16[32,16,128]{2,1,0:T(8,128)(2,1)}), bf16[32,16,128]{2,1,0:T(8,128)(2,1)S(1)}, u32[]{:S(2)}, u32[]{:S(2)}) async-start(bf16[32,16,128]{2,1,0:T(8,128)(2,1)} %get-tuple-element.19), calls=%async_computation | async-start | bytes 262144 | tf_op jit(solution)/shard_map/all_to_all | solution.py:236
  26.9 0.0 collective-permute-done.1
  27.0 1.9 %collective-permute-start.2 = (bf16[128,128]{1,0:T(8,128)(2,1)S(1)}, bf16[128,128]{1,0:T(8,128)(2,1)S(1)}, u32[]{:S(2)}, u32[]{:S(2)}) collective-permute-start(bf16[128,128]{1,0:T(8,128)(2,1)S(1)} %constant_dynamic-update-slice_fusion.low_ref), channel_id=1, source_target_pairs={{480,0},{0,32},{32,64},{64,96},{96,128},{128,160},{160,192},{192,2... | collective-permute-start | bytes 98312 | tf_op jit(solution)/shard_map/ppermute | solution.py:211
  28.9 0.0 copy-start.1
  28.9 2.4 %shard_map.87 = (f32[32,128]{1,0:T(8,128)S(1)}, bf16[32,2,128,128]{3,2,1,0:T(8,128)(2,1)S(1)}) custom-call(bf16[32,128]{1,0:T(8,128)(2,1)S(1)} %get-tuple-element.23.field_ref, bf16[32,3,128,128]{3,2,1,0:T(8,128)(2,1)} %vals_hbm.3), custom_call_target="tpu_custom_call" | custom-call | flops 33554432 | bytes 3145728 | tf_op jit(solution)/shard_map/pallas_call | solution.py:198
  31.3 2.7 %collective-permute-done.2.high_ref = bf16[128,128]{1,0:T(8,128)(2,1)S(1)} collective-permute-done((bf16[128,128]{1,0:T(8,128)(2,1)S(1)}, bf16[128,128]{1,0:T(8,128)(2,1)S(1)}, u32[]{:S(2)}, u32[]{:S(2)}) %collective-permute-start.2) | collective-permute-done | bytes 32800 | tf_op jit(solution)/shard_map/ppermute | solution.py:211
  34.0 0.0 copy-done
  34.0 1.0 %shard_map.88.near_ref = f32[32,128]{1,0:T(8,128)S(1)} custom-call(s32[1]{0:T(128)} %bitcast.4.pos_ref, s32[3,32]{1,0:T(4,128)S(1)} %bitcast.9, bf16[128,128]{1,0:T(8,128)(2,1)S(1)} %constant_dynamic-update-slice_fusion.low_ref, bf16[128,128]{1,0:T(8,128)(2,1)S(1)} %collective-permute-done.2.high_ref, ...), custom_call_target="tpu_custom_call" | custom-call | flops 67108864 | bytes 2097152 | tf_op jit(solution)/shard_map/pallas_call | solution.py:198
  35.0 2.7 %all-to-all-done = bf16[32,16,128]{2,1,0:T(8,128)(2,1)S(1)} async-done(((bf16[32,16,128]{2,1,0:T(8,128)(2,1)}), bf16[32,16,128]{2,1,0:T(8,128)(2,1)S(1)}, u32[]{:S(2)}, u32[]{:S(2)}) %all-to-all-start) | async-done | bytes 131104 | tf_op jit(solution)/shard_map/all_to_all | solution.py:236
  37.7 0.0 copy-done.1
  37.7 1.1 %shard_map.89 = (f32[32,128]{1,0:T(8,128)S(1)}, bf16[32,128]{1,0:T(8,128)(2,1)S(1)}, bf16[2048,128]{1,0:T(8,128)(2,1)S(1)}) custom-call(s32[2,32]{1,0:T(2,128)S(1)} %bitcast.11, bf16[512,128]{1,0:T(8,128)(2,1)S(1)} %bitcast.7, bf16[2048,128]{1,0:T(8,128)(2,1)S(1)} %get-tuple-element.20.coupling_ref, bf16[2048,128]{1,0:T(8,128)(2,1)S(1)} %get-tuple-element.21.target_ref, ...), custom_call_target="tpu_custom_call" | custom-call | flops 50331648 | bytes 1048576 | tf_op jit(solution)/shard_map/pallas_call | solution.py:198
  38.7 5.4 %collective-permute-start.3 = (bf16[32,128]{1,0:T(8,128)(2,1)S(1)}, bf16[32,128]{1,0:T(8,128)(2,1)S(1)}, u32[]{:S(2)}, u32[]{:S(2)}) collective-permute-start(bf16[32,128]{1,0:T(8,128)(2,1)S(1)} %get-tuple-element.26.field_ref), channel_id=1, source_target_pairs={{96,0},{128,32},{160,64},{192,96},{224,128},{256,160},{288,192},{3... | collective-permute-start | bytes 24584 | tf_op jit(solution)/shard_map/ppermute | solution.py:211
  44.2 1.1 %shard_map.91 = bf16[32,16,128]{2,1,0:T(8,128)(2,1)} custom-call(bf16[32,128]{1,0:T(8,128)(2,1)S(1)} %get-tuple-element.26.field_ref, bf16[2048,128]{1,0:T(8,128)(2,1)S(1)} %get-tuple-element.29.source_ref), custom_call_target="tpu_custom_call" | custom-call | flops 16777216 | bytes 1048576 | tf_op jit(solution)/shard_map/pallas_call | solution.py:198
  45.3 0.0 collective-permute-done.3
  45.3 1.9 %collective-permute-start.4 = (bf16[64,128]{1,0:T(8,128)(2,1)S(1)}, bf16[64,128]{1,0:T(8,128)(2,1)S(1)}, u32[]{:S(2)}, u32[]{:S(2)}) collective-permute-start(bf16[64,128]{1,0:T(8,128)(2,1)S(1)} %pad_maximum_fusion.1), channel_id=1, source_target_pairs={{448,0},{480,32},{0,64},{32,96},{64,128},{96,160},{128,192},{160,2... | collective-permute-start | bytes 49160 | tf_op jit(solution)/shard_map/ppermute | solution.py:211
  47.2 7.9 %all-to-all-start.1 = ((bf16[32,16,128]{2,1,0:T(8,128)(2,1)}), bf16[32,16,128]{2,1,0:T(8,128)(2,1)S(1)}, u32[]{:S(2)}, u32[]{:S(2)}) async-start(bf16[32,16,128]{2,1,0:T(8,128)(2,1)} %shard_map.91), calls=%async_computation.1 | async-start | bytes 262144 | tf_op jit(solution)/shard_map/all_to_all | solution.py:236
  55.1 0.0 collective-permute-done.4
  55.1 3.0 %collective-permute-start.5 = (bf16[128,128]{1,0:T(8,128)(2,1)S(1)}, bf16[128,128]{1,0:T(8,128)(2,1)S(1)}, u32[]{:S(2)}, u32[]{:S(2)}) collective-permute-start(bf16[128,128]{1,0:T(8,128)(2,1)S(1)} %constant_dynamic-update-slice_fusion.3.low_ref), channel_id=1, source_target_pairs={{480,0},{0,32},{32,64},{64,96},{96,128},{128,160},{160,192},{192,2... | collective-permute-start | bytes 98312 | tf_op jit(solution)/shard_map/ppermute | solution.py:211
  58.1 3.0 %shard_map.90 = (f32[32,128]{1,0:T(8,128)S(1)}, bf16[32,2,128,128]{3,2,1,0:T(8,128)(2,1)S(1)}, f32[32,128]{1,0:T(8,128)}) custom-call(bf16[32,128]{1,0:T(8,128)(2,1)S(1)} %get-tuple-element.26.field_ref, bf16[32,3,128,128]{3,2,1,0:T(8,128)(2,1)} %vals_hbm.3, f32[32,128]{1,0:T(8,128)S(1)} %get-tuple-element.27.kept_ref), custom_call_target="tpu_custom_call" | custom-call | flops 33554432 | bytes 3145728 | tf_op jit(solution)/shard_map/pallas_call | solution.py:198
  61.2 1.0 %collective-permute-done.5.high_ref = bf16[128,128]{1,0:T(8,128)(2,1)S(1)} collective-permute-done((bf16[128,128]{1,0:T(8,128)(2,1)S(1)}, bf16[128,128]{1,0:T(8,128)(2,1)S(1)}, u32[]{:S(2)}, u32[]{:S(2)}) %collective-permute-start.5) | collective-permute-done | bytes 32800 | tf_op jit(solution)/shard_map/ppermute | solution.py:211
  62.2 1.0 %shard_map.92.near_ref = f32[32,128]{1,0:T(8,128)S(1)} custom-call(s32[1]{0:T(128)} %bitcast.4.pos_ref, s32[3,32]{1,0:T(4,128)S(1)} %bitcast.10, bf16[128,128]{1,0:T(8,128)(2,1)S(1)} %constant_dynamic-update-slice_fusion.3.low_ref, bf16[128,128]{1,0:T(8,128)(2,1)S(1)} %collective-permute-done.5.high_ref, ...), custom_call_target="tpu_custom_call" | custom-call | flops 67108864 | bytes 2097152 | tf_op jit(solution)/shard_map/pallas_call | solution.py:198
  63.1 2.7 %all-to-all-done.1 = bf16[32,16,128]{2,1,0:T(8,128)(2,1)S(1)} async-done(((bf16[32,16,128]{2,1,0:T(8,128)(2,1)}), bf16[32,16,128]{2,1,0:T(8,128)(2,1)S(1)}, u32[]{:S(2)}, u32[]{:S(2)}) %all-to-all-start.1) | async-done | bytes 131104 | tf_op jit(solution)/shard_map/all_to_all | solution.py:236
  65.8 1.5 %shard_map.93 = f32[32,128]{1,0:T(8,128)} custom-call(s32[2,32]{1,0:T(2,128)S(1)} %bitcast.12, bf16[512,128]{1,0:T(8,128)(2,1)S(1)} %bitcast.8, bf16[2048,128]{1,0:T(8,128)(2,1)S(1)} %get-tuple-element.20.coupling_ref, bf16[2048,128]{1,0:T(8,128)(2,1)S(1)} %get-tuple-element.21.target_ref, f32[32,128]{1,0:T(8,128)S(1)} %shard_map.92.near_ref), custom_call_target="tpu_custom_call" | custom-call | flops 50331648 | bytes 1048576 | tf_op jit(solution)/shard_map/pallas_call | solution.py:198
  (8 shorter events, 0.0 us)
Async XLA Ops:
  0.6 10.0 %collective-permute-start = (bf16[32,128]{1,0:T(8,128)(2,1)}, bf16[32,128]{1,0:T(8,128)(2,1)S(1)}, u32[]{:S(2)}, u32[]{:S(2)}) collective-permute-start(bf16[32,128]{1,0:T(8,128)(2,1)} %charge_hbm.1), channel_id=1, source_target_pairs={{96,0},{128,32},{160,64},{192,96},{224,128},{256,160},{288,192},{3... | collective-permute-start | bytes 24584 | tf_op jit(solution)/shard_map/ppermute | solution.py:211
  10.7 23.4 %copy-start = (s32[32,3]{0,1:T(4,128)S(1)}, s32[32,3]{0,1:T(4,128)}, u32[]{:S(2)}) copy-start(s32[32,3]{0,1:T(4,128)} %param.9) | copy-start | bytes 1156
  10.7 16.2 %collective-permute-start.1 = (bf16[64,128]{1,0:T(8,128)(2,1)S(1)}, bf16[64,128]{1,0:T(8,128)(2,1)S(1)}, u32[]{:S(2)}, u32[]{:S(2)}) collective-permute-start(bf16[64,128]{1,0:T(8,128)(2,1)S(1)} %pad_maximum_fusion), channel_id=1, source_target_pairs={{448,0},{480,32},{0,64},{32,96},{64,128},{96,160},{128,192},{160,2... | collective-permute-start | bytes 49160 | tf_op jit(solution)/shard_map/ppermute | solution.py:211
  13.0 24.7 %all-to-all-start = ((bf16[32,16,128]{2,1,0:T(8,128)(2,1)}), bf16[32,16,128]{2,1,0:T(8,128)(2,1)S(1)}, u32[]{:S(2)}, u32[]{:S(2)}) async-start(bf16[32,16,128]{2,1,0:T(8,128)(2,1)} %get-tuple-element.19), calls=%async_computation | async-start | bytes 262144 | tf_op jit(solution)/shard_map/all_to_all | solution.py:236
  27.0 7.1 %collective-permute-start.2 = (bf16[128,128]{1,0:T(8,128)(2,1)S(1)}, bf16[128,128]{1,0:T(8,128)(2,1)S(1)}, u32[]{:S(2)}, u32[]{:S(2)}) collective-permute-start(bf16[128,128]{1,0:T(8,128)(2,1)S(1)} %constant_dynamic-update-slice_fusion.low_ref), channel_id=1, source_target_pairs={{480,0},{0,32},{32,64},{64,96},{96,128},{128,160},{160,192},{192,2... | collective-permute-start | bytes 98312 | tf_op jit(solution)/shard_map/ppermute | solution.py:211
  28.9 8.8 %copy-start.1 = (s32[32,2]{0,1:T(2,128)S(1)}, s32[32,2]{0,1:T(2,128)}, u32[]{:S(2)}) copy-start(s32[32,2]{0,1:T(2,128)} %param.13) | copy-start | bytes 772
  38.7 6.5 %collective-permute-start.3 = (bf16[32,128]{1,0:T(8,128)(2,1)S(1)}, bf16[32,128]{1,0:T(8,128)(2,1)S(1)}, u32[]{:S(2)}, u32[]{:S(2)}) collective-permute-start(bf16[32,128]{1,0:T(8,128)(2,1)S(1)} %get-tuple-element.26.field_ref), channel_id=1, source_target_pairs={{96,0},{128,32},{160,64},{192,96},{224,128},{256,160},{288,192},{3... | collective-permute-start | bytes 24584 | tf_op jit(solution)/shard_map/ppermute | solution.py:211
  45.3 9.8 %collective-permute-start.4 = (bf16[64,128]{1,0:T(8,128)(2,1)S(1)}, bf16[64,128]{1,0:T(8,128)(2,1)S(1)}, u32[]{:S(2)}, u32[]{:S(2)}) collective-permute-start(bf16[64,128]{1,0:T(8,128)(2,1)S(1)} %pad_maximum_fusion.1), channel_id=1, source_target_pairs={{448,0},{480,32},{0,64},{32,96},{64,128},{96,160},{128,192},{160,2... | collective-permute-start | bytes 49160 | tf_op jit(solution)/shard_map/ppermute | solution.py:211
  47.2 18.7 %all-to-all-start.1 = ((bf16[32,16,128]{2,1,0:T(8,128)(2,1)}), bf16[32,16,128]{2,1,0:T(8,128)(2,1)S(1)}, u32[]{:S(2)}, u32[]{:S(2)}) async-start(bf16[32,16,128]{2,1,0:T(8,128)(2,1)} %shard_map.91), calls=%async_computation.1 | async-start | bytes 262144 | tf_op jit(solution)/shard_map/all_to_all | solution.py:236
  55.1 7.1 %collective-permute-start.5 = (bf16[128,128]{1,0:T(8,128)(2,1)S(1)}, bf16[128,128]{1,0:T(8,128)(2,1)S(1)}, u32[]{:S(2)}, u32[]{:S(2)}) collective-permute-start(bf16[128,128]{1,0:T(8,128)(2,1)S(1)} %constant_dynamic-update-slice_fusion.3.low_ref), channel_id=1, source_target_pairs={{480,0},{0,32},{32,64},{64,96},{96,128},{128,160},{160,192},{192,2... | collective-permute-start | bytes 98312 | tf_op jit(solution)/shard_map/ppermute | solution.py:211

commit v10 on v8

--- a/solution.py
+++ b/solution.py
@@ -13,7 +13,7 @@
 NN = (((1,), (0,)), ((), ()))
 CHUNK = 4
 LANES = 128
-CHAIN = (-3, 2, 1)
+CHAIN = (2, -3, 1)
 
 
 def mul(a, b, dims):

time: 68 us -> 68.7 us (1.010)
  waiting for transfers between devices: 9.12 us -> 10.9 us
  starting transfers between devices: 42.9 us -> 42.2 us
    ppermute x6, starting transfers between devices: 22.2 us -> 18.7 us  [from_behind(): lax.ppermute(block, axis, [((i - distance) % size, i) for i in range(size)])]
    all_to_all x2, starting transfers between devices: 20.7 us -> 23.4 us  [far_exchange(): lax.all_to_all(copies, 'cluster', 0, 0, tiled=True).reshape(-1, 2 * rank)]
    ppermute x6, waiting for transfers between devices: 3.74 us -> 5.56 us  [from_behind(): lax.ppermute(block, axis, [((i - distance) % size, i) for i in range(size)])]
  transfers between devices with their start and end apart: 8 -> 8, of which waited for: 4 -> 6; matrix products, arithmetic and copies ran while one was open for 0% -> 0% of each run, Pallas kernels for 18% -> 17%
where the time goes in v10:
time: 68.7 us; the launch traced here: 68.2 us
  starting transfers between devices  42.2 us (61%)
  Pallas kernels  14.3 us (21%)
  waiting for transfers between devices  10.9 us (16%)
  between operations  0.8 us (1%)
    all_to_all x2, starting transfers between devices, far_exchange(): lax.all_to_all(copies, 'cluster', 0, 0, tiled=True).reshape(-1, 2 * rank)  23.4 us
    ppermute x6, starting transfers between devices, from_behind(): lax.ppermute(block, axis, [((i - distance) % size, i) for i in range(size)])  18.7 us
    pallas_call x8, Pallas kernels, call(): pl.pallas_call(kernel, out_shape=outs, in_specs=specs or [VMEM] * len(ope...  14.3 us
    ppermute x6, waiting for transfers between devices, from_behind(): lax.ppermute(block, axis, [((i - distance) % size, i) for i in range(size)])  5.56 us
    all_to_all x2, waiting for transfers between devices, far_exchange(): lax.all_to_all(copies, 'cluster', 0, 0, tiled=True).reshape(-1, 2 * rank)  5.38 us
  transfers between devices with their start and end apart: 8, of which 6 were waited for; matrix products, arithmetic and copies ran while one was open for 0% of the time, Pallas kernels for 17%

profile of v10, /device:TPU:1, one launch (start us, length us, event | category | flops | bytes accessed | tf_op | source)
XLA Modules:
  0.0 68.2 jit_solution(15149242140412646619)
XLA Ops:
  0.6 4.0 %collective-permute-start = (bf16[32,128]{1,0:T(8,128)(2,1)}, bf16[32,128]{1,0:T(8,128)(2,1)S(1)}, u32[]{:S(2)}, u32[]{:S(2)}) collective-permute-start(bf16[32,128]{1,0:T(8,128)(2,1)} %charge_hbm.1), channel_id=1, source_target_pairs={{448,0},{480,32},{0,64},{32,96},{64,128},{96,160},{128,192},{160,2... | collective-permute-start | bytes 24584 | tf_op jit(solution)/shard_map/ppermute | solution.py:210
  4.7 2.4 %shard_map.86 = (bf16[32,16,128]{2,1,0:T(8,128)(2,1)}, bf16[32,128]{1,0:T(8,128)(2,1)S(1)}, bf16[2048,128]{1,0:T(8,128)(2,1)S(1)}, bf16[2048,128]{1,0:T(8,128)(2,1)S(1)}) custom-call(bf16[32,128]{1,0:T(8,128)(2,1)} %charge_hbm.1, bf16[2048,128]{1,0:T(8,128)(2,1)} %bitcast.13, bf16[2048,128]{1,0:T(8,128)(2,1)} %bitcast.15, bf16[32,2,64,64]{3,2,1,0:T(8,128)(2,1)} %coupling_hbm.1), custom_call_target="tpu_custom_call" | custom-call | flops 16777216 | bytes 2097152 | tf_op jit(solution)/shard_map/pallas_call | solution.py:197
  7.1 0.0 copy-start
  7.1 0.7 %collective-permute-done = bf16[32,128]{1,0:T(8,128)(2,1)S(1)} collective-permute-done((bf16[32,128]{1,0:T(8,128)(2,1)}, bf16[32,128]{1,0:T(8,128)(2,1)S(1)}, u32[]{:S(2)}, u32[]{:S(2)}) %collective-permute-start) | collective-permute-done | bytes 8224 | tf_op jit(solution)/shard_map/ppermute | solution.py:210
  7.8 5.2 %collective-permute-start.1 = (bf16[64,128]{1,0:T(8,128)(2,1)S(1)}, bf16[64,128]{1,0:T(8,128)(2,1)S(1)}, u32[]{:S(2)}, u32[]{:S(2)}) collective-permute-start(bf16[64,128]{1,0:T(8,128)(2,1)S(1)} %pad_maximum_fusion), channel_id=1, source_target_pairs={{96,0},{128,32},{160,64},{192,96},{224,128},{256,160},{288,192},{3... | collective-permute-start | bytes 49160 | tf_op jit(solution)/shard_map/ppermute | solution.py:210
  13.0 14.6 %all-to-all-start = ((bf16[32,16,128]{2,1,0:T(8,128)(2,1)}), bf16[32,16,128]{2,1,0:T(8,128)(2,1)S(1)}, u32[]{:S(2)}, u32[]{:S(2)}) async-start(bf16[32,16,128]{2,1,0:T(8,128)(2,1)} %get-tuple-element.18), calls=%async_computation | async-start | bytes 262144 | tf_op jit(solution)/shard_map/all_to_all | solution.py:235
  27.6 0.0 collective-permute-done.1
  27.7 1.9 %collective-permute-start.2 = (bf16[128,128]{1,0:T(8,128)(2,1)S(1)}, bf16[128,128]{1,0:T(8,128)(2,1)S(1)}, u32[]{:S(2)}, u32[]{:S(2)}) collective-permute-start(bf16[128,128]{1,0:T(8,128)(2,1)S(1)} %constant_dynamic-update-slice_fusion.low_ref), channel_id=1, source_target_pairs={{480,0},{0,32},{32,64},{64,96},{96,128},{128,160},{160,192},{192,2... | collective-permute-start | bytes 98312 | tf_op jit(solution)/shard_map/ppermute | solution.py:210
  29.6 0.0 copy-start.1
  29.6 2.4 %shard_map.87 = (f32[32,128]{1,0:T(8,128)S(1)}, bf16[32,2,128,128]{3,2,1,0:T(8,128)(2,1)S(1)}) custom-call(bf16[32,128]{1,0:T(8,128)(2,1)S(1)} %get-tuple-element.22.field_ref, bf16[32,3,128,128]{3,2,1,0:T(8,128)(2,1)} %vals_hbm.3), custom_call_target="tpu_custom_call" | custom-call | flops 33554432 | bytes 3145728 | tf_op jit(solution)/shard_map/pallas_call | solution.py:197
  32.1 2.7 %collective-permute-done.2.high_ref = bf16[128,128]{1,0:T(8,128)(2,1)S(1)} collective-permute-done((bf16[128,128]{1,0:T(8,128)(2,1)S(1)}, bf16[128,128]{1,0:T(8,128)(2,1)S(1)}, u32[]{:S(2)}, u32[]{:S(2)}) %collective-permute-start.2) | collective-permute-done | bytes 32800 | tf_op jit(solution)/shard_map/ppermute | solution.py:210
  34.7 0.0 copy-done
  34.7 1.0 %shard_map.88.near_ref = f32[32,128]{1,0:T(8,128)S(1)} custom-call(s32[1]{0:T(128)} %bitcast.4.pos_ref, s32[3,32]{1,0:T(4,128)S(1)} %bitcast.9, bf16[128,128]{1,0:T(8,128)(2,1)S(1)} %constant_dynamic-update-slice_fusion.low_ref, bf16[128,128]{1,0:T(8,128)(2,1)S(1)} %collective-permute-done.2.high_ref, ...), custom_call_target="tpu_custom_call" | custom-call | flops 67108864 | bytes 2097152 | tf_op jit(solution)/shard_map/pallas_call | solution.py:197
  35.7 2.7 %all-to-all-done = bf16[32,16,128]{2,1,0:T(8,128)(2,1)S(1)} async-done(((bf16[32,16,128]{2,1,0:T(8,128)(2,1)}), bf16[32,16,128]{2,1,0:T(8,128)(2,1)S(1)}, u32[]{:S(2)}, u32[]{:S(2)}) %all-to-all-start) | async-done | bytes 131104 | tf_op jit(solution)/shard_map/all_to_all | solution.py:235
  38.4 0.0 copy-done.1
  38.4 0.9 %shard_map.89 = (f32[32,128]{1,0:T(8,128)S(1)}, bf16[32,128]{1,0:T(8,128)(2,1)S(1)}) custom-call(s32[2,32]{1,0:T(2,128)S(1)} %bitcast.11, bf16[512,128]{1,0:T(8,128)(2,1)S(1)} %bitcast.7, bf16[2048,128]{1,0:T(8,128)(2,1)S(1)} %get-tuple-element.19.coupling_ref, bf16[2048,128]{1,0:T(8,128)(2,1)S(1)} %get-tuple-element.20.target_ref, ...), custom_call_target="tpu_custom_call" | custom-call | flops 50331648 | bytes 1048576 | tf_op jit(solution)/shard_map/pallas_call | solution.py:197
  39.3 2.3 %collective-permute-start.3 = (bf16[32,128]{1,0:T(8,128)(2,1)S(1)}, bf16[32,128]{1,0:T(8,128)(2,1)S(1)}, u32[]{:S(2)}, u32[]{:S(2)}) collective-permute-start(bf16[32,128]{1,0:T(8,128)(2,1)S(1)} %get-tuple-element.25.field_ref), channel_id=1, source_target_pairs={{448,0},{480,32},{0,64},{32,96},{64,128},{96,160},{128,192},{160,2... | collective-permute-start | bytes 24584 | tf_op jit(solution)/shard_map/ppermute | solution.py:210
  41.6 2.1 %shard_map.91 = bf16[32,16,128]{2,1,0:T(8,128)(2,1)} custom-call(bf16[32,128]{1,0:T(8,128)(2,1)S(1)} %get-tuple-element.25.field_ref, bf16[2048,128]{1,0:T(8,128)(2,1)} %bitcast.14), custom_call_target="tpu_custom_call" | custom-call | flops 16777216 | bytes 1048576 | tf_op jit(solution)/shard_map/pallas_call | solution.py:197
  43.8 1.1 %collective-permute-done.3 = bf16[32,128]{1,0:T(8,128)(2,1)S(1)} collective-permute-done((bf16[32,128]{1,0:T(8,128)(2,1)S(1)}, bf16[32,128]{1,0:T(8,128)(2,1)S(1)}, u32[]{:S(2)}, u32[]{:S(2)}) %collective-permute-start.3) | collective-permute-done | bytes 8224 | tf_op jit(solution)/shard_map/ppermute | solution.py:210
  44.9 2.2 %collective-permute-start.4 = (bf16[64,128]{1,0:T(8,128)(2,1)S(1)}, bf16[64,128]{1,0:T(8,128)(2,1)S(1)}, u32[]{:S(2)}, u32[]{:S(2)}) collective-permute-start(bf16[64,128]{1,0:T(8,128)(2,1)S(1)} %pad_maximum_fusion.1), channel_id=1, source_target_pairs={{96,0},{128,32},{160,64},{192,96},{224,128},{256,160},{288,192},{3... | collective-permute-start | bytes 49160 | tf_op jit(solution)/shard_map/ppermute | solution.py:210
  47.2 8.8 %all-to-all-start.1 = ((bf16[32,16,128]{2,1,0:T(8,128)(2,1)}), bf16[32,16,128]{2,1,0:T(8,128)(2,1)S(1)}, u32[]{:S(2)}, u32[]{:S(2)}) async-start(bf16[32,16,128]{2,1,0:T(8,128)(2,1)} %shard_map.91), calls=%async_computation.1 | async-start | bytes 262144 | tf_op jit(solution)/shard_map/all_to_all | solution.py:235
  56.0 0.0 collective-permute-done.4
  56.0 3.0 %collective-permute-start.5 = (bf16[128,128]{1,0:T(8,128)(2,1)S(1)}, bf16[128,128]{1,0:T(8,128)(2,1)S(1)}, u32[]{:S(2)}, u32[]{:S(2)}) collective-permute-start(bf16[128,128]{1,0:T(8,128)(2,1)S(1)} %constant_dynamic-update-slice_fusion.3.low_ref), channel_id=1, source_target_pairs={{480,0},{0,32},{32,64},{64,96},{96,128},{128,160},{160,192},{192,2... | collective-permute-start | bytes 98312 | tf_op jit(solution)/shard_map/ppermute | solution.py:210
  59.1 3.0 %shard_map.90 = (f32[32,128]{1,0:T(8,128)S(1)}, bf16[32,2,128,128]{3,2,1,0:T(8,128)(2,1)S(1)}, f32[32,128]{1,0:T(8,128)}) custom-call(bf16[32,128]{1,0:T(8,128)(2,1)S(1)} %get-tuple-element.25.field_ref, bf16[32,3,128,128]{3,2,1,0:T(8,128)(2,1)} %vals_hbm.3, f32[32,128]{1,0:T(8,128)S(1)} %get-tuple-element.26.kept_ref), custom_call_target="tpu_custom_call" | custom-call | flops 33554432 | bytes 3145728 | tf_op jit(solution)/shard_map/pallas_call | solution.py:197
  62.1 1.0 %collective-permute-done.5.high_ref = bf16[128,128]{1,0:T(8,128)(2,1)S(1)} collective-permute-done((bf16[128,128]{1,0:T(8,128)(2,1)S(1)}, bf16[128,128]{1,0:T(8,128)(2,1)S(1)}, u32[]{:S(2)}, u32[]{:S(2)}) %collective-permute-start.5) | collective-permute-done | bytes 32800 | tf_op jit(solution)/shard_map/ppermute | solution.py:210
  63.1 1.0 %shard_map.92.near_ref = f32[32,128]{1,0:T(8,128)S(1)} custom-call(s32[1]{0:T(128)} %bitcast.4.pos_ref, s32[3,32]{1,0:T(4,128)S(1)} %bitcast.10, bf16[128,128]{1,0:T(8,128)(2,1)S(1)} %constant_dynamic-update-slice_fusion.3.low_ref, bf16[128,128]{1,0:T(8,128)(2,1)S(1)} %collective-permute-done.5.high_ref, ...), custom_call_target="tpu_custom_call" | custom-call | flops 67108864 | bytes 2097152 | tf_op jit(solution)/shard_map/pallas_call | solution.py:197
  64.0 2.7 %all-to-all-done.1 = bf16[32,16,128]{2,1,0:T(8,128)(2,1)S(1)} async-done(((bf16[32,16,128]{2,1,0:T(8,128)(2,1)}), bf16[32,16,128]{2,1,0:T(8,128)(2,1)S(1)}, u32[]{:S(2)}, u32[]{:S(2)}) %all-to-all-start.1) | async-done | bytes 131104 | tf_op jit(solution)/shard_map/all_to_all | solution.py:235
  66.7 1.5 %shard_map.93 = f32[32,128]{1,0:T(8,128)} custom-call(s32[2,32]{1,0:T(2,128)S(1)} %bitcast.12, bf16[512,128]{1,0:T(8,128)(2,1)S(1)} %bitcast.8, bf16[2048,128]{1,0:T(8,128)(2,1)S(1)} %get-tuple-element.19.coupling_ref, bf16[2048,128]{1,0:T(8,128)(2,1)S(1)} %get-tuple-element.20.target_ref, f32[32,128]{1,0:T(8,128)S(1)} %shard_map.92.near_ref), custom_call_target="tpu_custom_call" | custom-call | flops 50331648 | bytes 1048576 | tf_op jit(solution)/shard_map/pallas_call | solution.py:197
  (8 shorter events, 0.0 us)
Async XLA Ops:
  0.6 7.2 %collective-permute-start = (bf16[32,128]{1,0:T(8,128)(2,1)}, bf16[32,128]{1,0:T(8,128)(2,1)S(1)}, u32[]{:S(2)}, u32[]{:S(2)}) collective-permute-start(bf16[32,128]{1,0:T(8,128)(2,1)} %charge_hbm.1), channel_id=1, source_target_pairs={{448,0},{480,32},{0,64},{32,96},{64,128},{96,160},{128,192},{160,2... | collective-permute-start | bytes 24584 | tf_op jit(solution)/shard_map/ppermute | solution.py:210
  7.1 27.7 %copy-start = (s32[32,3]{0,1:T(4,128)S(1)}, s32[32,3]{0,1:T(4,128)}, u32[]{:S(2)}) copy-start(s32[32,3]{0,1:T(4,128)} %param.9) | copy-start | bytes 1156
  7.8 19.8 %collective-permute-start.1 = (bf16[64,128]{1,0:T(8,128)(2,1)S(1)}, bf16[64,128]{1,0:T(8,128)(2,1)S(1)}, u32[]{:S(2)}, u32[]{:S(2)}) collective-permute-start(bf16[64,128]{1,0:T(8,128)(2,1)S(1)} %pad_maximum_fusion), channel_id=1, source_target_pairs={{96,0},{128,32},{160,64},{192,96},{224,128},{256,160},{288,192},{3... | collective-permute-start | bytes 49160 | tf_op jit(solution)/shard_map/ppermute | solution.py:210
  13.0 25.4 %all-to-all-start = ((bf16[32,16,128]{2,1,0:T(8,128)(2,1)}), bf16[32,16,128]{2,1,0:T(8,128)(2,1)S(1)}, u32[]{:S(2)}, u32[]{:S(2)}) async-start(bf16[32,16,128]{2,1,0:T(8,128)(2,1)} %get-tuple-element.18), calls=%async_computation | async-start | bytes 262144 | tf_op jit(solution)/shard_map/all_to_all | solution.py:235
  27.7 7.1 %collective-permute-start.2 = (bf16[128,128]{1,0:T(8,128)(2,1)S(1)}, bf16[128,128]{1,0:T(8,128)(2,1)S(1)}, u32[]{:S(2)}, u32[]{:S(2)}) collective-permute-start(bf16[128,128]{1,0:T(8,128)(2,1)S(1)} %constant_dynamic-update-slice_fusion.low_ref), channel_id=1, source_target_pairs={{480,0},{0,32},{32,64},{64,96},{96,128},{128,160},{160,192},{192,2... | collective-permute-start | bytes 98312 | tf_op jit(solution)/shard_map/ppermute | solution.py:210
  29.6 8.8 %copy-start.1 = (s32[32,2]{0,1:T(2,128)S(1)}, s32[32,2]{0,1:T(2,128)}, u32[]{:S(2)}) copy-start(s32[32,2]{0,1:T(2,128)} %param.13) | copy-start | bytes 772
  39.3 5.6 %collective-permute-start.3 = (bf16[32,128]{1,0:T(8,128)(2,1)S(1)}, bf16[32,128]{1,0:T(8,128)(2,1)S(1)}, u32[]{:S(2)}, u32[]{:S(2)}) collective-permute-start(bf16[32,128]{1,0:T(8,128)(2,1)S(1)} %get-tuple-element.25.field_ref), channel_id=1, source_target_pairs={{448,0},{480,32},{0,64},{32,96},{64,128},{96,160},{128,192},{160,2... | collective-permute-start | bytes 24584 | tf_op jit(solution)/shard_map/ppermute | solution.py:210
  44.9 11.0 %collective-permute-start.4 = (bf16[64,128]{1,0:T(8,128)(2,1)S(1)}, bf16[64,128]{1,0:T(8,128)(2,1)S(1)}, u32[]{:S(2)}, u32[]{:S(2)}) collective-permute-start(bf16[64,128]{1,0:T(8,128)(2,1)S(1)} %pad_maximum_fusion.1), channel_id=1, source_target_pairs={{96,0},{128,32},{160,64},{192,96},{224,128},{256,160},{288,192},{3... | collective-permute-start | bytes 49160 | tf_op jit(solution)/shard_map/ppermute | solution.py:210
  47.2 19.6 %all-to-all-start.1 = ((bf16[32,16,128]{2,1,0:T(8,128)(2,1)}), bf16[32,16,128]{2,1,0:T(8,128)(2,1)S(1)}, u32[]{:S(2)}, u32[]{:S(2)}) async-start(bf16[32,16,128]{2,1,0:T(8,128)(2,1)} %shard_map.91), calls=%async_computation.1 | async-start | bytes 262144 | tf_op jit(solution)/shard_map/all_to_all | solution.py:235
  56.0 7.1 %collective-permute-start.5 = (bf16[128,128]{1,0:T(8,128)(2,1)S(1)}, bf16[128,128]{1,0:T(8,128)(2,1)S(1)}, u32[]{:S(2)}, u32[]{:S(2)}) collective-permute-start(bf16[128,128]{1,0:T(8,128)(2,1)S(1)} %constant_dynamic-update-slice_fusion.3.low_ref), channel_id=1, source_target_pairs={{480,0},{0,32},{32,64},{64,96},{96,128},{128,160},{160,192},{192,2... | collective-permute-start | bytes 98312 | tf_op jit(solution)/shard_map/ppermute | solution.py:210
